TPU v7x, 32 devices: a whole 2x2x4 slice. The times are simulated.
32 devices in a mesh: dp: 8 (over z, x), section: 2 (over core), tensor: 2 (over y).
Axes of the slice: x: 2, y: 2, z: 4, core: 2. Of those that a mesh axis runs over, the one named last changes fastest.
Arguments:
- patches: bfloat16 [16, 1024, 384], P(('dp', 'section'), 'tensor'), may hold values from -6 to 6
- image_ids: int32 [16, 1024], P('dp'), may hold values from 0 to 7, never falling along the last dimension, each value on 1 to 256 neighbouring positions
- cotangent: bfloat16 [16, 1024, 384], P(('dp', 'section'), 'tensor'), may hold values from -6 to 6
- norm_gains: float32 [2, 2, 384], P('section'), may hold values from 0.5 to 1.5
- qkv_weight: bfloat16 [2, 384, 3, 384], P('section', None, None, 'tensor'), may hold values from -0.4375 to 0.4375
- out_weight: bfloat16 [2, 384, 384], P('section', 'tensor'), may hold values from -1.25 to 1.25
- mlp_in: bfloat16 [384, 1536], P(None, 'tensor'), may hold values from -0.3125 to 0.3125
- mlp_out: bfloat16 [1536, 384], P('tensor'), may hold values from -0.15625 to 0.15625
- router: bfloat16 [384, 2], P(None, 'tensor'), may hold values from -0.21875 to 0.21875
- expert_in: bfloat16 [2, 384, 1536], P('tensor'), may hold values from -2 to 2
- expert_out: bfloat16 [2, 1536, 384], P('tensor'), may hold values from -0.15625 to 0.15625
Outputs:
- activations: bfloat16 [16, 1024, 384], P(('dp', 'section'), 'tensor')
- patch_grad: bfloat16 [16, 1024, 384], P(('dp', 'section'), 'tensor')
- gains_grad: float32 [2, 2, 384], P('section')
- qkv_grad: float32 [2, 384, 3, 384], P('section', None, None, 'tensor')
- out_grad: float32 [2, 384, 384], P('section', 'tensor')
- mlp_in_grad: float32 [384, 1536], P(None, 'tensor')
- mlp_out_grad: float32 [1536, 384], P('tensor')
- router_grad: float32 [384, 2], P(None, 'tensor')
- expert_in_grad: float32 [2, 384, 1536], P('tensor')
- expert_out_grad: float32 [2, 1536, 384], P('tensor')
Inputs may be any that keep to these rules, and one draw needn't show every extreme that they name: `image_ids`: in each row the ids never fall; all 8 images are present, each with 1 to 256 patches, and one has exactly 256.
All inputs are finite; a program needn't handle non-finite values.
Results may differ from a plain program's by a relative error of at most 0.028.
The roundings to bfloat16 on the way count: a program that leaves them out, or rounds other values in their place, can miss the bound.
Values may be sent and summed in bfloat16 or wider, within the bound.
A program may use at most 128 MiB of HBM per device.

v0:
```python
import jax
import jax.numpy as jnp
from jax import lax
from jax.sharding import PartitionSpec as P

HD = 64
IMAGES = 8


epsilon = 1e-06
highest = lax.Precision.HIGHEST
contract_first = (((0,), (0,)), ((), ()))
contract_last = (((1,), (1,)), ((), ()))


def partner(array, axis, stride):
    return lax.ppermute(array, axis, [(i, i ^ 1 << stride) for i in range(lax.axis_size(axis))])


def shifted(value, axis, steps):
    count = lax.axis_size(axis)
    leading, last = (max(0, -steps), min(count, count - steps))
    return lax.ppermute(value, axis, [(source, source + steps) for source in range(leading, last)])


def layer_norm(values, gain_row):
    average = jnp.mean(values, axis=-1, keepdims=True)
    centred = values - average
    spread = jnp.mean(centred * centred, axis=-1, keepdims=True)
    return centred * lax.rsqrt(spread + epsilon) * gain_row


def smooth_gate(values):
    return jax.nn.gelu(values, approximate=False)


def gate_back(pre_act, upstream):
    _, pullback = jax.vjp(smooth_gate, pre_act)
    return pullback(upstream)[0]


def norm_back(values, gain_row, upstream):
    _, pullback = jax.vjp(layer_norm, values, gain_row)
    return pullback(upstream)


def gather_rows(local_rows):
    return lax.all_gather(local_rows, "tensor", axis=0, tiled=True)


def gather_grads(local_rows):
    return lax.all_gather(local_rows, "tensor", axis=0, tiled=True)


def scatter_rows(term_fn, row_count):
    return lax.psum_scatter(
        term_fn(jnp.int32(0), lax.axis_size("tensor") * row_count),
        "tensor",
        scatter_dimension=0,
        tiled=True,
    )


def scatter_grads(term_fn, row_count):
    return lax.psum_scatter(
        term_fn(jnp.int32(0), row_count * lax.axis_size("tensor")).astype(jnp.bfloat16),
        "tensor",
        scatter_dimension=0,
        tiled=True,
    ).astype(jnp.float32)


def image_member(ids_row):
    return (ids_row[:, None] == jnp.arange(IMAGES, dtype=jnp.int32)[None, :]).astype(jnp.float32)


def first_local_expert(local_experts):
    return lax.axis_index("tensor") * local_experts


def attend(z_full, w_qkv, same_image):
    seq_len = z_full.shape[0]
    head_count = w_qkv.shape[2] // HD
    projected = jnp.einsum("td,dcf->ctf", z_full, w_qkv, preferred_element_type=jnp.float32).astype(
        jnp.bfloat16
    )
    queries = projected[0].reshape(seq_len, head_count, HD)
    key_rows = projected[1].reshape(seq_len, head_count, HD)
    value_rows = projected[2].reshape(seq_len, head_count, HD)
    scores = jnp.einsum(
        "qhd,khd->hqk", queries, key_rows, preferred_element_type=jnp.float32
    ) * HD ** (-0.5)
    scores = jnp.where(same_image[None], scores, -1e30)
    maxima = jnp.max(scores, axis=-1, keepdims=True)
    exp_scores = jnp.exp(scores - maxima)
    attn_probs = exp_scores / jnp.sum(exp_scores, axis=-1, keepdims=True)
    mixed_rows = jnp.einsum(
        "hqk,khd->qhd",
        attn_probs.astype(jnp.bfloat16),
        value_rows,
        preferred_element_type=jnp.float32,
    )
    mixed_rows = mixed_rows.reshape(seq_len, head_count * HD).astype(jnp.bfloat16)
    return (queries, key_rows, value_rows, attn_probs, mixed_rows)


def attend_back(z_full, w_qkv, w_attn_out, same_image, grad_full, row_count):
    seq_len = z_full.shape[0]
    head_count = w_qkv.shape[2] // HD
    queries, key_rows, value_rows, attn_probs, mixed_rows = attend(z_full, w_qkv, same_image)
    attn_out_grad = lax.dot_general(
        mixed_rows, grad_full, contract_first, preferred_element_type=jnp.float32
    )
    mixed_grad = lax.dot_general(
        grad_full, w_attn_out, contract_last, preferred_element_type=jnp.float32
    )
    mixed_grad = mixed_grad.astype(jnp.bfloat16).reshape(seq_len, head_count, HD)
    prob_grad = jnp.einsum(
        "qhd,khd->hqk", mixed_grad, value_rows, preferred_element_type=jnp.float32
    )
    inner_sum = jnp.sum(attn_probs * prob_grad, axis=-1, keepdims=True)
    score_grad = (attn_probs * (prob_grad - inner_sum)).astype(jnp.bfloat16)
    query_grad = jnp.einsum(
        "hqk,khd->qhd", score_grad, key_rows, preferred_element_type=jnp.float32
    ) * HD ** (-0.5)
    key_grad = jnp.einsum(
        "hqk,qhd->khd", score_grad, queries, preferred_element_type=jnp.float32
    ) * HD ** (-0.5)
    value_grad = jnp.einsum(
        "hqk,qhd->khd",
        attn_probs.astype(jnp.bfloat16),
        mixed_grad,
        preferred_element_type=jnp.float32,
    )
    proj_grad = jnp.stack([query_grad, key_grad, value_grad]).reshape(3, seq_len, head_count * HD)
    proj_grad = proj_grad.astype(jnp.bfloat16)
    qkv_grad = jnp.einsum("td,ctf->dcf", z_full, proj_grad, preferred_element_type=jnp.float32)

    def term_rows(start_row, row_total):
        return jnp.einsum("ctf,dcf->td", proj_grad, w_qkv, preferred_element_type=jnp.float32)

    return (scatter_grads(term_rows, row_count), qkv_grad, attn_out_grad)


def expert_parts(z_full, member, router_part, w_in, w_out):
    seq_len = z_full.shape[0]
    logits = jnp.dot(z_full, router_part, preferred_element_type=jnp.float32)
    exp_logits = jnp.exp(logits)
    totals = lax.dot_general(member, exp_logits, contract_first, precision=highest)
    dispatch = exp_logits / jnp.dot(member, totals, precision=highest)
    member_low = member.astype(jnp.bfloat16)
    spread_rows = (dispatch.astype(jnp.bfloat16)[:, :, None] * member_low[:, None, :]).reshape(
        seq_len, -1
    )
    slot_rows = lax.dot_general(
        spread_rows, z_full, contract_first, preferred_element_type=jnp.float32
    )
    slot_rows = slot_rows.astype(jnp.bfloat16).reshape(w_in.shape[0], IMAGES, -1)
    pre_act = jnp.einsum("egd,edf->egf", slot_rows, w_in, preferred_element_type=jnp.float32)
    hidden = smooth_gate(pre_act).astype(jnp.bfloat16)
    outputs = jnp.einsum("egf,efd->egd", hidden, w_out, preferred_element_type=jnp.float32).astype(
        jnp.bfloat16
    )
    return (dispatch, spread_rows, slot_rows, pre_act, hidden, outputs)


def empty_parts(z_full, w_in):
    seq_len = z_full.shape[0]
    local_experts, width, hidden_width = w_in.shape
    return (
        jnp.zeros((seq_len, local_experts), jnp.float32),
        jnp.zeros((seq_len, local_experts * IMAGES), jnp.bfloat16),
        jnp.zeros((local_experts, IMAGES, width), jnp.bfloat16),
        jnp.zeros((local_experts, IMAGES, hidden_width), jnp.float32),
        jnp.zeros((local_experts, IMAGES, hidden_width), jnp.bfloat16),
        jnp.zeros((local_experts, IMAGES, width), jnp.bfloat16),
    )


def expert_phase(first_section, z_full, member, router_part, w_in, w_out):
    seq_len = z_full.shape[0]
    local_parts = lax.cond(
        first_section,
        lambda: empty_parts(z_full, w_in),
        lambda: expert_parts(z_full, member, router_part, w_in, w_out),
    )
    outputs = local_parts[5]
    outputs_all, router_all = (
        lax.all_gather(outputs, "tensor", axis=0, tiled=True),
        lax.all_gather(router_part, "tensor", axis=1, tiled=True),
    )
    all_exp = jnp.exp(jnp.dot(z_full, router_all, preferred_element_type=jnp.float32))
    combine = all_exp / jnp.sum(all_exp, axis=-1, keepdims=True)
    member_low = member.astype(jnp.bfloat16)
    mixing = (combine.astype(jnp.bfloat16)[:, :, None] * member_low[:, None, :]).reshape(
        seq_len, -1
    )
    return (local_parts, outputs_all, combine, mixing)


def second_forward(
    first_section, z_full, member, mlp_in, mlp_out, router_part, w_in, w_out, row_count
):
    seq_len = z_full.shape[0]
    local_experts = w_in.shape[0]
    local_parts, outputs_all, combine, mixing = expert_phase(
        first_section, z_full, member, router_part, w_in, w_out
    )
    first_expert = first_local_expert(local_experts)
    own_mixing = lax.dynamic_slice_in_dim(mixing, first_expert * IMAGES, local_experts * IMAGES, 1)
    flat_local = local_parts[5].reshape(-1, local_parts[5].shape[-1])
    hidden_dense = lax.cond(
        first_section,
        lambda: smooth_gate(jnp.dot(z_full, mlp_in, preferred_element_type=jnp.float32)).astype(
            jnp.bfloat16
        ),
        lambda: jnp.zeros((seq_len, mlp_in.shape[1]), jnp.bfloat16),
    )

    def term_rows(start_row, row_total):
        return lax.cond(
            first_section,
            lambda: jnp.dot(hidden_dense, mlp_out, preferred_element_type=jnp.float32),
            lambda: jnp.dot(own_mixing, flat_local, preferred_element_type=jnp.float32),
        )

    return scatter_rows(term_rows, row_count)


def second_backward(
    first_section, z_full, member, grad_full, mlp_in, mlp_out, router_part, w_in, w_out, row_count
):
    seq_len = z_full.shape[0]
    local_experts = w_in.shape[0]
    width = z_full.shape[1]
    local_parts, outputs_all, combine, mixing = expert_phase(
        first_section, z_full, member, router_part, w_in, w_out
    )
    dispatch, spread_rows, slot_rows, pre_act, hidden, outputs = local_parts
    first_expert = first_local_expert(local_experts)

    def dense_side():
        dense_pre = jnp.dot(z_full, mlp_in, preferred_element_type=jnp.float32)
        dense_hidden = smooth_gate(dense_pre).astype(jnp.bfloat16)
        w_out_grad = lax.dot_general(
            dense_hidden, grad_full, contract_first, preferred_element_type=jnp.float32
        )
        hidden_grad = lax.dot_general(
            grad_full, mlp_out, contract_last, preferred_element_type=jnp.float32
        )
        pre_grad = gate_back(dense_pre, hidden_grad).astype(jnp.bfloat16)
        w_in_grad = lax.dot_general(
            z_full, pre_grad, contract_first, preferred_element_type=jnp.float32
        )
        return (
            pre_grad,
            jnp.zeros((local_experts * IMAGES, width), jnp.bfloat16),
            jnp.zeros((seq_len, local_experts), jnp.bfloat16),
            w_in_grad,
            w_out_grad,
            jnp.zeros(router_part.shape, jnp.float32),
            jnp.zeros(w_in.shape, jnp.float32),
            jnp.zeros(w_out.shape, jnp.float32),
        )

    def expert_side():
        total_experts = combine.shape[1]
        flat_outputs = outputs_all.reshape(-1, outputs_all.shape[-1])
        per_slot = lax.dot_general(
            grad_full, flat_outputs, contract_last, preferred_element_type=jnp.float32
        )
        combine_grad = jnp.sum(
            per_slot.reshape(seq_len, total_experts, IMAGES) * member[:, None, :], axis=-1
        )
        inner_sum = jnp.sum(combine * combine_grad, axis=-1, keepdims=True)
        logit_comb = lax.dynamic_slice_in_dim(
            combine * (combine_grad - inner_sum), first_expert, local_experts, 1
        )
        own_mixing = lax.dynamic_slice_in_dim(
            mixing, first_expert * IMAGES, local_experts * IMAGES, 1
        )
        output_grad = lax.dot_general(
            own_mixing, grad_full, contract_first, preferred_element_type=jnp.float32
        )
        output_grad = output_grad.astype(jnp.bfloat16).reshape(local_experts, IMAGES, -1)
        w_out_grad = jnp.einsum(
            "egf,egd->efd", hidden, output_grad, preferred_element_type=jnp.float32
        )
        hidden_grad = jnp.einsum(
            "egd,efd->egf", output_grad, w_out, preferred_element_type=jnp.float32
        )
        pre_grad = gate_back(pre_act, hidden_grad).astype(jnp.bfloat16)
        w_in_grad = jnp.einsum(
            "egd,egf->edf", slot_rows, pre_grad, preferred_element_type=jnp.float32
        )
        slot_grad = jnp.einsum("egf,edf->egd", pre_grad, w_in, preferred_element_type=jnp.float32)
        slot_grad = slot_grad.astype(jnp.bfloat16).reshape(local_experts * IMAGES, -1)
        per_dispatch = lax.dot_general(
            z_full, slot_grad, contract_last, preferred_element_type=jnp.float32
        )
        dispatch_grad = jnp.sum(
            per_dispatch.reshape(seq_len, local_experts, IMAGES) * member[:, None, :], axis=-1
        )
        weighted = dispatch * dispatch_grad
        image_sums = lax.dot_general(member, weighted, contract_first, precision=highest)
        logit_disp = weighted - dispatch * jnp.dot(member, image_sums, precision=highest)
        logit_grad = (logit_comb + logit_disp).astype(jnp.bfloat16)
        router_grad = lax.dot_general(
            z_full, logit_grad, contract_first, preferred_element_type=jnp.float32
        )
        return (
            jnp.zeros((seq_len, mlp_in.shape[1]), jnp.bfloat16),
            slot_grad,
            logit_grad,
            jnp.zeros(mlp_in.shape, jnp.float32),
            jnp.zeros(mlp_out.shape, jnp.float32),
            router_grad,
            w_in_grad,
            w_out_grad,
        )

    results = lax.cond(first_section, dense_side, expert_side)
    dense_grad, slot_grad, logit_grad = (results[0], results[1], results[2])

    def term_rows(start_row, row_total):

        def dense_term():
            return lax.dot_general(
                dense_grad, mlp_in, contract_last, preferred_element_type=jnp.float32
            )

        def expert_term():
            through_slots = jnp.dot(spread_rows, slot_grad, preferred_element_type=jnp.float32)
            through_logits = lax.dot_general(
                logit_grad, router_part, contract_last, preferred_element_type=jnp.float32
            )
            return through_slots + through_logits

        return lax.cond(first_section, dense_term, expert_term)

    return (scatter_grads(term_rows, row_count),) + tuple(results[3:])


def per_device(
    patches,
    image_ids,
    cotangent,
    norm_gains,
    qkv_weight,
    out_weight,
    mlp_in,
    mlp_out,
    router,
    expert_in,
    expert_out,
):
    first_section = lax.axis_index("section") == 0
    half_micros = patches.shape[0]
    feature_width = patches.shape[2]
    gain_rows = norm_gains[0]
    payload = jnp.where(first_section, cotangent, patches)
    arrived = partner(payload, "section", 0)
    section_inputs = jnp.concatenate([patches, arrived], axis=0)
    section_cotangents = jnp.concatenate([arrived, cotangent], axis=0)
    micros = image_ids.shape[0]
    w_qkv = qkv_weight[0]
    w_attn_out = out_weight[0]
    row_count = patches.shape[1]
    full_rows = row_count * lax.axis_size("tensor")

    def block_forward(inputs_local, ids_row):
        same_image = ids_row[:, None] == ids_row[None, :]
        member = image_member(ids_row)
        z_first = gather_rows(layer_norm(inputs_local, gain_rows[0]).astype(jnp.bfloat16))
        mixed_rows = attend(z_first, w_qkv, same_image)[4]

        def term_rows(start_row, row_total):
            return jnp.dot(mixed_rows, w_attn_out, preferred_element_type=jnp.float32)

        middle = inputs_local + scatter_rows(term_rows, row_count)
        z_second = gather_rows(layer_norm(middle, gain_rows[1]).astype(jnp.bfloat16))
        branch = second_forward(
            first_section,
            z_second,
            member,
            mlp_in,
            mlp_out,
            router,
            expert_in,
            expert_out,
            row_count,
        )
        return (middle + branch, (z_first, z_second, inputs_local, middle))

    def forward_tick(tick_index, loop_state):
        incoming, store_first, store_second, store_input, store_middle, finished = loop_state
        micro_index = jnp.clip(jnp.where(first_section, tick_index, tick_index - 1), 0, micros - 1)
        own_input = lax.dynamic_index_in_dim(section_inputs, micro_index, 0, keepdims=False)
        source = jnp.where(first_section, own_input, incoming).astype(jnp.float32)
        ids_row = lax.dynamic_index_in_dim(image_ids, micro_index, 0, keepdims=False)
        result, kept_rows = block_forward(source, ids_row)
        store_first = lax.dynamic_update_index_in_dim(store_first, kept_rows[0], micro_index, 0)
        store_second = lax.dynamic_update_index_in_dim(store_second, kept_rows[1], micro_index, 0)
        store_input = lax.dynamic_update_index_in_dim(store_input, kept_rows[2], micro_index, 0)
        store_middle = lax.dynamic_update_index_in_dim(store_middle, kept_rows[3], micro_index, 0)
        result_low = result.astype(jnp.bfloat16)
        finished = lax.dynamic_update_index_in_dim(finished, result_low, micro_index, 0)
        outgoing = shifted(result_low, "section", 1)
        return (outgoing, store_first, store_second, store_input, store_middle, finished)

    forward_init = (
        jnp.zeros((row_count, feature_width), jnp.bfloat16),
        jnp.zeros((micros, full_rows, feature_width), jnp.bfloat16),
        jnp.zeros((micros, full_rows, feature_width), jnp.bfloat16),
        jnp.zeros((micros, row_count, feature_width), jnp.float32),
        jnp.zeros((micros, row_count, feature_width), jnp.float32),
        jnp.zeros((micros, row_count, feature_width), jnp.bfloat16),
    )
    forward_state = lax.fori_loop(0, micros + 1, forward_tick, forward_init)
    store_first, store_second, store_input, store_middle, finished = forward_state[1:]

    def zero_like(array_in):
        return jnp.zeros(array_in.shape, jnp.float32)

    def block_backward(kept_rows, upstream, ids_row):
        z_first, z_second, inputs_local, middle = kept_rows
        same_image = ids_row[:, None] == ids_row[None, :]
        member = image_member(ids_row)
        grad_second = gather_grads(upstream.astype(jnp.bfloat16))
        branch_grads = second_backward(
            first_section,
            z_second,
            member,
            grad_second,
            mlp_in,
            mlp_out,
            router,
            expert_in,
            expert_out,
            row_count,
        )
        middle_grad, gain_second = norm_back(middle, gain_rows[1], branch_grads[0])
        middle_total = upstream + middle_grad
        grad_first = gather_grads(middle_total.astype(jnp.bfloat16))
        z_first_grad, qkv_grad, attn_out_grad = attend_back(
            z_first, w_qkv, w_attn_out, same_image, grad_first, row_count
        )
        input_grad, gain_first = norm_back(inputs_local, gain_rows[0], z_first_grad)
        fresh_grads = (jnp.stack([gain_first, gain_second]), qkv_grad, attn_out_grad) + tuple(
            branch_grads[1:]
        )
        return (middle_total + input_grad, fresh_grads)

    def backward_tick(tick_index, loop_state):
        incoming, grad_sums, finished_grads = loop_state
        micro_index = jnp.clip(jnp.where(first_section, tick_index - 1, tick_index), 0, micros - 1)
        is_valid = jnp.where(first_section, tick_index >= 1, tick_index < micros)
        own_cotangent = lax.dynamic_index_in_dim(section_cotangents, micro_index, 0, keepdims=False)
        upstream = jnp.where(first_section, incoming, own_cotangent).astype(jnp.float32)
        kept_rows = (
            lax.dynamic_index_in_dim(store_first, micro_index, 0, keepdims=False),
            lax.dynamic_index_in_dim(store_second, micro_index, 0, keepdims=False),
            lax.dynamic_index_in_dim(store_input, micro_index, 0, keepdims=False),
            lax.dynamic_index_in_dim(store_middle, micro_index, 0, keepdims=False),
        )
        ids_row = lax.dynamic_index_in_dim(image_ids, micro_index, 0, keepdims=False)
        input_grad, fresh_grads = block_backward(kept_rows, upstream, ids_row)
        grad_sums = jax.tree.map(
            lambda total_now, fresh_now: total_now + jnp.where(is_valid, fresh_now, 0.0),
            grad_sums,
            fresh_grads,
        )
        grad_low = input_grad.astype(jnp.bfloat16)
        finished_grads = lax.dynamic_update_index_in_dim(finished_grads, grad_low, micro_index, 0)
        outgoing = shifted(grad_low, "section", -1)
        return (outgoing, grad_sums, finished_grads)

    grad_init = (
        jnp.zeros((2, feature_width), jnp.float32),
        zero_like(w_qkv),
        zero_like(w_attn_out),
        zero_like(mlp_in),
        zero_like(mlp_out),
        zero_like(router),
        zero_like(expert_in),
        zero_like(expert_out),
    )
    backward_init = (
        jnp.zeros((row_count, feature_width), jnp.bfloat16),
        grad_init,
        jnp.zeros((micros, row_count, feature_width), jnp.bfloat16),
    )
    backward_state = lax.fori_loop(0, micros + 1, backward_tick, backward_init)
    grad_sums = backward_state[1]
    finished_grads = backward_state[2]
    gain_total = lax.psum(grad_sums[0], ("dp", "tensor"))
    attn_totals = lax.psum((grad_sums[1], grad_sums[2]), "dp")
    ffn_totals = lax.psum(
        (grad_sums[3], grad_sums[4], grad_sums[5], grad_sums[6], grad_sums[7]), ("dp", "section")
    )
    payload_out = jnp.where(first_section, finished_grads[half_micros:], finished[:half_micros])
    returned = partner(payload_out, "section", 0)
    activations = jnp.where(first_section, returned, finished[half_micros:])
    patch_grad = jnp.where(first_section, finished_grads[:half_micros], returned)
    return (
        activations,
        patch_grad,
        gain_total[None],
        attn_totals[0][None],
        attn_totals[1][None],
        ffn_totals[0],
        ffn_totals[1],
        ffn_totals[2],
        ffn_totals[3],
        ffn_totals[4],
    )


def solution(mesh):
    return jax.shard_map(
        per_device,
        mesh=mesh,
        in_specs=(
            P(("dp", "section"), "tensor", None),
            P("dp", None),
            P(("dp", "section"), "tensor", None),
            P("section", None, None),
            P("section", None, None, "tensor"),
            P("section", "tensor", None),
            P(None, "tensor"),
            P("tensor", None),
            P(None, "tensor"),
            P("tensor", None, None),
            P("tensor", None, None),
        ),
        out_specs=(
            P(("dp", "section"), "tensor", None),
            P(("dp", "section"), "tensor", None),
            P("section", None, None),
            P("section", None, None, "tensor"),
            P("section", "tensor", None),
            P(None, "tensor"),
            P("tensor", None),
            P(None, "tensor"),
            P("tensor", None, None),
            P("tensor", None, None),
        ),
        check_vma=False,
    )
```

profile of v0, /device:TPU:0, one launch (start us, length us, event | category | flops | bytes accessed | tf_op | source)
XLA Modules:
  0.0 1152.2 jit_solution(4750533799098445989)
XLA Ops:
  19.1 384.6 %while.59 = (s32[]{:T(128)}, bf16[512,384]{1,0:T(8,128)(2,1)}, bf16[2,1024,384]{2,1,0:T(8,128)(2,1)}, bf16[2,1024,384]{2,1,0:T(8,128)(2,1)}, f32[2,512,384]{2,1,...) while((s32[]{:T(128)}, bf16[512,384]{1,0:T(8,128)(2,1)}, ...), condition=%wide.region_16.17_spmd, body=%wide.region_0.16_spmd.sunk | while | flops 2724154368 | bytes 91914904 | solution.py:419
  24.9 13.1 %all_gather.78 = bf16[1024,384]{1,0:T(8,128)(2,1)S(1)} all-gather(bf16[512,384]{1,0:T(8,128)(2,1)S(1)} %fusion.336), channel_id=1, replica_groups=mesh['dp'=8,'section'=2,'tensor'=2] {'tensor'}, dimensions={0}, use_global_device_ids=true | all-gather | bytes 1179648 | tf_op jit(solution)/shard_map/while/body/eval_jaxpr/all_gather | solution.py:48
  41.2 11.2 fusion.339
  65.1 23.3 %reduce-scatter.5.cloned.1.call-done = f32[512,384]{1,0:T(8,128)} async-done(((f32[1024,384]{1,0:T(8,128)}), f32[512,384]{1,0:T(8,128)}) %reduce-scatter.5.cloned.1.call-update) | async-done | bytes 786448 | tf_op jit(solution)/shard_map/while/body/eval_jaxpr/reduce_scatter | solution.py:56
  92.4 11.5 %all_gather.79 = bf16[1024,384]{1,0:T(8,128)(2,1)S(1)} all-gather(bf16[512,384]{1,0:T(8,128)(2,1)S(1)} %multiply_convert_fusion.6), channel_id=1, replica_groups=mesh['dp'=8,'section'=2,'tensor'=2] {'tensor'}, dimensions={0}, use_global_device_ids=true | all-gather | bytes 1179648 | tf_op jit(solution)/shard_map/while/body/eval_jaxpr/all_gather | solution.py:48
  104.4 9.3 conditional.16
  104.4 9.3 fusion.27
  119.5 24.1 %reduce-scatter.7.cloned.1.call-done = f32[512,384]{1,0:T(8,128)} async-done(((f32[1024,384]{1,0:T(8,128)}), f32[512,384]{1,0:T(8,128)}) %reduce-scatter.7.cloned.1.call-update) | async-done | bytes 786448 | tf_op jit(solution)/shard_map/while/body/eval_jaxpr/reduce_scatter | solution.py:56
  155.0 11.8 %all_gather.78 = bf16[1024,384]{1,0:T(8,128)(2,1)S(1)} all-gather(bf16[512,384]{1,0:T(8,128)(2,1)S(1)} %fusion.336), channel_id=1, replica_groups=mesh['dp'=8,'section'=2,'tensor'=2] {'tensor'}, dimensions={0}, use_global_device_ids=true | all-gather | bytes 1179648 | tf_op jit(solution)/shard_map/while/body/eval_jaxpr/all_gather | solution.py:48
  169.9 11.2 fusion.339
  193.9 21.8 %reduce-scatter.5.cloned.1.call-done = f32[512,384]{1,0:T(8,128)} async-done(((f32[1024,384]{1,0:T(8,128)}), f32[512,384]{1,0:T(8,128)}) %reduce-scatter.5.cloned.1.call-update) | async-done | bytes 786448 | tf_op jit(solution)/shard_map/while/body/eval_jaxpr/reduce_scatter | solution.py:56
  219.7 11.5 %all_gather.79 = bf16[1024,384]{1,0:T(8,128)(2,1)S(1)} all-gather(bf16[512,384]{1,0:T(8,128)(2,1)S(1)} %multiply_convert_fusion.6), channel_id=1, replica_groups=mesh['dp'=8,'section'=2,'tensor'=2] {'tensor'}, dimensions={0}, use_global_device_ids=true | all-gather | bytes 1179648 | tf_op jit(solution)/shard_map/while/body/eval_jaxpr/all_gather | solution.py:48
  231.7 9.3 conditional.16
  231.7 9.3 fusion.27
  246.8 24.1 %reduce-scatter.7.cloned.1.call-done = f32[512,384]{1,0:T(8,128)} async-done(((f32[1024,384]{1,0:T(8,128)}), f32[512,384]{1,0:T(8,128)}) %reduce-scatter.7.cloned.1.call-update) | async-done | bytes 786448 | tf_op jit(solution)/shard_map/while/body/eval_jaxpr/reduce_scatter | solution.py:56
  282.3 11.8 %all_gather.78 = bf16[1024,384]{1,0:T(8,128)(2,1)S(1)} all-gather(bf16[512,384]{1,0:T(8,128)(2,1)S(1)} %fusion.336), channel_id=1, replica_groups=mesh['dp'=8,'section'=2,'tensor'=2] {'tensor'}, dimensions={0}, use_global_device_ids=true | all-gather | bytes 1179648 | tf_op jit(solution)/shard_map/while/body/eval_jaxpr/all_gather | solution.py:48
  297.2 11.2 fusion.339
  321.2 21.8 %reduce-scatter.5.cloned.1.call-done = f32[512,384]{1,0:T(8,128)} async-done(((f32[1024,384]{1,0:T(8,128)}), f32[512,384]{1,0:T(8,128)}) %reduce-scatter.5.cloned.1.call-update) | async-done | bytes 786448 | tf_op jit(solution)/shard_map/while/body/eval_jaxpr/reduce_scatter | solution.py:56
  347.0 11.5 all_gather.79
  358.9 9.3 conditional.16
  359.0 9.3 fusion.27
  374.1 24.1 %reduce-scatter.7.cloned.1.call-done = f32[512,384]{1,0:T(8,128)} async-done(((f32[1024,384]{1,0:T(8,128)}), f32[512,384]{1,0:T(8,128)}) %reduce-scatter.7.cloned.1.call-update) | async-done | bytes 786448 | tf_op jit(solution)/shard_map/while/body/eval_jaxpr/reduce_scatter | solution.py:56
  405.6 488.7 %while.60 = (s32[]{:T(128)}, bf16[512,384]{1,0:T(8,128)(2,1)}, f32[2,384]{1,0:T(2,128)}, f32[384,3,192]{0,2,1:T(8,128)}, f32[192,384]{1,0:T(8,128)}, /*index=5*/...) while((s32[]{:T(128)}, bf16[512,384]{1,0:T(8,128)(2,1)}, ...), condition=%wide.region_43.44_spmd.clone, body=%wide.region_17.43_spmd.clone.sunk | while | flops 7258640384 | bytes 370454752 | solution.py:493
  442.8 10.5 all_gather.80
  454.6 30.6 %conditional.19 = (bf16[1024,768]{1,0:T(8,128)(2,1)S(1)}, bf16[8,384]{1,0:T(8,128)(2,1)S(1)}, bf16[1024,1]{0,1:T(2,128)(2,1)S(1)}, f32[384,768]{1,0:T(8,128)}, f...) conditional(s32[]{:T(128)} %convert_element_type.625, ...), branch_computations={%region_21.24_spmd, %region_25.25_spmd} | conditional | flops 2478047232 | bytes 50734756 | solution.py:322
  454.6 17.7 %fusion.96 = (f32[1024,768]{1,0:T(8,128)S(1)}, f32[1024,768]{1,0:T(8,128)S(1)}) fusion(bf16[1024,384]{1,0:T(8,128)(2,1)S(1)} %get-tuple-element.1188, bf16[384,768]{1,0:T(8,128)(2,1)} %get-tuple-element.1189), kind=kOutput, calls=%fused_computation.136 | convolution fusion | flops 652738560 | bytes 7667712 | tf_op jit(solution)/shard_map/while/body/eval_jaxpr/cond/branch_1_fun/dot_general | solution.py:243
  497.3 10.6 fusion.376
  520.8 8.5 all_gather.82
  531.7 7.5 fusion.377
  556.9 12.9 %reduce-scatter.11.cloned.1.call-done = bf16[512,384]{1,0:T(8,128)(2,1)} async-done(((bf16[1024,384]{1,0:T(8,128)(2,1)}), bf16[512,384]{1,0:T(8,128)(2,1)}) %reduce-scatter.11.cloned.1.call-update) | async-done | bytes 393232 | tf_op jit(solution)/shard_map/while/body/eval_jaxpr/reduce_scatter | solution.py:65
  594.3 9.8 all_gather.80
  605.5 30.6 %conditional.19 = (bf16[1024,768]{1,0:T(8,128)(2,1)S(1)}, bf16[8,384]{1,0:T(8,128)(2,1)S(1)}, bf16[1024,1]{0,1:T(2,128)(2,1)S(1)}, f32[384,768]{1,0:T(8,128)}, f...) conditional(s32[]{:T(128)} %convert_element_type.625, ...), branch_computations={%region_21.24_spmd, %region_25.25_spmd} | conditional | flops 2478047232 | bytes 50734756 | solution.py:322
  605.5 17.7 %fusion.96 = (f32[1024,768]{1,0:T(8,128)S(1)}, f32[1024,768]{1,0:T(8,128)S(1)}) fusion(bf16[1024,384]{1,0:T(8,128)(2,1)S(1)} %get-tuple-element.1188, bf16[384,768]{1,0:T(8,128)(2,1)} %get-tuple-element.1189), kind=kOutput, calls=%fused_computation.136 | convolution fusion | flops 652738560 | bytes 7667712 | tf_op jit(solution)/shard_map/while/body/eval_jaxpr/cond/branch_1_fun/dot_general | solution.py:243
  654.5 10.6 fusion.376
  667.7 6.6 fusion.383
  677.9 8.5 all_gather.82
  688.8 7.5 fusion.377
  717.3 9.9 reduce-scatter.11.cloned.1.call-done
  751.7 9.8 all_gather.80
  762.9 30.6 %conditional.19 = (bf16[1024,768]{1,0:T(8,128)(2,1)S(1)}, bf16[8,384]{1,0:T(8,128)(2,1)S(1)}, bf16[1024,1]{0,1:T(2,128)(2,1)S(1)}, f32[384,768]{1,0:T(8,128)}, f...) conditional(s32[]{:T(128)} %convert_element_type.625, ...), branch_computations={%region_21.24_spmd, %region_25.25_spmd} | conditional | flops 2478047232 | bytes 50734756 | solution.py:322
  762.9 17.7 %fusion.96 = (f32[1024,768]{1,0:T(8,128)S(1)}, f32[1024,768]{1,0:T(8,128)S(1)}) fusion(bf16[1024,384]{1,0:T(8,128)(2,1)S(1)} %get-tuple-element.1188, bf16[384,768]{1,0:T(8,128)(2,1)} %get-tuple-element.1189), kind=kOutput, calls=%fused_computation.136 | convolution fusion | flops 652738560 | bytes 7667712 | tf_op jit(solution)/shard_map/while/body/eval_jaxpr/cond/branch_1_fun/dot_general | solution.py:243
  811.9 10.6 fusion.376
  835.3 8.5 all_gather.82
  846.2 7.5 fusion.377
  874.7 9.9 reduce-scatter.11.cloned.1.call-done
  903.2 34.3 %psum.61 = f32[384,1]{0,1:T(1,128)} all-reduce(f32[384,1]{0,1:T(1,128)S(1)} %copy-done.54), channel_id=1, replica_groups=mesh['dp'=8,'section'=2,'tensor'=2] {'dp','section'}, use_global_device_ids=true, to_apply=%region_49.50 | all-reduce | flops 384 | bytes 3072 | tf_op jit(solution)/shard_map/psum | solution.py:498
  937.5 38.2 %psum.56 = f32[1,2,384]{2,1,0:T(2,128)} all-reduce(f32[1,2,384]{2,1,0:T(2,128)S(1)} %bitcast.473), channel_id=1, replica_groups=mesh['dp'=8,'section'=2,'tensor'=2] {'dp','tensor'}, use_global_device_ids=true, to_apply=%region_44.45 | all-reduce | flops 768 | bytes 6144 | tf_op jit(solution)/shard_map/psum | solution.py:496
  979.3 156.3 %all-reduce.5.cloned.1.call-done = (f32[384,768]{1,0:T(8,128)}, f32[768,384]{1,0:T(8,128)}, f32[1,384,1536]{2,1,0:T(8,128)}, f32[1,1536,384]{2,1,0:T(8,128)}) async-done(((f32[384,768]{1,0:T(8,128)}, f32[768,384]{1,0:T(8,128)}, f32[1,384,1536]{2,1,0:T(8,128)}, f32[1,1536,384]{2,1,0:T(8,128)}), (f32[384,768]{1,0:T(8,128)}, f32[768,384]{1,0:T(8,128)}, f32[1,384,1536]{2,1,0:T(8,128)}, ...) | async-done | bytes 7077904 | tf_op jit(solution)/shard_map/psum | solution.py:498
  (669 shorter events, 425.6 us)
Async XLA Ops:
  9.1 1.9 collective-permute-start.2
  19.1 69.3 %reduce-scatter.5.cloned.1.call-start = ((), (), s32[]{:S(2)}) async-start(), calls=%async_computation.6 | async-start | bytes 2359296 | tf_op jit(solution)/shard_map/while/body/eval_jaxpr/reduce_scatter | solution.py:56
  38.0 14.3 %copy-start.3 = (bf16[1024,384]{1,0:T(8,128)(2,1)}, bf16[1024,384]{1,0:T(8,128)(2,1)S(1)}, u32[]{:S(2)}) copy-start(bf16[1024,384]{1,0:T(8,128)(2,1)S(1)} %all_gather.78) | copy-start | bytes 2359300 | tf_op jit(solution)/shard_map/while
  60.7 82.9 %reduce-scatter.7.cloned.1.call-start = ((), (), s32[]{:S(2)}) async-start(), calls=%async_computation.7 | async-start | bytes 2359296 | tf_op jit(solution)/shard_map/while/body/eval_jaxpr/reduce_scatter | solution.py:56
  117.3 26.3 %copy-start = (f32[512,384]{1,0:T(8,128)S(1)}, f32[512,384]{1,0:T(8,128)}, u32[]{:S(2)}) copy-start(f32[512,384]{1,0:T(8,128)} %reduce-scatter.5.cloned.1.call-done) | copy-start | bytes 2359300 | tf_op jit(solution)/shard_map/while
  145.6 3.6 collective-permute-start
  149.2 66.5 %reduce-scatter.5.cloned.1.call-start = ((), (), s32[]{:S(2)}) async-start(), calls=%async_computation.6 | async-start | bytes 2359296 | tf_op jit(solution)/shard_map/while/body/eval_jaxpr/reduce_scatter | solution.py:56
  166.8 14.3 %copy-start.3 = (bf16[1024,384]{1,0:T(8,128)(2,1)}, bf16[1024,384]{1,0:T(8,128)(2,1)S(1)}, u32[]{:S(2)}) copy-start(bf16[1024,384]{1,0:T(8,128)(2,1)S(1)} %all_gather.78) | copy-start | bytes 2359300 | tf_op jit(solution)/shard_map/while
  189.5 81.4 %reduce-scatter.7.cloned.1.call-start = ((), (), s32[]{:S(2)}) async-start(), calls=%async_computation.7 | async-start | bytes 2359296 | tf_op jit(solution)/shard_map/while/body/eval_jaxpr/reduce_scatter | solution.py:56
  244.6 26.3 %copy-start = (f32[512,384]{1,0:T(8,128)S(1)}, f32[512,384]{1,0:T(8,128)}, u32[]{:S(2)}) copy-start(f32[512,384]{1,0:T(8,128)} %reduce-scatter.5.cloned.1.call-done) | copy-start | bytes 2359300 | tf_op jit(solution)/shard_map/while
  272.9 3.5 collective-permute-start
  276.4 66.6 %reduce-scatter.5.cloned.1.call-start = ((), (), s32[]{:S(2)}) async-start(), calls=%async_computation.6 | async-start | bytes 2359296 | tf_op jit(solution)/shard_map/while/body/eval_jaxpr/reduce_scatter | solution.py:56
  294.1 14.3 %copy-start.3 = (bf16[1024,384]{1,0:T(8,128)(2,1)}, bf16[1024,384]{1,0:T(8,128)(2,1)S(1)}, u32[]{:S(2)}) copy-start(bf16[1024,384]{1,0:T(8,128)(2,1)S(1)} %all_gather.78) | copy-start | bytes 2359300 | tf_op jit(solution)/shard_map/while
  316.8 81.4 %reduce-scatter.7.cloned.1.call-start = ((), (), s32[]{:S(2)}) async-start(), calls=%async_computation.7 | async-start | bytes 2359296 | tf_op jit(solution)/shard_map/while/body/eval_jaxpr/reduce_scatter | solution.py:56
  371.9 26.3 %copy-start = (f32[512,384]{1,0:T(8,128)S(1)}, f32[512,384]{1,0:T(8,128)}, u32[]{:S(2)}) copy-start(f32[512,384]{1,0:T(8,128)} %reduce-scatter.5.cloned.1.call-done) | copy-start | bytes 2359300 | tf_op jit(solution)/shard_map/while
  400.2 3.5 collective-permute-start
  428.1 91.1 %copy-start.1 = (f32[2,512,384]{2,1,0:T(8,128)}, f32[2,512,384]{2,1,0:T(8,128)S(1)}, u32[]{:S(2)}) copy-start(f32[2,512,384]{2,1,0:T(8,128)S(1)} %get-tuple-element.2097) | copy-start | bytes 4718596 | tf_op jit(solution)/shard_map/while
  428.1 89.1 %reduce-scatter.9.cloned.1.call-start = ((), (), s32[]{:S(2)}) async-start(), calls=%async_computation.8 | async-start | bytes 1179648 | tf_op jit(solution)/shard_map/while/body/eval_jaxpr/reduce_scatter | solution.py:65
  442.8 77.8 %copy-start.8 = (bf16[512,384]{1,0:T(8,128)(2,1)}, bf16[512,384]{1,0:T(8,128)(2,1)S(1)}, u32[]{:S(2)}) copy-start(bf16[512,384]{1,0:T(8,128)(2,1)S(1)} %bitcast_select_fusion.4) | copy-start | bytes 1179652 | tf_op jit(solution)/shard_map/while
  488.2 81.6 %reduce-scatter.11.cloned.1.call-start = ((), (), s32[]{:S(2)}) async-start(), calls=%async_computation.9 | async-start | bytes 1179648 | tf_op jit(solution)/shard_map/while/body/eval_jaxpr/reduce_scatter | solution.py:65
  508.0 23.7 %copy-start.44 = (f32[3,1024]{1,0:T(4,128)}, f32[3,1024]{1,0:T(4,128)S(1)}, u32[]{:S(2)}) copy-start(f32[3,1024]{1,0:T(4,128)S(1)} %get-tuple-element.1901) | copy-start | bytes 36868 | tf_op jit(solution)/shard_map/while
  555.9 17.5 %copy-start.5 = (f32[512,384]{1,0:T(8,128)S(1)}, f32[512,384]{1,0:T(8,128)}, u32[]{:S(2)}) copy-start(f32[512,384]{1,0:T(8,128)} %copy-done.4) | copy-start | bytes 2359300 | tf_op jit(solution)/shard_map/while
  555.9 17.5 %copy-start.9 = (bf16[512,384]{1,0:T(8,128)(2,1)S(1)}, bf16[512,384]{1,0:T(8,128)(2,1)}, u32[]{:S(2)}) copy-start(bf16[512,384]{1,0:T(8,128)(2,1)} %copy-done.8) | copy-start | bytes 1179652 | tf_op jit(solution)/shard_map/while
  556.9 20.2 %copy-start.7 = (bf16[1024,384]{1,0:T(8,128)(2,1)S(1)}, bf16[1024,384]{1,0:T(8,128)(2,1)}, u32[]{:S(2)}) copy-start(bf16[1024,384]{1,0:T(8,128)(2,1)} %copy-done.6) | copy-start | bytes 2359300 | tf_op jit(solution)/shard_map/while
  575.8 3.7 collective-permute-start.1
  579.6 96.8 %copy-start.1 = (f32[2,512,384]{2,1,0:T(8,128)}, f32[2,512,384]{2,1,0:T(8,128)S(1)}, u32[]{:S(2)}) copy-start(f32[2,512,384]{2,1,0:T(8,128)S(1)} %get-tuple-element.2097) | copy-start | bytes 4718596 | tf_op jit(solution)/shard_map/while
  579.6 94.7 %reduce-scatter.9.cloned.1.call-start = ((), (), s32[]{:S(2)}) async-start(), calls=%async_computation.8 | async-start | bytes 1179648 | tf_op jit(solution)/shard_map/while/body/eval_jaxpr/reduce_scatter | solution.py:65
  594.3 83.4 %copy-start.8 = (bf16[512,384]{1,0:T(8,128)(2,1)}, bf16[512,384]{1,0:T(8,128)(2,1)S(1)}, u32[]{:S(2)}) copy-start(bf16[512,384]{1,0:T(8,128)(2,1)S(1)} %bitcast_select_fusion.4) | copy-start | bytes 1179652 | tf_op jit(solution)/shard_map/while
  639.1 88.1 %reduce-scatter.11.cloned.1.call-start = ((), (), s32[]{:S(2)}) async-start(), calls=%async_computation.9 | async-start | bytes 1179648 | tf_op jit(solution)/shard_map/while/body/eval_jaxpr/reduce_scatter | solution.py:65
  654.5 13.3 %copy-start.25 = (bf16[1,1024,192]{1,2,0:T(8,128)(2,1)S(1)}, bf16[1,1024,192]{1,2,0:T(8,128)(2,1)}, u32[]{:S(2)}) copy-start(bf16[1,1024,192]{1,2,0:T(8,128)(2,1)} %get-tuple-element.1902) | copy-start | bytes 1179652 | tf_op jit(solution)/shard_map/while
  665.1 23.7 %copy-start.44 = (f32[3,1024]{1,0:T(4,128)}, f32[3,1024]{1,0:T(4,128)S(1)}, u32[]{:S(2)}) copy-start(f32[3,1024]{1,0:T(4,128)S(1)} %get-tuple-element.1901) | copy-start | bytes 36868 | tf_op jit(solution)/shard_map/while
  714.8 15.9 %copy-start.5 = (f32[512,384]{1,0:T(8,128)S(1)}, f32[512,384]{1,0:T(8,128)}, u32[]{:S(2)}) copy-start(f32[512,384]{1,0:T(8,128)} %copy-done.4) | copy-start | bytes 2359300 | tf_op jit(solution)/shard_map/while
  714.8 15.9 %copy-start.9 = (bf16[512,384]{1,0:T(8,128)(2,1)S(1)}, bf16[512,384]{1,0:T(8,128)(2,1)}, u32[]{:S(2)}) copy-start(bf16[512,384]{1,0:T(8,128)(2,1)} %copy-done.8) | copy-start | bytes 1179652 | tf_op jit(solution)/shard_map/while
  717.3 17.2 %copy-start.7 = (bf16[1024,384]{1,0:T(8,128)(2,1)S(1)}, bf16[1024,384]{1,0:T(8,128)(2,1)}, u32[]{:S(2)}) copy-start(bf16[1024,384]{1,0:T(8,128)(2,1)} %copy-done.6) | copy-start | bytes 2359300 | tf_op jit(solution)/shard_map/while
  733.2 3.7 collective-permute-start.1
  737.0 96.8 %copy-start.1 = (f32[2,512,384]{2,1,0:T(8,128)}, f32[2,512,384]{2,1,0:T(8,128)S(1)}, u32[]{:S(2)}) copy-start(f32[2,512,384]{2,1,0:T(8,128)S(1)} %get-tuple-element.2097) | copy-start | bytes 4718596 | tf_op jit(solution)/shard_map/while
  737.0 94.7 %reduce-scatter.9.cloned.1.call-start = ((), (), s32[]{:S(2)}) async-start(), calls=%async_computation.8 | async-start | bytes 1179648 | tf_op jit(solution)/shard_map/while/body/eval_jaxpr/reduce_scatter | solution.py:65
  751.7 83.4 %copy-start.8 = (bf16[512,384]{1,0:T(8,128)(2,1)}, bf16[512,384]{1,0:T(8,128)(2,1)S(1)}, u32[]{:S(2)}) copy-start(bf16[512,384]{1,0:T(8,128)(2,1)S(1)} %bitcast_select_fusion.4) | copy-start | bytes 1179652 | tf_op jit(solution)/shard_map/while
  796.5 88.0 %reduce-scatter.11.cloned.1.call-start = ((), (), s32[]{:S(2)}) async-start(), calls=%async_computation.9 | async-start | bytes 1179648 | tf_op jit(solution)/shard_map/while/body/eval_jaxpr/reduce_scatter | solution.py:65
  822.5 23.7 %copy-start.44 = (f32[3,1024]{1,0:T(4,128)}, f32[3,1024]{1,0:T(4,128)S(1)}, u32[]{:S(2)}) copy-start(f32[3,1024]{1,0:T(4,128)S(1)} %get-tuple-element.1901) | copy-start | bytes 36868 | tf_op jit(solution)/shard_map/while
  872.2 15.9 %copy-start.5 = (f32[512,384]{1,0:T(8,128)S(1)}, f32[512,384]{1,0:T(8,128)}, u32[]{:S(2)}) copy-start(f32[512,384]{1,0:T(8,128)} %copy-done.4) | copy-start | bytes 2359300 | tf_op jit(solution)/shard_map/while
  872.2 15.9 %copy-start.9 = (bf16[512,384]{1,0:T(8,128)(2,1)S(1)}, bf16[512,384]{1,0:T(8,128)(2,1)}, u32[]{:S(2)}) copy-start(bf16[512,384]{1,0:T(8,128)(2,1)} %copy-done.8) | copy-start | bytes 1179652 | tf_op jit(solution)/shard_map/while
  874.7 17.2 %copy-start.7 = (bf16[1024,384]{1,0:T(8,128)(2,1)S(1)}, bf16[1024,384]{1,0:T(8,128)(2,1)}, u32[]{:S(2)}) copy-start(bf16[1024,384]{1,0:T(8,128)(2,1)} %copy-done.6) | copy-start | bytes 2359300 | tf_op jit(solution)/shard_map/while
  890.5 3.7 collective-permute-start.1
  894.3 85.0 %all-reduce.7.cloned.1.call-start = ((), (), s32[]{:S(2)}) async-start(), calls=%async_computation.5 | async-start | bytes 2359296 | tf_op jit(solution)/shard_map/psum | solution.py:497
  894.9 240.7 %all-reduce.5.cloned.1.call-start = ((), (), s32[]{:S(2)}) async-start(), calls=%async_computation.4 | async-start | bytes 14155776 | tf_op jit(solution)/shard_map/psum | solution.py:498
  901.1 36.5 %copy-start.51 = (f32[2,384]{1,0:T(2,128)S(1)}, f32[2,384]{1,0:T(2,128)}, u32[]{:S(2)}) copy-start(f32[2,384]{1,0:T(2,128)} %get-tuple-element.1269) | copy-start | bytes 9220
  902.5 73.3 %collective-permute-start.3 = (bf16[1,512,384]{2,1,0:T(8,128)(2,1)S(1)}, bf16[1,512,384]{2,1,0:T(8,128)(2,1)S(1)}, u32[]{:S(2)}, u32[]{:S(2)}) collective-permute-start(bf16[1,512,384]{2,1,0:T(8,128)(2,1)S(1)} %slice_select_fusion.2), channel_id=1, source_target_pairs={{0,2},{2,0},{1,3},{3,1},{4,6},{6,4},{5,7},{7,5},{8,10},{10,8},{9,1... | collective-permute-start | bytes 1179656 | tf_op jit(solution)/shard_map/ppermute | solution.py:17
  (121 other events, 541.5 us)
Sparse Core Ops, SparseCore 0:
  60.9 27.5 reduce-scatter.4
  117.5 26.0 reduce-scatter.6
  189.6 26.0 reduce-scatter.4
  244.8 26.0 reduce-scatter.6
  316.9 26.0 reduce-scatter.4
  372.0 26.0 reduce-scatter.6
  488.3 17.4 reduce-scatter.8
  552.3 17.4 reduce-scatter.10
  639.2 17.4 reduce-scatter.8
  709.5 17.6 reduce-scatter.10
  796.6 17.4 reduce-scatter.8
  866.9 17.6 reduce-scatter.10
Sparse Core Ops, SparseCore 1:
  898.8 80.4 all-reduce.6
  984.8 150.7 all-reduce.4
where the time goes:
time: 1170 us; the launch traced here: 1150 us
  waiting for transfers between devices  338 us (29%)
  matrix products  302 us (26%)
  blocking collectives  239 us (20%)
  other arithmetic  136 us (12%)
  local copies, waits for them, and re-layouts  82.5 us (7%)
  loops' own time  25.3 us (2%)
  between operations  15.9 us (1%)
  starting transfers between devices  13.1 us (1%)
    psum x1, waiting for transfers between devices, per_device(): lax.psum((grad_sums[3], grad_sums[4], grad_sums[5], grad_sums[6], grad_su...  156 us
    reduce_scatter x6, waiting for transfers between devices, scatter_rows(): lax.psum_scatter(term_fn(jnp.int32(0), lax.axis_size('tensor') * row_coun...  139 us
    all_gather x6, blocking collectives, gather_rows(): return lax.all_gather(local_rows, 'tensor', axis=0, tiled=True)  71.2 us
    sub x6, matrix products, attend(): exp_scores = jnp.exp(scores - maxima)  65.4 us
    all_gather x6, blocking collectives, gather_grads(): return lax.all_gather(local_rows, 'tensor', axis=0, tiled=True)  55.5 us
    dot_general x3, matrix products, dense_side(): dense_pre = jnp.dot(z_full, mlp_in, preferred_element_type=jnp.float32)  53.2 us
    psum x1, blocking collectives, per_device(): gain_total = lax.psum(grad_sums[0], ('dp', 'tensor'))  38.2 us
    dot_general x6, matrix products, attend(): jnp.einsum('hqk,khd->qhd', attn_probs.astype(jnp.bfloat16), value_rows, p...  37.1 us
  transfers between devices with their start and end apart: 22, of which 15 were waited for; matrix products, arithmetic and copies ran while one was open for 12% of the time, Pallas kernels for 0%

commit v1 on v0

v1 whole, which is shorter than its diff:
```python
import functools

import jax
import jax.numpy as jnp
from jax import lax
from jax.experimental import pallas as pl
from jax.experimental.pallas import tpu as pltpu
from jax.sharding import PartitionSpec as P

HD = 64
IMAGES = 8
MOST = 256
LANES = 128
SLOTS = 16
EPSILON = 1e-06
BF = jnp.bfloat16
F32 = jnp.float32


def dot(a, b):
    return jnp.dot(a, b, preferred_element_type=F32)


def dot_t(a, b):
    return lax.dot_general(a, b, (((1,), (1,)), ((), ())), preferred_element_type=F32)


def t_dot(a, b):
    return lax.dot_general(a, b, (((0,), (0,)), ((), ())), preferred_element_type=F32)


def normalise(x):
    centred = x - jnp.mean(x, axis=-1, keepdims=True)
    scale = lax.rsqrt(jnp.mean(centred * centred, axis=-1, keepdims=True) + EPSILON)
    return centred * scale, scale


def norm_back(x, gain, gz):
    unit, scale = normalise(x)
    scaled = gz * gain
    mean_plain = jnp.mean(scaled, axis=-1, keepdims=True)
    mean_unit = jnp.mean(scaled * unit, axis=-1, keepdims=True)
    return scale * (scaled - mean_plain - unit * mean_unit), jnp.sum(gz * unit, axis=0, keepdims=True)


def gelu_parts(u):
    cdf = 0.5 * (1.0 + lax.erf(u * 0.7071067811865476))
    return u * cdf, cdf + u * (0.3989422804014327 * jnp.exp(-0.5 * u * u))


def pair_up(tile):
    row = lax.broadcasted_iota(jnp.int32, tile.shape, 0)
    zero = jnp.zeros_like(tile)
    return jnp.concatenate([jnp.where(row < HD, tile, zero), jnp.where(row >= HD, tile, zero)], axis=1)


def pair_down(both):
    n = both.shape[1] // 2
    row = lax.broadcasted_iota(jnp.int32, (both.shape[0], n), 0)
    return jnp.where(row < HD, both[:, :n], both[:, n:])


def bands(window):
    reach = MOST // LANES
    found, at = [], 0
    for i in range(window // LANES):
        first = max(0, i - reach) * LANES
        count = min(window, (i + reach + 1) * LANES) - first
        found.append((i * LANES, first, count, at))
        at += count
    return found, at


def compute_kernel(
    xw, cw, ids, gains, wqkv, wo, mi, mo, routert, ei, eo,
    act, pg, grad_attn, grad_mi, grad_mot, packs, small,
    z, x1, sent, x3, qt, kt, vt, kr, vr, ot, pt, tok, hidden, slope, gx, low, got, gt, gtok, gk_sum, gv_sum,
    bias, own, mixing, eslope, eout,
):
    window, width = xw.shape
    half = window // 2
    pairs = width // LANES
    total = ids.shape[1]
    tensor = lax.axis_index("tensor")
    section = lax.axis_index("section")
    blocks, _ = bands(window)
    row_blocks = window // LANES

    def rows(i, n=LANES):
        return pl.ds(pl.multiple_of(i * n, n), n)

    def loop(n, body):
        def step(i, carry):
            body(i)
            return carry

        lax.fori_loop(0, n, step, 0)

    ids_row = ids[pl.ds(section, 1), :].astype(F32)
    image = lax.broadcasted_iota(jnp.int32, (SLOTS, total), 0).astype(F32)
    spread = jnp.broadcast_to(ids_row, (SLOTS, total))
    middle = jnp.sum((spread < image).astype(F32) + (spread <= image).astype(F32), axis=1, keepdims=True)
    first_half = (middle < total).astype(F32)
    mine = jnp.where(tensor == 0, first_half, 1.0 - first_half)
    start = pl.multiple_of(tensor * (total - window), LANES)
    window_ids = ids[pl.ds(section, 1), pl.ds(start, window)].astype(F32)
    member = (jnp.broadcast_to(window_ids, (SLOTS, window)) == image[:, :window]).astype(F32)
    own_row = jnp.sum(member * mine, axis=0, keepdims=True)
    own[...] = jnp.broadcast_to(own_row, (LANES, window)).T
    ids_col = jnp.broadcast_to(window_ids, (LANES, window)).T
    for q0, k0, count, at in blocks:
        same = ids_col[k0 : k0 + count] == jnp.broadcast_to(window_ids[:, q0 : q0 + LANES], (count, LANES))
        bias[at : at + count, :] = jnp.where(same, 0.0, -1e30)

    def attention(b, x_of, out_ref):
        def norm(i):
            unit, _ = normalise(x_of(rows(i)))
            z[2 * b, rows(i)] = (unit * gains[2 * b : 2 * b + 1, :]).astype(BF)

        loop(row_blocks, norm)
        zz = z[2 * b]
        for c, dest in enumerate((qt, kt, vt)):
            tall = dot_t(wqkv[b, c * width : (c + 1) * width], zz)
            tall = (tall.astype(BF) * jnp.asarray(HD**-0.5 if c == 0 else 1.0, BF)).reshape(pairs, LANES, window)
            dest[b] = tall
        for c, dest in ((1, kr), (2, vr)):
            flat = dot_t(zz, wqkv[b, c * width : (c + 1) * width]).astype(BF)
            for j in range(pairs):
                dest[b, j] = flat[:, j * LANES : (j + 1) * LANES]

        def pair(j):
            for q0, k0, count, at in blocks:
                scores = dot(kr[b, j, k0 : k0 + count, :], pair_up(qt[b, j, :, q0 : q0 + LANES]))
                veil = bias[at : at + count, :]
                scores = scores + jnp.concatenate([veil, veil], axis=1)
                powers = jnp.exp(scores - jnp.max(scores, axis=0, keepdims=True))
                probs = (powers * (1.0 / jnp.sum(powers, axis=0, keepdims=True))).astype(BF)
                pt[b, j, at : at + count, :] = probs
                ot[b, j, :, q0 : q0 + LANES] = pair_down(dot(vt[b, j, :, k0 : k0 + count], probs)).astype(BF)

        loop(pairs, pair)
        for j in range(pairs):
            tok[:, j * LANES : (j + 1) * LANES] = ot[b, j].T

        def out(i):
            out_ref[rows(i, half)] = x_of(rows(i, half)) + dot(tok[rows(i, half)], wo[b])

        loop(2, out)

    def attention_back(b, x_of):
        ga = low[...]
        got[...] = dot_t(wo[b], ga).astype(BF).reshape(pairs, LANES, window)
        for j in range(pairs):
            piece = dot(ot[b, j], ga).astype(BF)
            put_grad(b, 3, j, piece)

        def pair(j):
            gk_sum[...] = jnp.zeros_like(gk_sum)
            gv_sum[...] = jnp.zeros_like(gv_sum)
            for q0, k0, count, at in blocks:
                go_pair = pair_up(got[j, :, q0 : q0 + LANES])
                q_pair = pair_up(qt[b, j, :, q0 : q0 + LANES])
                low_probs = pt[b, j, at : at + count, :]
                probs = low_probs.astype(F32)
                weighted = dot(vr[b, j, k0 : k0 + count, :], go_pair) * probs
                inner = jnp.sum(weighted, axis=0, keepdims=True)
                gs = (weighted - probs * inner).astype(BF)
                gq = pair_down(dot(kt[b, j, :, k0 : k0 + count], gs)) * HD**-0.5
                gt[pl.ds(pl.multiple_of(j * LANES, LANES), LANES), q0 : q0 + LANES] = gq.astype(BF)
                gk_sum[k0 : k0 + count] += dot_t(gs, q_pair)
                gv_sum[k0 : k0 + count] += dot_t(low_probs, go_pair)
            for c, total_of in ((1, gk_sum), (2, gv_sum)):
                gtok[c * pairs + j] = total_of[...].astype(BF)

        loop(pairs, pair)
        for j in range(pairs):
            gtok[j] = gt[j * LANES : (j + 1) * LANES].T
        for c in (1, 2):
            for j in range(pairs):
                at = (c * pairs + j) * LANES
                gt[at : at + LANES] = gtok[c * pairs + j].T
        zz = z[2 * b]
        for c in range(3):
            for j in range(pairs):
                at = (c * pairs + j) * LANES
                put_grad(b, c, j, dot(gt[at : at + LANES], zz).astype(BF))
        gain = gains[2 * b : 2 * b + 1, :]
        gain_grad = jnp.zeros((1, width), F32)

        def back(i, gain_grad):
            wide = jnp.concatenate([gtok[c, rows(i, half)] for c in range(3 * pairs)], axis=1)
            step, part = norm_back(x_of(rows(i, half)), gain, dot(wide, wqkv[b]))
            gx[rows(i, half)] += step
            return gain_grad + part

        small[2 * b : 2 * b + 1, :] = lax.fori_loop(0, 2, back, gain_grad)

    def put_grad(b, c, j, piece):
        at = c * 3 * HD
        if j < 2:
            grad_attn[b, j, at : at + 2 * HD, :] = piece
        else:
            for t in range(2):
                grad_attn[b, t, at + 2 * HD : at + 3 * HD, :] = piece[t * HD : (t + 1) * HD]

    attention(0, lambda r: xw[r].astype(F32), x1)

    def norm_middle(source, which):
        def body(i):
            unit, _ = normalise(source[rows(i)])
            z[which, rows(i)] = (unit * gains[which : which + 1, :]).astype(BF)

        loop(row_blocks, body)

    norm_middle(x1, 1)
    chunk = 256
    chunks = mi.shape[2] // chunk

    def hidden_chunk(i):
        part, at = i // chunks, pl.multiple_of(i % chunks * chunk, chunk)
        value, grad = gelu_parts(dot(z[1], mi[part, :, pl.ds(at, chunk)]))
        hidden[i] = value.astype(BF)
        slope[i] = grad

    loop(2 * chunks, hidden_chunk)

    def dense_out(i):
        h = jnp.concatenate([hidden[c, rows(i, half)] for c in range(2 * chunks)], axis=1)
        sent[rows(i, half)] = (x1[rows(i, half)] + dot(h, mo[...])).astype(BF)

    loop(2, dense_out)

    attention(1, lambda r: sent[r].astype(F32), x3)
    norm_middle(x3, 3)
    z3 = z[3]
    logits = dot_t(routert[...], z3)
    powers = [jnp.exp(logits[e : e + 1, :]) for e in range(2)]
    dispatch, combine = [], []
    for e in range(2):
        totals = jnp.sum(member * powers[e], axis=1, keepdims=True)
        dispatch.append(powers[e] / jnp.sum(member * totals, axis=0, keepdims=True))
        combine.append(powers[e] / (powers[0] + powers[1]))
        d_low = (member * dispatch[e].astype(BF).astype(F32)).astype(BF)
        c_low = (member * combine[e].astype(BF).astype(F32)).astype(BF)
        mixing[0, e * SLOTS : (e + 1) * SLOTS] = d_low
        mixing[1, e * SLOTS : (e + 1) * SLOTS] = c_low
        packs[e, :SLOTS] = dot(d_low, z3).astype(BF)
    for e in range(2):
        value, grad = gelu_parts(dot(packs[e, :SLOTS], ei[e]))
        eslope[e] = grad
        eout[e * SLOTS : (e + 1) * SLOTS] = dot(value.astype(BF), eo[e]).astype(BF)

    def finish(i):
        mixed = t_dot(mixing[1, :, pl.ds(pl.multiple_of(i * LANES, LANES), LANES)], eout[...])
        act[rows(i)] = (x3[rows(i)] + mixed).astype(BF)
        wide = jnp.concatenate([own[rows(i)]] * pairs, axis=1)
        low[rows(i)] = jnp.where(wide > 0.0, cw[rows(i)].astype(F32), 0.0).astype(BF)

    loop(row_blocks, finish)

    gy = low[...]
    slot_grads, logit_grads = [], []
    per_token = []
    for e in range(2):
        part = slice(e * SLOTS, (e + 1) * SLOTS)
        per_token.append(jnp.sum(dot_t(eout[part], gy) * member, axis=0, keepdims=True))
        packs[e, SLOTS:] = dot(mixing[1, part], gy).astype(BF)
    inner = combine[0] * per_token[0] + combine[1] * per_token[1]
    for e in range(2):
        g_hidden = dot_t(packs[e, SLOTS:], eo[e])
        slot_grad = dot_t((g_hidden * eslope[e]).astype(BF), ei[e]).astype(BF)
        slot_grads.append(slot_grad)
        g_dispatch = jnp.sum(dot_t(slot_grad, z3) * member, axis=0, keepdims=True)
        weighted = dispatch[e] * g_dispatch
        sums = jnp.sum(member * weighted, axis=1, keepdims=True)
        from_dispatch = weighted - dispatch[e] * jnp.sum(member * sums, axis=0, keepdims=True)
        logit_grads.append(combine[e] * (per_token[e] - inner) + from_dispatch)
    which = lax.broadcasted_iota(jnp.int32, (SLOTS, window), 0)
    logit_grad = jnp.where(which == 0, logit_grads[0], jnp.where(which == 1, logit_grads[1], 0.0)).astype(BF)
    small[4:6, :] = dot(logit_grad, z3)[:2]
    small[6:8, :] = jnp.zeros((2, width), F32)
    mixing[1, :SLOTS] = logit_grad
    slots_and_router = jnp.concatenate(slot_grads + [routert[...]], axis=0)

    def experts_back(i, gain_grad):
        at = pl.ds(pl.multiple_of(i * LANES, LANES), LANES)
        parts = jnp.concatenate([mixing[0, :, at], mixing[1, :SLOTS, at]], axis=0)
        step, part = norm_back(x3[rows(i)], gains[3:4, :], t_dot(parts, slots_and_router))
        total_of = low[rows(i)].astype(F32) + step
        gx[rows(i)] = total_of
        low[rows(i)] = total_of.astype(BF)
        return gain_grad + part

    small[3:4, :] = lax.fori_loop(0, row_blocks, experts_back, jnp.zeros((1, width), F32))
    attention_back(1, lambda r: sent[r].astype(F32))

    low[...] = gx[...].astype(BF)
    gsent = low[...]
    gsent_t = gsent.T
    z2 = z[1]
    z2_t = z2.T

    def hidden_back(i):
        part, at = i // chunks, pl.multiple_of(i % chunks * chunk, chunk)
        lanes = pl.ds(pl.multiple_of(i * chunk, chunk), chunk)
        grad_mot[:, lanes] = dot(gsent_t, hidden[i]).astype(BF)
        g_hidden = dot_t(gsent, mo[pl.ds(pl.multiple_of(i * chunk, chunk), chunk), :])
        g_pre = (g_hidden * slope[i]).astype(BF)
        hidden[i] = g_pre
        grad_mi[:, lanes] = dot(z2_t, g_pre).astype(BF)

    loop(2 * chunks, hidden_back)

    def dense_back(i, gain_grad):
        gz = jnp.zeros((half, width), F32)
        for part in range(2):
            g = jnp.concatenate([hidden[part * chunks + c, rows(i, half)] for c in range(chunks)], axis=1)
            gz = gz + dot_t(g, mi[part])
        step, part = norm_back(x1[rows(i, half)], gains[1:2, :], gz)
        total_of = low[rows(i, half)].astype(F32) + step
        gx[rows(i, half)] = total_of
        low[rows(i, half)] = total_of.astype(BF)
        return gain_grad + part

    small[1:2, :] = lax.fori_loop(0, 2, dense_back, jnp.zeros((1, width), F32))
    attention_back(0, lambda r: xw[r].astype(F32))
    pg[...] = gx[...].astype(BF)


def compute(xw, cw, ids, gains, wqkv, wo, mi, mo, routert, ei, eo):
    window, width = xw.shape
    pairs = width // LANES
    ff = ei.shape[2]
    _, kept = bands(window)
    chunk_count = 2 * mi.shape[2] // 256
    vmem = pl.BlockSpec(memory_space=pltpu.VMEM)
    return pl.pallas_call(
        compute_kernel,
        out_shape=(
            jax.ShapeDtypeStruct((window, width), BF),
            jax.ShapeDtypeStruct((window, width), BF),
            jax.ShapeDtypeStruct((2, 2, 2 * width, width), BF),
            jax.ShapeDtypeStruct((width, ff), BF),
            jax.ShapeDtypeStruct((width, ff), BF),
            jax.ShapeDtypeStruct((2, 2 * SLOTS, width), BF),
            jax.ShapeDtypeStruct((8, width), F32),
        ),
        in_specs=[vmem] * 11,
        out_specs=[vmem] * 7,
        scratch_shapes=[
            pltpu.VMEM((4, window, width), BF),
            pltpu.VMEM((window, width), F32),
            pltpu.VMEM((window, width), BF),
            pltpu.VMEM((window, width), F32),
            pltpu.VMEM((2, pairs, LANES, window), BF),
            pltpu.VMEM((2, pairs, LANES, window), BF),
            pltpu.VMEM((2, pairs, LANES, window), BF),
            pltpu.VMEM((2, pairs, window, LANES), BF),
            pltpu.VMEM((2, pairs, window, LANES), BF),
            pltpu.VMEM((2, pairs, LANES, window), BF),
            pltpu.VMEM((2, pairs, kept, 2 * LANES), BF),
            pltpu.VMEM((window, width), BF),
            pltpu.VMEM((chunk_count, window, 256), BF),
            pltpu.VMEM((chunk_count, window, 256), F32),
            pltpu.VMEM((window, width), F32),
            pltpu.VMEM((window, width), BF),
            pltpu.VMEM((pairs, LANES, window), BF),
            pltpu.VMEM((3 * width, window), BF),
            pltpu.VMEM((3 * pairs, window, LANES), BF),
            pltpu.VMEM((window, LANES), F32),
            pltpu.VMEM((window, LANES), F32),
            pltpu.VMEM((kept, LANES), F32),
            pltpu.VMEM((window, LANES), F32),
            pltpu.VMEM((2, 2 * SLOTS, window), BF),
            pltpu.VMEM((2, SLOTS, ff), F32),
            pltpu.VMEM((2 * SLOTS, width), BF),
        ],
        compiler_params=pltpu.CompilerParams(vmem_limit_bytes=60 * 1024 * 1024),
    )(xw, cw, ids, gains, wqkv, wo, mi, mo, routert, ei, eo)


def per_device(
    patches, image_ids, cotangent, norm_gains, qkv_weight, out_weight, mlp_in, mlp_out, router, expert_in, expert_out
):
    row_count, width = patches.shape[1:]
    tensor = lax.axis_index("tensor")
    tensors = lax.axis_size("tensor")
    extra = MOST // 2

    def swap(a):
        return lax.ppermute(a, "tensor", [(i, i ^ 1) for i in range(tensors)])

    def edge(a):
        return jnp.where(tensor == 0, a[-extra:], a[:extra])

    def widen(a):
        other = swap(edge(a))
        return jnp.where(tensor == 0, jnp.concatenate([a, other]), jnp.concatenate([other, a]))

    xw, cw = widen(patches[0]), widen(cotangent[0])

    def gathered(a, axes):
        for axis in axes:
            a = lax.all_gather(a, axis)
        return a

    heads = qkv_weight.shape[3] // HD
    tall = jnp.transpose(qkv_weight[0], (1, 2, 0)).reshape(3, heads, HD, width)
    tall = gathered(tall, ("tensor", "section"))

    def by_pairs(a):
        n = a.shape[2]
        a0, a1 = a[:, 0], a[:, 1]
        order = [a0[:, :, 0], a0[:, :, 1], a1[:, :, 0], a1[:, :, 1], a0[:, :, 2], a1[:, :, 2]]
        return jnp.stack(order, axis=2).reshape(a.shape[0], n * 2 * heads * HD, width)

    wqkv = by_pairs(tall)
    wo = by_pairs(gathered(out_weight[0].reshape(1, heads, HD, width), ("tensor", "section")))
    mi = gathered(mlp_in, ("tensor",))
    mo = gathered(mlp_out, ("tensor",)).reshape(-1, width)
    routert = gathered(router.T, ("tensor",)).reshape(-1, width)
    routert = jnp.pad(routert, ((0, SLOTS - routert.shape[0]), (0, 0)))
    ei = gathered(expert_in[0], ("tensor",))
    eo = gathered(expert_out[0], ("tensor",))
    gains = gathered(norm_gains[0], ("section",)).reshape(-1, width)

    act, pg, grad_attn, grad_mi, grad_mot, packs, small = compute(
        xw, cw, image_ids, gains, wqkv, wo, mi, mo, routert, ei, eo
    )

    ids_row = lax.dynamic_index_in_dim(image_ids, lax.axis_index("section"), 0, keepdims=False)
    total = ids_row.shape[0]
    of_image = jnp.arange(IMAGES)
    middle = jnp.sum(ids_row[None] < of_image[:, None], axis=1) + jnp.sum(ids_row[None] <= of_image[:, None], axis=1)
    is_first = jnp.sum((ids_row[:, None] == of_image[None]) * (middle < total)[None], axis=1)
    mine = lax.dynamic_slice_in_dim(is_first == (1 - tensor), tensor * row_count, row_count, 0)

    def merge(a):
        sent_out = jnp.where(tensor == 0, a[-extra:], a[:extra])
        arrived = swap(sent_out)
        own = jnp.where(tensor == 0, a[:row_count], a[extra:])
        blank = jnp.zeros((row_count - extra, width), a.dtype)
        other = jnp.where(tensor == 0, jnp.concatenate([blank, arrived]), jnp.concatenate([arrived, blank]))
        return jnp.where(mine[:, None], own, other)[None]

    activations, patch_grad = merge(act), merge(pg)

    rest = tuple(n for n in ("dp", "section", "tensor"))
    small = lax.psum(small, rest)
    gains_grad = lax.dynamic_slice_in_dim(small, 2 * lax.axis_index("section"), 2, 0)[None]
    router_grad = lax.dynamic_slice_in_dim(small, 4 + tensor, 1, 0).T
    grad_attn = lax.psum(grad_attn.astype(F32), rest)
    attn = lax.dynamic_index_in_dim(grad_attn, lax.axis_index("section"), 0, keepdims=False)
    attn = lax.dynamic_index_in_dim(attn, tensor, 0, keepdims=False)
    rows = 3 * heads * HD
    qkv_grad = jnp.transpose(attn[:rows].reshape(3, heads * HD, width), (2, 0, 1))[None]
    out_grad = attn[rows:][None]
    grad_mi = lax.psum(grad_mi.astype(F32), rest)
    grad_mot = lax.psum(grad_mot.astype(F32), rest)
    part = mlp_in.shape[1]
    mlp_in_grad = lax.dynamic_slice_in_dim(grad_mi, tensor * part, part, 1)
    mlp_out_grad = lax.dynamic_slice_in_dim(grad_mot, tensor * part, part, 1).T
    packs = lax.all_gather(packs, rest)
    packs = lax.dynamic_index_in_dim(packs, tensor, 1, keepdims=False)
    slots = packs[:, :SLOTS].reshape(-1, width)
    geo = packs[:, SLOTS:].reshape(-1, width)
    value, slope = gelu_parts(dot(slots, expert_in[0]))
    g_pre = (dot_t(geo, expert_out[0]) * slope).astype(BF)
    expert_in_grad = t_dot(slots, g_pre)[None]
    expert_out_grad = t_dot(value.astype(BF), geo)[None]
    return (
        activations, patch_grad, gains_grad, qkv_grad, out_grad, mlp_in_grad, mlp_out_grad, router_grad,
        expert_in_grad, expert_out_grad,
    )


def solution(mesh):
    return jax.shard_map(
        per_device,
        mesh=mesh,
        in_specs=(
            P(("dp", "section"), "tensor", None),
            P("dp", None),
            P(("dp", "section"), "tensor", None),
            P("section", None, None),
            P("section", None, None, "tensor"),
            P("section", "tensor", None),
            P(None, "tensor"),
            P("tensor", None),
            P(None, "tensor"),
            P("tensor", None, None),
            P("tensor", None, None),
        ),
        out_specs=(
            P(("dp", "section"), "tensor", None),
            P(("dp", "section"), "tensor", None),
            P("section", None, None),
            P("section", None, None, "tensor"),
            P("section", "tensor", None),
            P(None, "tensor"),
            P("tensor", None),
            P(None, "tensor"),
            P("tensor", None, None),
            P("tensor", None, None),
        ),
        check_vma=False,
    )
```

time: 1170 us -> 441 us (0.38); the launches traced: 1150 us -> 440 us
  matrix products: 302 us -> 10.5 us
  waiting for transfers between devices: 338 us -> 110 us
  other arithmetic: 136 us -> 7.65 us
  Pallas kernels: 0 us -> 71.6 us
  local copies, waits for them, and re-layouts: 82.5 us -> 14.5 us
  blocking collectives: 239 us -> 207 us
  loops' own time: 25.3 us -> 0 us
    dot_general x57 -> x3, matrix products: 222 us -> 10.5 us  [the longest x2 8.25 us: t_dot(): lax.dot_general(a, b, (((0,), (0,)), ((), ())), preferred_element_type=F32)]
    reduce_scatter x12 -> x0, waiting for transfers between devices: 172 us -> none  [the longest x6 139 us: scatter_rows(): lax.psum_scatter(term_fn(jnp.int32(0), lax.axis_size('tensor') * row_coun...]
    psum x2 -> x0, waiting for transfers between devices: 159 us -> none  [the longest x1 156 us: per_device(): lax.psum((grad_sums[3], grad_sums[4], grad_sums[5], grad_sums[6], grad_su...]
    all_gather x21 -> x5, blocking collectives: 166 us -> 33.9 us  [gathered(): a = lax.all_gather(a, axis)]
    all_gather x0 -> x6, waiting for transfers between devices: none -> 108 us  [the longest x5 108 us: gathered(): a = lax.all_gather(a, axis)]
    psum x2 -> x1, blocking collectives: 72.6 us -> 173 us  [per_device(): small = lax.psum(small, rest)]
    pallas_call x0 -> x1, Pallas kernels: none -> 71.6 us  [compute(): pl.pallas_call(compute_kernel, out_shape=(jax.ShapeDtypeStruct((window, w...]
    sub x6 -> x0, matrix products: 65.4 us -> none  [attend(): exp_scores = jnp.exp(scores - maxima)]
  transfers between devices with their start and end apart: 22 -> 10, of which waited for: 15 -> 4; matrix products, arithmetic and copies ran while one was open for 12% -> 5% of each run, Pallas kernels for 0% -> 0%
where the time goes in v1:
time: 441 us; the launch traced here: 440 us
  blocking collectives  207 us (47%)
  waiting for transfers between devices  110 us (25%)
  Pallas kernels  71.6 us (16%)
  local copies, waits for them, and re-layouts  14.5 us (3%)
  between operations  14.4 us (3%)
  matrix products  10.5 us (2%)
  other arithmetic  7.65 us (2%)
  starting transfers between devices  4.52 us (1%)
    psum x1, blocking collectives, per_device(): small = lax.psum(small, rest)  173 us
    all_gather x5, waiting for transfers between devices, gathered(): a = lax.all_gather(a, axis)  108 us
    pallas_call x1, Pallas kernels, compute(): pl.pallas_call(compute_kernel, out_shape=(jax.ShapeDtypeStruct((window, w...  71.6 us
    all_gather x5, blocking collectives, gathered(): a = lax.all_gather(a, axis)  33.9 us
  transfers between devices with their start and end apart: 10, of which 4 were waited for; matrix products, arithmetic and copies ran while one was open for 5% of the time, Pallas kernels for 0%

profile of v1, /device:TPU:0, one launch (start us, length us, event | category | flops | bytes accessed | tf_op | source)
XLA Modules:
  0.0 440.1 jit_solution(14112477339442420393)
XLA Ops:
  7.2 18.5 %all_gather.49 = bf16[2,3,3,64,384]{4,3,2,1,0:T(8,128)(2,1)} all-gather(bf16[1,3,3,64,384]{4,3,2,1,0:T(8,128)(2,1)} %bitcast.78), channel_id=1, replica_groups=mesh['dp'=8,'section'=2,'tensor'=2] {'tensor'}, dimensions={0}, use_global_device_ids=true | all-gather | bytes 1327104 | tf_op jit(solution)/shard_map/all_gather | solution.py:404
  25.7 0.0 all-gather.19.cloned.1.call-start
  25.8 0.7 all-gather.19.cloned.1.call-update
  26.5 0.7 all-gather.21.cloned.1.call-update
  27.3 0.5 all-gather.13.cloned.1.call-update
  27.8 0.5 all-gather.15.cloned.1.call-update
  28.4 0.0 all-gather.23.cloned.1.call-start
  28.5 0.1 collective-permute-start
  28.6 2.1 collective-permute-start.1
  30.7 7.1 %all_gather.52 = bf16[2,1,3,64,384]{4,3,2,1,0:T(8,128)(2,1)S(1)} all-gather(bf16[1,1,3,64,384]{4,3,2,1,0:T(8,128)(2,1)S(1)} %bitcast.82), channel_id=1, replica_groups=mesh['dp'=8,'section'=2,'tensor'=2] {'tensor'}, dimensions={0}, use_global_device_ids=true | all-gather | bytes 442368 | tf_op jit(solution)/shard_map/all_gather | solution.py:404
  37.8 2.2 all-gather.1
  40.0 0.1 slice_bitcast_fusion.3
  40.2 1.8 all_gather.48
  42.0 0.6 reshape.67.gains
  42.6 4.3 all-gather.4
  47.0 0.6 pad.8.routert
  47.6 0.9 pad_maximum_fusion.1
  48.5 0.9 maximum_select_fusion.xw
  49.4 0.9 maximum_select_fusion.1.cw
  50.3 1.6 slice_bitcast_fusion.1
  52.0 0.1 slice.129
  52.1 0.1 slice.127
  52.2 1.5 pad_maximum_fusion
  53.7 8.1 %all-gather.19.cloned.1.call-done = bf16[768,768]{1,0:T(8,128)(2,1)} async-done(((bf16[384,768]{1,0:T(8,128)(2,1)}), bf16[768,768]{1,0:T(8,128)(2,1)}) %all-gather.19.cloned.1.call-update) | async-done | bytes 1179664 | tf_op jit(solution)/shard_map/all_gather | solution.py:404
  61.8 24.4 %all-gather.21.cloned.1.call-done.mo = bf16[1536,384]{1,0:T(8,128)(2,1)} async-done(((bf16[768,384]{1,0:T(8,128)(2,1)}), bf16[1536,384]{1,0:T(8,128)(2,1)}) %all-gather.21.cloned.1.call-update) | async-done | bytes 1179664 | tf_op jit(solution)/shard_map/all_gather | solution.py:404
  86.2 37.5 %all-gather.13.cloned.1.call-done.ei = bf16[2,384,1536]{2,1,0:T(8,128)(2,1)} async-done(((bf16[1,384,1536]{2,1,0:T(8,128)(2,1)}), bf16[2,384,1536]{2,1,0:T(8,128)(2,1)}) %all-gather.13.cloned.1.call-update) | async-done | bytes 2359312 | tf_op jit(solution)/shard_map/all_gather | solution.py:404
  123.7 37.5 %all-gather.15.cloned.1.call-done.eo = bf16[2,1536,384]{2,1,0:T(8,128)(2,1)} async-done(((bf16[1,1536,384]{2,1,0:T(8,128)(2,1)}), bf16[2,1536,384]{2,1,0:T(8,128)(2,1)}) %all-gather.15.cloned.1.call-update) | async-done | bytes 2359312 | tf_op jit(solution)/shard_map/all_gather | solution.py:404
  161.2 71.6 %shard_map.186 = (bf16[640,384]{1,0:T(8,128)(2,1)}, bf16[640,384]{1,0:T(8,128)(2,1)}, bf16[2,2,768,384]{3,2,1,0:T(8,128)(2,1)}, bf16[384,1536]{1,0:T(8,128)(2,1)...) custom-call(bf16[640,384]{1,0:T(8,128)(2,1)} %maximum_select_fusion.xw, ...), custom_call_target="tpu_custom_call" | custom-call | tf_op jit(solution)/shard_map/pallas_call | solution.py:337
  232.8 0.2 convert_reduce_fusion.1
  233.0 0.1 convert_reduce_fusion
  233.1 0.1 dynamic_slice.30
  233.2 1.0 slice_select_fusion
  234.2 0.4 collective-permute-start.3
  234.5 1.0 slice_select_fusion.1
  235.5 1.8 collective-permute-start.2
  237.3 173.1 %all-reduce.7 = (f32[8,384]{1,0:T(8,128)S(1)}, f32[2,2,768,384]{3,2,1,0:T(8,128)}, f32[384,1536]{1,0:T(8,128)}, f32[384,1536]{1,0:T(8,128)}) all-reduce(f32[8,384]{1,0:T(8,128)} %get-tuple-element.19, bf16[2,2,768,384]{3,2,1,0:T(8,128)(2,1)} %get-tuple-element.20, ...), channel_id=1, replica_groups=mesh['dp'=8,'section'=2,'tensor'=2] {'dp','section','tensor'}, use_global_device_ids=true, to_apply=%region_3.4 | all-reduce | flops 2362368 | bytes 14180352 | tf_op jit(solution)/shard_map/psum | solution.py:449
  410.3 2.8 dynamic-slice_bitcast_fusion
  413.1 1.4 copy.30
  414.5 0.6 dynamic-slice_bitcast_fusion.3
  415.1 1.7 dynamic-slice_bitcast_fusion.2
  416.8 2.1 constant_dynamic-slice_fusion
  418.9 0.6 fusion.11
  419.5 1.2 select_bitcast_fusion
  420.7 1.2 dynamic-slice_bitcast_fusion.1
  421.9 0.8 fusion.14
  422.8 2.2 fusion.5
  425.0 5.0 %convolution_bitcast_fusion.1 = f32[1,384,1536]{2,1,0:T(8,128)} fusion(bf16[512,384]{1,0:T(8,128)(2,1)S(1)} %bitcast.70, f32[512,1536]{1,0:T(8,128)S(1)} %fusion.5, bf16[512,384]{1,0:T(8,128)(2,1)} %bitcast.80, bf16[1,1536,384]{2,1,0:T(8,128)(2,1)} %param.21), kind=kOutput, calls=%fused_computation.10 | convolution fusion | flops 1215823872 | bytes 7471104 | tf_op jit(solution)/shard_map/dot_general | solution.py:29
  430.0 3.3 convolution_bitcast_fusion
  (41 shorter events, 0.5 us)
Async XLA Ops:
  7.2 43.1 %all-gather.17.cloned.1.call-start = ((), (), s32[]{:S(2)}) async-start(), calls=%async_computation.2 | async-start | bytes 2654208 | tf_op jit(solution)/shard_map/all_gather | solution.py:404
  25.7 2.8 copy-start.2
  25.7 2.9 copy-start.3
  25.7 5.0 %copy-start.4 = (bf16[1,192,384]{2,1,0:T(8,128)(2,1)S(1)}, bf16[1,192,384]{2,1,0:T(8,128)(2,1)}, u32[]{:S(2)}) copy-start(bf16[1,192,384]{2,1,0:T(8,128)(2,1)} %param.16) | copy-start | bytes 442372
  25.7 36.1 %all-gather.19.cloned.1.call-start = ((), (), s32[]{:S(2)}) async-start(), calls=%async_computation.3 | async-start | bytes 1769472 | tf_op jit(solution)/shard_map/all_gather | solution.py:404
  26.5 59.7 %all-gather.21.cloned.1.call-start = ((), (), s32[]{:S(2)}) async-start(), calls=%async_computation.4 | async-start | bytes 1769472 | tf_op jit(solution)/shard_map/all_gather | solution.py:404
  27.2 96.5 %all-gather.13.cloned.1.call-start = ((), (), s32[]{:S(2)}) async-start(), calls=%async_computation | async-start | bytes 3538944 | tf_op jit(solution)/shard_map/all_gather | solution.py:404
  27.8 133.4 %all-gather.15.cloned.1.call-start = ((), (), s32[]{:S(2)}) async-start(), calls=%async_computation.1 | async-start | bytes 3538944 | tf_op jit(solution)/shard_map/all_gather | solution.py:404
  28.4 11.8 %copy-start.6 = (f32[1,2,384]{2,1,0:T(2,128)S(1)}, f32[1,2,384]{2,1,0:T(2,128)}, u32[]{:S(2)}) copy-start(f32[1,2,384]{2,1,0:T(2,128)} %param.14) | copy-start | bytes 9220
  28.4 14.2 %copy-start.7 = (bf16[384,1]{0,1:T(2,128)(2,1)S(1)}, bf16[384,1]{0,1:T(2,128)(2,1)}, u32[]{:S(2)}) copy-start(bf16[384,1]{0,1:T(2,128)(2,1)} %param.19) | copy-start | bytes 2308
  28.4 392.3 %all-gather.23.cloned.1.call-start = ((), (), s32[]{:S(2)}) async-start(), calls=%async_computation.5 | async-start | bytes 1622016 | tf_op jit(solution)/shard_map/all_gather | solution.py:463
  28.5 20.0 %collective-permute-start = (bf16[128,384]{1,0:T(8,128)(2,1)S(1)}, bf16[128,384]{1,0:T(8,128)(2,1)S(1)}, u32[]{:S(2)}, u32[]{:S(2)}) collective-permute-start(bf16[128,384]{1,0:T(8,128)(2,1)S(1)} %select_bitcast_fusion.3), channel_id=1, source_target_pairs={{0,1},{1,0},{2,3},{3,2},{4,5},{5,4},{6,7},{7,6},{8,9},{9,8},{10,11... | collective-permute-start | bytes 294920 | tf_op jit(solution)/shard_map/ppermute | solution.py:391
  28.6 20.8 %collective-permute-start.1 = (bf16[128,384]{1,0:T(8,128)(2,1)S(1)}, bf16[128,384]{1,0:T(8,128)(2,1)S(1)}, u32[]{:S(2)}, u32[]{:S(2)}) collective-permute-start(bf16[128,384]{1,0:T(8,128)(2,1)S(1)} %select_bitcast_fusion.2), channel_id=1, source_target_pairs={{0,1},{1,0},{2,3},{3,2},{4,5},{5,4},{6,7},{7,6},{8,9},{9,8},{10,11... | collective-permute-start | bytes 294920 | tf_op jit(solution)/shard_map/ppermute | solution.py:391
  161.2 71.6 %copy-start.5 = (s32[2,1024]{1,0:T(2,128)S(1)}, s32[2,1024]{1,0:T(2,128)}, u32[]{:S(2)}) copy-start(s32[2,1024]{1,0:T(2,128)} %ids.1) | copy-start | bytes 24580
  234.2 185.4 %collective-permute-start.3 = (bf16[128,384]{1,0:T(8,128)(2,1)S(1)}, bf16[128,384]{1,0:T(8,128)(2,1)S(1)}, u32[]{:S(2)}, u32[]{:S(2)}) collective-permute-start(bf16[128,384]{1,0:T(8,128)(2,1)S(1)} %slice_select_fusion), channel_id=1, source_target_pairs={{0,1},{1,0},{2,3},{3,2},{4,5},{5,4},{6,7},{7,6},{8,9},{9,8},{10,11... | collective-permute-start | bytes 294920 | tf_op jit(solution)/shard_map/ppermute | solution.py:391
  235.5 184.0 %collective-permute-start.2 = (bf16[128,384]{1,0:T(8,128)(2,1)S(1)}, bf16[128,384]{1,0:T(8,128)(2,1)S(1)}, u32[]{:S(2)}, u32[]{:S(2)}) collective-permute-start(bf16[128,384]{1,0:T(8,128)(2,1)S(1)} %slice_select_fusion.1), channel_id=1, source_target_pairs={{0,1},{1,0},{2,3},{3,2},{4,5},{5,4},{6,7},{7,6},{8,9},{9,8},{10,11... | collective-permute-start | bytes 294920 | tf_op jit(solution)/shard_map/ppermute | solution.py:391
  413.1 6.4 %copy-start = (bf16[640,384]{1,0:T(8,128)(2,1)S(1)}, bf16[640,384]{1,0:T(8,128)(2,1)}, u32[]{:S(2)}) copy-start(bf16[640,384]{1,0:T(8,128)(2,1)} %get-tuple-element.17) | copy-start | bytes 1474564
  413.1 6.4 %copy-start.1 = (bf16[640,384]{1,0:T(8,128)(2,1)S(1)}, bf16[640,384]{1,0:T(8,128)(2,1)}, u32[]{:S(2)}) copy-start(bf16[640,384]{1,0:T(8,128)(2,1)} %get-tuple-element.18) | copy-start | bytes 1474564
Sparse Core Ops, SparseCore 0:
  25.8 10.3 all-gather.16
  37.8 23.9 all-gather.18
  63.3 22.7 all-gather.20
  87.6 36.0 all-gather.12
  125.1 36.0 all-gather.14
  232.9 58.0 all-gather.22

commit v2 on v1

v2 whole, which is shorter than its diff:
```python
import functools

import jax
import jax.numpy as jnp
from jax import lax
from jax.experimental import pallas as pl
from jax.experimental.pallas import tpu as pltpu
from jax.sharding import PartitionSpec as P

HD = 64
IMAGES = 8
MOST = 256
LANES = 128
SLOTS = 16
EPSILON = 1e-06
BF = jnp.bfloat16
F32 = jnp.float32


def dot(a, b):
    return jnp.dot(a, b, preferred_element_type=F32)


def dot_t(a, b):
    return lax.dot_general(a, b, (((1,), (1,)), ((), ())), preferred_element_type=F32)


def t_dot(a, b):
    return lax.dot_general(a, b, (((0,), (0,)), ((), ())), preferred_element_type=F32)


def normalise(x):
    centred = x - jnp.mean(x, axis=-1, keepdims=True)
    scale = lax.rsqrt(jnp.mean(centred * centred, axis=-1, keepdims=True) + EPSILON)
    return centred * scale, scale


def norm_back(x, gain, gz):
    unit, scale = normalise(x)
    scaled = gz * gain
    mean_plain = jnp.mean(scaled, axis=-1, keepdims=True)
    mean_unit = jnp.mean(scaled * unit, axis=-1, keepdims=True)
    return scale * (scaled - mean_plain - unit * mean_unit), jnp.sum(gz * unit, axis=0, keepdims=True)


def gelu_parts(u):
    cdf = 0.5 * (1.0 + lax.erf(u * 0.7071067811865476))
    return u * cdf, cdf + u * (0.3989422804014327 * jnp.exp(-0.5 * u * u))


def pair_up(tile):
    row = lax.broadcasted_iota(jnp.int32, tile.shape, 0)
    zero = jnp.zeros_like(tile)
    return jnp.concatenate([jnp.where(row < HD, tile, zero), jnp.where(row >= HD, tile, zero)], axis=1)


def pair_down(both):
    n = both.shape[1] // 2
    row = lax.broadcasted_iota(jnp.int32, (both.shape[0], n), 0)
    return jnp.where(row < HD, both[:, :n], both[:, n:])


def bands(window):
    reach = MOST // LANES
    found, at = [], 0
    for i in range(window // LANES):
        first = max(0, i - reach) * LANES
        count = min(window, (i + reach + 1) * LANES) - first
        found.append((i * LANES, first, count, at))
        at += count
    return found, at


MESH = pl.DeviceIdType.MESH


def compute_kernel(
    x_own, c_own, ids, gains_own, w_own, mi_own, mo_own, router_own, ei, eo,
    act_out, pg_out, grad_attn, grad_mi, grad_mot, pack, small,
    xw, cw, gains, wy, wc, wqkv, wo, mi, mo, routert, act, edge_in, slots, geos, slot_in,
    z, x1, sent, x3, qt, kt, vt, kr, vr, ot, pt, tok, hidden, slope, gx, low, got, gt, gtok, gk_sum, gv_sum,
    bias, own, mixing, eslope, eout, gslot, send_sem, recv_sem,
):
    row_count, width = x_own.shape
    window = xw.shape[0]
    extra = window - row_count
    half = window // 2
    pairs = width // LANES
    total = ids.shape[1]
    dp = lax.axis_index("dp")
    section = lax.axis_index("section")
    tensor = lax.axis_index("tensor")
    core = (dp, 1 - section, tensor)
    beside = (dp, section, 1 - tensor)
    blocks, _ = bands(window)
    row_blocks = window // LANES

    def at(start, size, step=LANES):
        return pl.ds(pl.multiple_of(start, step), size)

    def rows(i, n=LANES):
        return pl.ds(pl.multiple_of(i * n, n), n)

    def loop(n, body):
        def step(i, carry):
            body(i)
            return carry

        lax.fori_loop(0, n, step, 0)

    sending = []

    def copy(key, source, dest, device):
        return pltpu.make_async_remote_copy(
            src_ref=source,
            dst_ref=dest,
            send_sem=send_sem.at[key],
            recv_sem=recv_sem.at[key],
            device_id=device,
            device_id_type=MESH,
        )

    def send(key, source, dest, device):
        copy(key, source, dest, device).start()
        sending.append((key, source, dest, device, None))

    def arrived(key, dest):
        copy(key, dest, dest, core).wait_recv()

    def on(which, body):
        pl.when(section == which)(body)

    barrier = pltpu.get_barrier_semaphore()
    for device in (core, beside):
        pl.semaphore_signal(barrier, inc=1, device_id=device, device_id_type=MESH)
    pl.semaphore_wait(barrier, 2)

    edge = x_own.at[at((1 - tensor) * (row_count - extra), extra)]
    send(0, edge, xw.at[at(tensor * row_count, extra)], beside)
    send(1, gains_own, gains.at[section], core)
    send(2, w_own, wc.at[0], core)

    @pl.when(section == 0)
    def _():
        copy(3, w_own, wy, beside).start()

    def local(dest, source):
        dest[...] = source[...]

    local(xw.at[at(tensor * extra, row_count)], x_own)
    local(cw.at[at(tensor * extra, row_count)], c_own)
    local(mi.at[tensor], mi_own)
    local(mo.at[tensor], mo_own)
    local(gains.at[section], gains_own)

    ids_row = ids[pl.ds(section, 1), :].astype(F32)
    image = lax.broadcasted_iota(jnp.int32, (SLOTS, total), 0).astype(F32)
    spread = jnp.broadcast_to(ids_row, (SLOTS, total))
    middle = jnp.sum((spread < image).astype(F32) + (spread <= image).astype(F32), axis=1, keepdims=True)
    first_half = (middle < total).astype(F32)
    mine = jnp.where(tensor == 0, first_half, 1.0 - first_half)
    window_ids = ids[pl.ds(section, 1), at(tensor * (total - window), window)].astype(F32)
    member = (jnp.broadcast_to(window_ids, (SLOTS, window)) == image[:, :window]).astype(F32)
    member_own = member * mine
    own_row = jnp.sum(member_own, axis=0, keepdims=True)
    own[...] = jnp.broadcast_to(own_row, (LANES, window)).T
    ids_col = jnp.broadcast_to(window_ids, (LANES, window)).T
    for q0, k0, count, kept in blocks:
        same = ids_col[k0 : k0 + count] == jnp.broadcast_to(window_ids[:, q0 : q0 + LANES], (count, LANES))
        bias[kept : kept + count, :] = jnp.where(same, 0.0, -1e30)

    def place(source, b, t):
        for c in range(4):
            dest, base = (wqkv, c * width) if c < 3 else (wo, 0)
            first = c * 3 * HD
            dest[b, at(base + t * LANES, 2 * HD)] = source[first : first + 2 * HD]
            dest[b, at(base + 2 * LANES + t * HD, HD, HD)] = source[first + 2 * HD : first + 3 * HD]

    arrived(0, xw.at[at((1 - tensor) * row_count, extra)])
    arrived(1, gains.at[1 - section])
    arrived(2, wc.at[0])
    place(w_own, section, tensor)
    place(wc.at[0], 1 - section, tensor)

    @pl.when(section == 0)
    def _():
        arrived(3, wy)
        copy(4, wy, wc.at[1], core).start()
        copy(5, mi_own, mi.at[tensor], beside).start()
        place(wy, 0, 1 - tensor)

    @pl.when(section == 1)
    def _():
        copy(5, mo_own, mo.at[tensor], beside).start()
        copy(3, w_own, wy, beside).start()
        arrived(4, wc.at[1])
        place(wc.at[1], 0, 1 - tensor)

    c_edge = c_own.at[at((1 - tensor) * (row_count - extra), extra)]
    send(7, c_edge, cw.at[at(tensor * row_count, extra)], beside)
    send(8, router_own, routert.at[tensor], beside)

    def attention(b, x_of, out_ref):
        def norm(i):
            unit, _ = normalise(x_of(rows(i)))
            z[2 * b, rows(i)] = (unit * gains[b, 0:1, :]).astype(BF)

        loop(row_blocks, norm)
        zz = z[2 * b]
        for c, dest in enumerate((qt, kt, vt)):
            tall = dot_t(wqkv[b, c * width : (c + 1) * width], zz)
            tall = (tall.astype(BF) * jnp.asarray(HD**-0.5 if c == 0 else 1.0, BF)).reshape(pairs, LANES, window)
            dest[b] = tall
        for c, dest in ((1, kr), (2, vr)):
            flat = dot_t(zz, wqkv[b, c * width : (c + 1) * width]).astype(BF)
            for j in range(pairs):
                dest[b, j] = flat[:, j * LANES : (j + 1) * LANES]

        def pair(j):
            for q0, k0, count, kept in blocks:
                scores = dot(kr[b, j, k0 : k0 + count, :], pair_up(qt[b, j, :, q0 : q0 + LANES]))
                veil = bias[kept : kept + count, :]
                scores = scores + jnp.concatenate([veil, veil], axis=1)
                powers = jnp.exp(scores - jnp.max(scores, axis=0, keepdims=True))
                probs = (powers * (1.0 / jnp.sum(powers, axis=0, keepdims=True))).astype(BF)
                pt[b, j, kept : kept + count, :] = probs
                ot[b, j, :, q0 : q0 + LANES] = pair_down(dot(vt[b, j, :, k0 : k0 + count], probs)).astype(BF)

        loop(pairs, pair)
        for j in range(pairs):
            tok[:, j * LANES : (j + 1) * LANES] = ot[b, j].T

        def out(i):
            out_ref[rows(i, half)] = x_of(rows(i, half)) + dot(tok[rows(i, half)], wo[b])

        loop(2, out)

    def attention_back(b, x_of):
        ga = low[...]
        got[...] = dot_t(wo[b], ga).astype(BF).reshape(pairs, LANES, window)
        for j in range(pairs):
            piece = dot(ot[b, j], ga).astype(BF)
            put_grad(b, 3, j, piece)

        def pair(j):
            gk_sum[...] = jnp.zeros_like(gk_sum)
            gv_sum[...] = jnp.zeros_like(gv_sum)
            for q0, k0, count, kept in blocks:
                go_pair = pair_up(got[j, :, q0 : q0 + LANES])
                q_pair = pair_up(qt[b, j, :, q0 : q0 + LANES])
                low_probs = pt[b, j, kept : kept + count, :]
                probs = low_probs.astype(F32)
                weighted = dot(vr[b, j, k0 : k0 + count, :], go_pair) * probs
                inner = jnp.sum(weighted, axis=0, keepdims=True)
                gs = (weighted - probs * inner).astype(BF)
                gq = pair_down(dot(kt[b, j, :, k0 : k0 + count], gs)) * HD**-0.5
                gt[pl.ds(pl.multiple_of(j * LANES, LANES), LANES), q0 : q0 + LANES] = gq.astype(BF)
                gk_sum[k0 : k0 + count] += dot_t(gs, q_pair)
                gv_sum[k0 : k0 + count] += dot_t(low_probs, go_pair)
            for c, total_of in ((1, gk_sum), (2, gv_sum)):
                gtok[c * pairs + j] = total_of[...].astype(BF)

        loop(pairs, pair)
        for j in range(pairs):
            gtok[j] = gt[j * LANES : (j + 1) * LANES].T
        for c in (1, 2):
            for j in range(pairs):
                first = (c * pairs + j) * LANES
                gt[first : first + LANES] = gtok[c * pairs + j].T
        zz = z[2 * b]
        for c in range(3):
            for j in range(pairs):
                first = (c * pairs + j) * LANES
                put_grad(b, c, j, dot(gt[first : first + LANES], zz).astype(BF))
        gain = gains[b, 0:1, :]
        gain_grad = jnp.zeros((1, width), F32)

        def back(i, gain_grad):
            wide = jnp.concatenate([gtok[c, rows(i, half)] for c in range(3 * pairs)], axis=1)
            step, part = norm_back(x_of(rows(i, half)), gain, dot(wide, wqkv[b]))
            gx[rows(i, half)] += step
            return gain_grad + part

        small[2 * b : 2 * b + 1, :] = lax.fori_loop(0, 2, back, gain_grad)

    def put_grad(b, c, j, piece):
        first = c * 3 * HD
        if j < 2:
            grad_attn[b, j, first : first + 2 * HD, :] = piece
        else:
            for t in range(2):
                grad_attn[b, t, first + 2 * HD : first + 3 * HD, :] = piece[t * HD : (t + 1) * HD]

    attention(0, lambda r: xw[r].astype(F32), x1)

    def norm_middle(source, which):
        def body(i):
            unit, _ = normalise(source[rows(i)])
            z[which, rows(i)] = (unit * gains[which // 2, 1:2, :]).astype(BF)

        loop(row_blocks, body)

    norm_middle(x1, 1)

    @pl.when(section == 0)
    def _():
        arrived(5, mi.at[1 - tensor])
        copy(6, mi.at[1 - tensor], mi.at[1 - tensor], core).start()
        arrived(6, mo.at[1 - tensor])

    @pl.when(section == 1)
    def _():
        arrived(5, mo.at[1 - tensor])
        copy(6, mo.at[1 - tensor], mo.at[1 - tensor], core).start()
        arrived(6, mi.at[1 - tensor])

    chunk = 256
    chunks = mi.shape[2] // chunk

    def hidden_chunk(i):
        part, first = i // chunks, pl.multiple_of(i % chunks * chunk, chunk)
        value, grad = gelu_parts(dot(z[1], mi[part, :, pl.ds(first, chunk)]))
        hidden[i] = value.astype(BF)
        slope[i] = grad

    loop(2 * chunks, hidden_chunk)

    def dense_out(i):
        h = jnp.concatenate([hidden[c, rows(i, half)] for c in range(2 * chunks)], axis=1)
        sent[rows(i, half)] = (x1[rows(i, half)] + dot(h, mo[...].reshape(-1, width))).astype(BF)

    loop(2, dense_out)

    @pl.when(section == 0)
    def _():
        arrived(4, wc.at[1])
        place(wc.at[1], 1, 1 - tensor)

    @pl.when(section == 1)
    def _():
        arrived(3, wy)
        copy(4, wy, wc.at[1], core).start()
        place(wy, 1, 1 - tensor)

    attention(1, lambda r: sent[r].astype(F32), x3)
    norm_middle(x3, 3)
    z3 = z[3]
    local(routert.at[tensor], router_own)
    arrived(8, routert.at[1 - tensor])
    powers = [jnp.exp(dot_t(routert[e], z3)[:1]) for e in range(2)]
    dispatch, combine = [], []
    for e in range(2):
        totals = jnp.sum(member * powers[e], axis=1, keepdims=True)
        dispatch.append(powers[e] / jnp.sum(member * totals, axis=0, keepdims=True))
        combine.append(powers[e] / (powers[0] + powers[1]))
        d_low = (member_own * dispatch[e].astype(BF).astype(F32)).astype(BF)
        c_low = (member * combine[e].astype(BF).astype(F32)).astype(BF)
        mixing[0, e * SLOTS : (e + 1) * SLOTS] = d_low
        mixing[1, e * SLOTS : (e + 1) * SLOTS] = c_low
        slots[e] = dot(d_low, z3).astype(BF)
    send(9, slots.at[1 - tensor], slot_in.at[0], beside)
    arrived(7, cw.at[at((1 - tensor) * row_count, extra)])

    def mask(i):
        wide = jnp.concatenate([own[rows(i)]] * pairs, axis=1)
        low[rows(i)] = jnp.where(wide > 0.0, cw[rows(i)].astype(F32), 0.0).astype(BF)

    loop(row_blocks, mask)
    gy = low[...]
    for e in range(2):
        geos[e] = dot(mixing[1, e * SLOTS : (e + 1) * SLOTS], gy).astype(BF)
    send(10, geos.at[1 - tensor], slot_in.at[1], beside)

    arrived(9, slot_in.at[0])
    pack[:SLOTS] = slots[tensor] + slot_in[0]
    value, grad = gelu_parts(dot(pack[:SLOTS], ei[...]))
    eslope[...] = grad
    eout[tensor] = dot(value.astype(BF), eo[...]).astype(BF)
    send(11, eout.at[tensor], eout.at[tensor], beside)
    arrived(10, slot_in.at[1])
    pack[SLOTS:] = geos[tensor] + slot_in[1]
    g_hidden = dot_t(pack[SLOTS:], eo[...])
    gslot[tensor] = dot_t((g_hidden * eslope[...]).astype(BF), ei[...]).astype(BF)
    send(12, gslot.at[tensor], gslot.at[tensor], beside)
    arrived(11, eout.at[1 - tensor])
    outputs = eout[...].reshape(2 * SLOTS, width)

    def finish(i):
        mixed = t_dot(mixing[1, :, rows(i)], outputs)
        act[rows(i)] = (x3[rows(i)] + mixed).astype(BF)

    loop(row_blocks, finish)
    send(13, act.at[at((1 - tensor) * row_count, extra)], edge_in.at[0], beside)

    per_token = [jnp.sum(dot_t(eout[e], gy) * member, axis=0, keepdims=True) for e in range(2)]
    inner = combine[0] * per_token[0] + combine[1] * per_token[1]
    arrived(12, gslot.at[1 - tensor])
    logit_grads = []
    for e in range(2):
        g_dispatch = jnp.sum(dot_t(gslot[e], z3) * member_own, axis=0, keepdims=True)
        weighted = dispatch[e] * g_dispatch
        sums = jnp.sum(member * weighted, axis=1, keepdims=True)
        from_dispatch = weighted - dispatch[e] * jnp.sum(member * sums, axis=0, keepdims=True)
        logit_grads.append(combine[e] * (per_token[e] - inner) + from_dispatch)
    which_row = lax.broadcasted_iota(jnp.int32, (SLOTS, width), 0)
    router_rows = jnp.where(
        which_row == 0,
        jnp.broadcast_to(routert[0].astype(F32)[:1], (SLOTS, width)),
        jnp.where(which_row == 1, jnp.broadcast_to(routert[1].astype(F32)[:1], (SLOTS, width)), 0.0),
    ).astype(BF)
    which = lax.broadcasted_iota(jnp.int32, (SLOTS, window), 0)
    logit_grad = jnp.where(which == 0, logit_grads[0], jnp.where(which == 1, logit_grads[1], 0.0)).astype(BF)
    small[4:6, :] = dot(logit_grad, z3)[:2]
    small[6:8, :] = jnp.zeros((2, width), F32)
    mixing[1, :SLOTS] = logit_grad
    slots_and_router = jnp.concatenate([gslot[0], gslot[1], router_rows], axis=0)

    def experts_back(i, gain_grad):
        at = pl.ds(pl.multiple_of(i * LANES, LANES), LANES)
        parts = jnp.concatenate([mixing[0, :, at], mixing[1, :SLOTS, at]], axis=0)
        step, part = norm_back(x3[rows(i)], gains[1, 1:2, :], t_dot(parts, slots_and_router))
        total_of = low[rows(i)].astype(F32) + step
        gx[rows(i)] = total_of
        low[rows(i)] = total_of.astype(BF)
        return gain_grad + part

    small[3:4, :] = lax.fori_loop(0, row_blocks, experts_back, jnp.zeros((1, width), F32))
    attention_back(1, lambda r: sent[r].astype(F32))

    low[...] = gx[...].astype(BF)
    gsent = low[...]
    gsent_t = gsent.T
    z2 = z[1]
    z2_t = z2.T

    def hidden_back(i):
        part, first = i // chunks, pl.multiple_of(i % chunks * chunk, chunk)
        lanes = pl.ds(pl.multiple_of(i * chunk, chunk), chunk)
        grad_mot[:, lanes] = dot(gsent_t, hidden[i]).astype(BF)
        g_hidden = dot_t(gsent, mo[part, pl.ds(first, chunk), :])
        g_pre = (g_hidden * slope[i]).astype(BF)
        hidden[i] = g_pre
        grad_mi[:, lanes] = dot(z2_t, g_pre).astype(BF)

    loop(2 * chunks, hidden_back)

    def dense_back(i, gain_grad):
        gz = jnp.zeros((half, width), F32)
        for part in range(2):
            g = jnp.concatenate([hidden[part * chunks + c, rows(i, half)] for c in range(chunks)], axis=1)
            gz = gz + dot_t(g, mi[part])
        step, part = norm_back(x1[rows(i, half)], gains[0, 1:2, :], gz)
        total_of = low[rows(i, half)].astype(F32) + step
        gx[rows(i, half)] = total_of
        low[rows(i, half)] = total_of.astype(BF)
        return gain_grad + part

    small[1:2, :] = lax.fori_loop(0, 2, dense_back, jnp.zeros((1, width), F32))
    attention_back(0, lambda r: xw[r].astype(F32))
    low[...] = gx[...].astype(BF)
    send(14, low.at[at((1 - tensor) * row_count, extra)], edge_in.at[1], beside)

    for n, (source, dest) in enumerate(((act, act_out), (low, pg_out))):
        dest[...] = source[at(tensor * extra, row_count)]
        arrived(13 + n, edge_in.at[n])
        near = at(row_count - extra - tensor * (row_count - 2 * extra), extra)
        wide = jnp.concatenate([own[near]] * pairs, axis=1)
        merged = jnp.where(wide > 0.0, source[near].astype(F32), edge_in[n].astype(F32)).astype(BF)
        dest[at((1 - tensor) * (row_count - extra), extra)] = merged

    for key, source, dest, device, _ in sending:
        copy(key, source, dest, device).wait_send()
    copy(3, w_own, wy, beside).wait_send()
    copy(4, wy, wc.at[1], core).wait_send()
    copy(5, mi_own, mi.at[tensor], beside).wait_send()
    copy(6, mi.at[1 - tensor], mi.at[1 - tensor], core).wait_send()


def compute(x_own, c_own, ids, gains, w_own, mi, mo, router, ei, eo):
    row_count, width = x_own.shape
    window = row_count + MOST // 2
    extra = window - row_count
    pairs = width // LANES
    ff = ei.shape[1]
    _, kept = bands(window)
    chunk_count = 2 * mi.shape[1] // 256
    vmem = pl.BlockSpec(memory_space=pltpu.VMEM)
    copies = 15
    return pl.pallas_call(
        compute_kernel,
        out_shape=(
            jax.ShapeDtypeStruct((row_count, width), BF),
            jax.ShapeDtypeStruct((row_count, width), BF),
            jax.ShapeDtypeStruct((2, 2, 2 * width, width), BF),
            jax.ShapeDtypeStruct((width, ff), BF),
            jax.ShapeDtypeStruct((width, ff), BF),
            jax.ShapeDtypeStruct((2 * SLOTS, width), BF),
            jax.ShapeDtypeStruct((8, width), F32),
        ),
        in_specs=[vmem] * 10,
        out_specs=[vmem] * 7,
        scratch_shapes=[
            pltpu.VMEM((window, width), BF),
            pltpu.VMEM((window, width), BF),
            pltpu.VMEM((2, 8, width), F32),
            pltpu.VMEM((2 * width, width), BF),
            pltpu.VMEM((2, 2 * width, width), BF),
            pltpu.VMEM((2, 3 * width, width), BF),
            pltpu.VMEM((2, width, width), BF),
            pltpu.VMEM((2, *mi.shape), BF),
            pltpu.VMEM((2, *mo.shape), BF),
            pltpu.VMEM((2, SLOTS, width), BF),
            pltpu.VMEM((window, width), BF),
            pltpu.VMEM((2, extra, width), BF),
            pltpu.VMEM((2, SLOTS, width), BF),
            pltpu.VMEM((2, SLOTS, width), BF),
            pltpu.VMEM((2, SLOTS, width), BF),
            pltpu.VMEM((4, window, width), BF),
            pltpu.VMEM((window, width), F32),
            pltpu.VMEM((window, width), BF),
            pltpu.VMEM((window, width), F32),
            pltpu.VMEM((2, pairs, LANES, window), BF),
            pltpu.VMEM((2, pairs, LANES, window), BF),
            pltpu.VMEM((2, pairs, LANES, window), BF),
            pltpu.VMEM((2, pairs, window, LANES), BF),
            pltpu.VMEM((2, pairs, window, LANES), BF),
            pltpu.VMEM((2, pairs, LANES, window), BF),
            pltpu.VMEM((2, pairs, kept, 2 * LANES), BF),
            pltpu.VMEM((window, width), BF),
            pltpu.VMEM((chunk_count, window, 256), BF),
            pltpu.VMEM((chunk_count, window, 256), F32),
            pltpu.VMEM((window, width), F32),
            pltpu.VMEM((window, width), BF),
            pltpu.VMEM((pairs, LANES, window), BF),
            pltpu.VMEM((3 * width, window), BF),
            pltpu.VMEM((3 * pairs, window, LANES), BF),
            pltpu.VMEM((window, LANES), F32),
            pltpu.VMEM((window, LANES), F32),
            pltpu.VMEM((kept, LANES), F32),
            pltpu.VMEM((window, LANES), F32),
            pltpu.VMEM((2, 2 * SLOTS, window), BF),
            pltpu.VMEM((SLOTS, ff), F32),
            pltpu.VMEM((2, SLOTS, width), BF),
            pltpu.VMEM((2, SLOTS, width), BF),
            pltpu.SemaphoreType.DMA((copies,)),
            pltpu.SemaphoreType.DMA((copies,)),
        ],
        compiler_params=pltpu.CompilerParams(
            vmem_limit_bytes=60 * 1024 * 1024, collective_id=0, has_side_effects=True
        ),
    )(x_own, c_own, ids, gains, w_own, mi, mo, router, ei, eo)


def per_device(
    patches, image_ids, cotangent, norm_gains, qkv_weight, out_weight, mlp_in, mlp_out, router, expert_in, expert_out
):
    width = patches.shape[2]
    tensor = lax.axis_index("tensor")
    heads = qkv_weight.shape[3] // HD
    w_own = jnp.concatenate([jnp.transpose(qkv_weight[0], (1, 2, 0)).reshape(-1, width), out_weight[0]], axis=0)
    gains = jnp.pad(norm_gains[0], ((0, 6), (0, 0)))
    router_own = jnp.pad(router.T, ((0, SLOTS - router.shape[1]), (0, 0)))
    activations, patch_grad, grad_attn, grad_mi, grad_mot, pack, small = compute(
        patches[0], cotangent[0], image_ids, gains, w_own, mlp_in, mlp_out, router_own, expert_in[0], expert_out[0]
    )
    activations, patch_grad = activations[None], patch_grad[None]

    rest = tuple(n for n in ("dp", "section", "tensor"))
    small = lax.psum(small, rest)
    gains_grad = lax.dynamic_slice_in_dim(small, 2 * lax.axis_index("section"), 2, 0)[None]
    router_grad = lax.dynamic_slice_in_dim(small, 4 + tensor, 1, 0).T
    grad_attn = lax.psum(grad_attn.astype(F32), rest)
    attn = lax.dynamic_index_in_dim(grad_attn, lax.axis_index("section"), 0, keepdims=False)
    attn = lax.dynamic_index_in_dim(attn, tensor, 0, keepdims=False)
    rows = 3 * heads * HD
    qkv_grad = jnp.transpose(attn[:rows].reshape(3, heads * HD, width), (2, 0, 1))[None]
    out_grad = attn[rows:][None]
    grad_mi = lax.psum(grad_mi.astype(F32), rest)
    grad_mot = lax.psum(grad_mot.astype(F32), rest)
    part = mlp_in.shape[1]
    mlp_in_grad = lax.dynamic_slice_in_dim(grad_mi, tensor * part, part, 1)
    mlp_out_grad = lax.dynamic_slice_in_dim(grad_mot, tensor * part, part, 1).T
    packs = lax.all_gather(pack, ("dp", "section"))
    slots = packs[:, :SLOTS].reshape(-1, width)
    geo = packs[:, SLOTS:].reshape(-1, width)
    value, slope = gelu_parts(dot(slots, expert_in[0]))
    g_pre = (dot_t(geo, expert_out[0]) * slope).astype(BF)
    expert_in_grad = t_dot(slots, g_pre)[None]
    expert_out_grad = t_dot(value.astype(BF), geo)[None]
    return (
        activations, patch_grad, gains_grad, qkv_grad, out_grad, mlp_in_grad, mlp_out_grad, router_grad,
        expert_in_grad, expert_out_grad,
    )


def solution(mesh):
    return jax.shard_map(
        per_device,
        mesh=mesh,
        in_specs=(
            P(("dp", "section"), "tensor", None),
            P("dp", None),
            P(("dp", "section"), "tensor", None),
            P("section", None, None),
            P("section", None, None, "tensor"),
            P("section", "tensor", None),
            P(None, "tensor"),
            P("tensor", None),
            P(None, "tensor"),
            P("tensor", None, None),
            P("tensor", None, None),
        ),
        out_specs=(
            P(("dp", "section"), "tensor", None),
            P(("dp", "section"), "tensor", None),
            P("section", None, None),
            P("section", None, None, "tensor"),
            P("section", "tensor", None),
            P(None, "tensor"),
            P("tensor", None),
            P(None, "tensor"),
            P("tensor", None, None),
            P("tensor", None, None),
        ),
        check_vma=False,
    )
```

time: 441 us -> 313 us (0.71)
  waiting for transfers between devices: 110 us -> 0 us
  Pallas kernels: 71.6 us -> 103 us
  blocking collectives: 207 us -> 188 us
  between operations: 14.4 us -> 0.68 us
  other arithmetic: 7.65 us -> 1.97 us
  starting transfers between devices: 4.52 us -> 0 us
    all_gather x6 -> x0, waiting for transfers between devices: 108 us -> none  [the longest x5 108 us: gathered(): a = lax.all_gather(a, axis)]
    pallas_call x1, Pallas kernels: 71.6 us -> 103 us  [compute(): pl.pallas_call(compute_kernel, out_shape=(jax.ShapeDtypeStruct((row_count...]
    all_gather x5 -> x1, blocking collectives: 33.9 us -> 19.6 us  [per_device(): packs = lax.all_gather(pack, ('dp', 'section'))]
    psum x1, blocking collectives: 173 us -> 168 us  [per_device(): small = lax.psum(small, rest)]
  transfers between devices with their start and end apart: 10 -> 0, of which waited for: 4 -> 0; matrix products, arithmetic and copies ran while one was open for 5% -> 0% of each run, Pallas kernels for 0% -> 0%
where the time goes in v2:
time: 313 us
  blocking collectives  188 us (60%)
  Pallas kernels  103 us (33%)
  local copies, waits for them, and re-layouts  13 us (4%)
  matrix products  6.42 us (2%)
    psum x1, blocking collectives, per_device(): small = lax.psum(small, rest)  168 us
    pallas_call x1, Pallas kernels, compute(): pl.pallas_call(compute_kernel, out_shape=(jax.ShapeDtypeStruct((row_count...  103 us
    all_gather x1, blocking collectives, per_device(): packs = lax.all_gather(pack, ('dp', 'section'))  19.6 us

profile of v2, /device:TPU:0, one launch (start us, length us, event | category | flops | bytes accessed | tf_op | source)
XLA Modules:
  0.0 312.6 jit_solution(2851974665254055769)
XLA Ops:
  0.6 2.0 pad_maximum_fusion.w_own
  2.6 1.3 pad.8.gains_own
  3.9 1.3 pad.9.router_own
  5.2 102.8 %shard_map.186 = (bf16[512,384]{1,0:T(8,128)(2,1)}, bf16[512,384]{1,0:T(8,128)(2,1)}, bf16[2,2,768,384]{3,2,1,0:T(8,128)(2,1)}, bf16[384,1536]{1,0:T(8,128)(2,1)...) custom-call(bf16[512,384]{1,0:T(8,128)(2,1)} %bitcast.52, bf16[512,384]{1,0:T(8,128)(2,1)} %bitcast.53, ...), custom_call_target="tpu_custom_call" | custom-call | tf_op jit(solution)/shard_map/pallas_call | solution.py:489
  108.0 168.1 %all-reduce.4 = (f32[8,384]{1,0:T(8,128)S(1)}, f32[2,2,768,384]{3,2,1,0:T(8,128)}, f32[384,1536]{1,0:T(8,128)S(1)}, f32[384,1536]{1,0:T(8,128)}) all-reduce(f32[8,384]{1,0:T(8,128)} %get-tuple-element.19, bf16[2,2,768,384]{3,2,1,0:T(8,128)(2,1)} %get-tuple-element.20, ...), channel_id=1, replica_groups=mesh['dp'=8,'section'=2,'tensor'=2] {'dp','section','tensor'}, use_global_device_ids=true, to_apply=%region_0.1 | all-reduce | flops 2362368 | bytes 14180352 | tf_op jit(solution)/shard_map/psum | solution.py:569
  276.1 2.5 dynamic-slice_bitcast_fusion
  278.6 1.4 copy.21
  279.9 0.0 copy-start.3
  279.9 0.0 copy-start
  279.9 2.2 constant_dynamic-slice_fusion
  282.2 1.7 dynamic-slice_bitcast_fusion.1
  283.9 0.6 dynamic-slice_bitcast_fusion.3
  284.4 0.6 dynamic-slice_bitcast_fusion.2
  285.0 0.0 copy-done.3
  285.0 19.6 %all-gather = bf16[512,384]{1,0:T(8,128)(2,1)S(1)} all-gather(bf16[32,384]{1,0:T(8,128)(2,1)S(1)} %copy-done.3), channel_id=2, replica_groups=mesh['dp'=8,'section'=2,'tensor'=2] {'dp','section'}, dimensions={0}, use_global_device_ids=true | all-gather | bytes 417792 | tf_op jit(solution)/shard_map/all_gather | solution.py:583
  304.7 0.0 copy-done
  304.7 0.6 fusion.9
  305.3 3.8 %convolution_bitcast_fusion.1 = f32[1,384,1536]{2,1,0:T(8,128)} fusion(bf16[256,384]{1,0:T(8,128)(2,1)S(1)} %bitcast.50, bf16[256,384]{1,0:T(8,128)(2,1)S(1)} %bitcast.47, f32[256,1536]{1,0:T(8,128)S(1)} %fusion.9, bf16[1,1536,384]{2,1,0:T(8,128)(2,1)} %param.21), kind=kOutput, calls=%fused_computation.1 | convolution fusion | flops 607911936 | bytes 5505024 | tf_op jit(solution)/shard_map/dot_general | solution.py:29
  309.1 0.0 copy-start.2
  309.1 0.0 copy-start.1
  309.1 2.0 convolution_bitcast_fusion
  311.1 0.0 copy-done.2
  311.1 0.7 copy.31
  311.9 0.0 copy-done.1
  311.9 0.7 copy.32
  (1 shorter events, 0.0 us)
Async XLA Ops:
  279.9 5.1 %copy-start.3 = (bf16[32,384]{1,0:T(8,128)(2,1)S(1)}, bf16[32,384]{1,0:T(8,128)(2,1)}, u32[]{:S(2)}) copy-start(bf16[32,384]{1,0:T(8,128)(2,1)} %get-tuple-element.23) | copy-start | bytes 73732
  279.9 24.7 %copy-start = (bf16[1,384,1536]{2,1,0:T(8,128)(2,1)S(1)}, bf16[1,384,1536]{2,1,0:T(8,128)(2,1)}, u32[]{:S(2)}) copy-start(bf16[1,384,1536]{2,1,0:T(8,128)(2,1)} %param.20) | copy-start | bytes 3538948
  309.1 2.0 copy-start.2
  309.1 2.8 copy-start.1

commit v3 on v2

--- a/solution.py
+++ b/solution.py
@@ -76,10 +76,14 @@
 
 def compute_kernel(
     x_own, c_own, ids, gains_own, w_own, mi_own, mo_own, router_own, ei, eo,
-    act_out, pg_out, grad_attn, grad_mi, grad_mot, pack, small,
-    xw, cw, gains, wy, wc, wqkv, wo, mi, mo, routert, act, edge_in, slots, geos, slot_in,
+    act_out, pg_out, attn_out, mlp_out, expert_in_out, expert_out_out, small_out,
+    xw, cw, gains, wy, wc, wqkv, wo, mi, mo, routert, act, edge_in, slots, geos, slot_in, pack,
     z, x1, sent, x3, qt, kt, vt, kr, vr, ot, pt, tok, hidden, slope, gx, low, got, gt, gtok, gk_sum, gv_sum,
-    bias, own, mixing, eslope, eout, gslot, send_sem, recv_sem,
+    bias, own, mixing, eslope, eout, gslot,
+    grad_attn, attn_parts, attn_across, attn_sum,
+    grad_mlp, mlp_core, mlp_beside, mlp_parts, mlp_across, mlp_sum,
+    small, small_in, small_parts, small_across, packs, small_pack, send_sem, recv_sem,
+    *, team, teams,
 ):
     row_count, width = x_own.shape
     window = xw.shape[0]
@@ -92,6 +96,21 @@
     tensor = lax.axis_index("tensor")
     core = (dp, 1 - section, tensor)
     beside = (dp, section, 1 - tensor)
+
+    spot = lax.rem(dp, team)
+    this_team = dp // team
+
+    def mate(k):
+        place, bit = spot, 1
+        while bit < team:
+            if k & bit:
+                place = jnp.where(lax.rem(spot // bit, 2) == 0, place + bit, place - bit)
+            bit *= 2
+        return (dp - spot + place, section, tensor), place
+
+    def partner(k):
+        return (lax.rem(dp + k * team, team * teams), section, tensor)
+
     blocks, _ = bands(window)
     row_blocks = window // LANES
 
@@ -108,7 +127,7 @@
 
         lax.fori_loop(0, n, step, 0)
 
-    sending = []
+    sent_off = {}
 
     def copy(key, source, dest, device):
         return pltpu.make_async_remote_copy(
@@ -120,20 +139,18 @@
             device_id_type=MESH,
         )
 
-    def send(key, source, dest, device):
+    def send(key, source, dest, device, like=None):
         copy(key, source, dest, device).start()
-        sending.append((key, source, dest, device, None))
+        sent_off[key] = source if like is None else like
 
     def arrived(key, dest):
         copy(key, dest, dest, core).wait_recv()
 
-    def on(which, body):
-        pl.when(section == which)(body)
-
     barrier = pltpu.get_barrier_semaphore()
-    for device in (core, beside):
+    neighbours = [core, beside] + [mate(k)[0] for k in range(1, team)] + [partner(k) for k in range(1, teams)]
+    for device in neighbours:
         pl.semaphore_signal(barrier, inc=1, device_id=device, device_id_type=MESH)
-    pl.semaphore_wait(barrier, 2)
+    pl.semaphore_wait(barrier, len(neighbours))
 
     edge = x_own.at[at((1 - tensor) * (row_count - extra), extra)]
     send(0, edge, xw.at[at(tensor * row_count, extra)], beside)
@@ -142,7 +159,7 @@
 
     @pl.when(section == 0)
     def _():
-        copy(3, w_own, wy, beside).start()
+        send(3, w_own, wy, beside)
 
     def local(dest, source):
         dest[...] = source[...]
@@ -185,20 +202,79 @@
     @pl.when(section == 0)
     def _():
         arrived(3, wy)
-        copy(4, wy, wc.at[1], core).start()
-        copy(5, mi_own, mi.at[tensor], beside).start()
+        send(4, wy, wc.at[1], core)
+        send(5, mi_own, mi.at[tensor], beside)
         place(wy, 0, 1 - tensor)
 
     @pl.when(section == 1)
     def _():
-        copy(5, mo_own, mo.at[tensor], beside).start()
-        copy(3, w_own, wy, beside).start()
+        send(5, mo_own, mo.at[tensor], beside)
+        send(3, w_own, wy, beside)
         arrived(4, wc.at[1])
         place(wc.at[1], 0, 1 - tensor)
 
     c_edge = c_own.at[at((1 - tensor) * (row_count - extra), extra)]
     send(7, c_edge, cw.at[at(tensor * row_count, extra)], beside)
     send(8, router_own, routert.at[tensor], beside)
+
+    class Sum:
+        def __init__(self, key, core_in, beside_in, parts, across, total):
+            self.key, self.core_in, self.beside_in = key, core_in, beside_in
+            self.parts, self.across, self.total = parts, across, total
+            self.size = parts.shape[1]
+            self.like = parts.at[0]
+
+        def part(self, place):
+            return at(place * self.size, self.size, 16)
+
+        def to_core(self, source):
+            send(self.key, source, self.core_in, core, self.core_in)
+
+        def to_beside(self, far):
+            arrived(self.key, self.core_in)
+            far[...] = (far[...].astype(F32) + self.core_in[1 - tensor].astype(F32)).astype(BF)
+            send(self.key + 1, far, self.beside_in, beside, self.beside_in)
+
+        def to_team(self, near):
+            arrived(self.key + 1, self.beside_in)
+            both = near[...].astype(F32) + self.core_in[tensor].astype(F32)
+            near[...] = (both + self.beside_in[...].astype(F32)).astype(BF)
+            for k in range(1, team):
+                device, place = mate(k)
+                send(self.key + 1 + k, near.at[self.part(place)], self.parts.at[k], device, self.like)
+
+        def add_parts(self, near):
+            whole = near[self.part(spot)].astype(F32)
+            for k in range(1, team):
+                arrived(self.key + 1 + k, self.parts.at[k])
+                whole = whole + self.parts[k].astype(F32)
+            piece = self.total.at[self.part(spot)]
+            piece[...] = whole.astype(BF)
+            first = self.key + 2 * team
+            for k in range(1, teams):
+                copy(first + team + k, piece, self.across.at[k], partner(k)).start()
+            for k in range(1, teams):
+                arrived(first + team + k, self.across.at[k])
+                copy(first + team + k, piece, self.across.at[k], partner(k)).wait_send()
+                whole = whole + self.across[k].astype(F32)
+            if teams > 1:
+                piece[...] = whole.astype(BF)
+            for k in range(1, team):
+                send(first + k, piece, piece, mate(k)[0], self.like)
+
+        def finish(self):
+            for k in range(1, team):
+                arrived(self.key + 2 * team + k, self.total.at[self.part(mate(k)[1])])
+
+        keys = 3 * team + teams
+
+    key = 15
+    attn = Sum(key, wc, wy, attn_parts, attn_across, attn_sum)
+    key += Sum.keys
+    mlp = Sum(key, mlp_core, mlp_beside, mlp_parts, mlp_across, mlp_sum.at[section])
+    key += Sum.keys
+    mlp_far, mlp_near = grad_mlp.at[section, 1 - tensor], grad_mlp.at[section, tensor]
+    mlp_key, pack_key, small_key = key, key + 1, key + 1 + team + teams
 
     def attention(b, x_of, out_ref):
         def norm(i):
@@ -207,10 +283,10 @@
 
         loop(row_blocks, norm)
         zz = z[2 * b]
-        for c, dest in enumerate((qt, kt, vt)):
+        for c, dest in enumerate((qt.at[b], kt.at[b], vt)):
             tall = dot_t(wqkv[b, c * width : (c + 1) * width], zz)
             tall = (tall.astype(BF) * jnp.asarray(HD**-0.5 if c == 0 else 1.0, BF)).reshape(pairs, LANES, window)
-            dest[b] = tall
+            dest[...] = tall
         for c, dest in ((1, kr), (2, vr)):
             flat = dot_t(zz, wqkv[b, c * width : (c + 1) * width]).astype(BF)
             for j in range(pairs):
@@ -224,7 +300,7 @@
                 powers = jnp.exp(scores - jnp.max(scores, axis=0, keepdims=True))
                 probs = (powers * (1.0 / jnp.sum(powers, axis=0, keepdims=True))).astype(BF)
                 pt[b, j, kept : kept + count, :] = probs
-                ot[b, j, :, q0 : q0 + LANES] = pair_down(dot(vt[b, j, :, k0 : k0 + count], probs)).astype(BF)
+                ot[b, j, :, q0 : q0 + LANES] = pair_down(dot(vt[j, :, k0 : k0 + count], probs)).astype(BF)
 
         loop(pairs, pair)
         for j in range(pairs):
@@ -235,7 +311,7 @@
 
         loop(2, out)
 
-    def attention_back(b, x_of):
+    def attention_back(b, x_of, beside_pairs, beside_rest):
         ga = low[...]
         got[...] = dot_t(wo[b], ga).astype(BF).reshape(pairs, LANES, window)
         for j in range(pairs):
@@ -243,6 +319,8 @@
             put_grad(b, 3, j, piece)
 
         def pair(j):
+            for at_pair, body in enumerate(beside_pairs):
+                pl.when(j == at_pair)(body)
             gk_sum[...] = jnp.zeros_like(gk_sum)
             gv_sum[...] = jnp.zeros_like(gv_sum)
             for q0, k0, count, kept in blocks:
@@ -272,6 +350,7 @@
             for j in range(pairs):
                 first = (c * pairs + j) * LANES
                 put_grad(b, c, j, dot(gt[first : first + LANES], zz).astype(BF))
+        beside_rest()
         gain = gains[b, 0:1, :]
         gain_grad = jnp.zeros((1, width), F32)
 
@@ -305,13 +384,13 @@
     @pl.when(section == 0)
     def _():
         arrived(5, mi.at[1 - tensor])
-        copy(6, mi.at[1 - tensor], mi.at[1 - tensor], core).start()
+        send(6, mi.at[1 - tensor], mi.at[1 - tensor], core, mi_own)
         arrived(6, mo.at[1 - tensor])
 
     @pl.when(section == 1)
     def _():
         arrived(5, mo.at[1 - tensor])
-        copy(6, mo.at[1 - tensor], mo.at[1 - tensor], core).start()
+        send(6, mo.at[1 - tensor], mo.at[1 - tensor], core, mo_own)
         arrived(6, mi.at[1 - tensor])
 
     chunk = 256
@@ -321,7 +400,7 @@
         part, first = i // chunks, pl.multiple_of(i % chunks * chunk, chunk)
         value, grad = gelu_parts(dot(z[1], mi[part, :, pl.ds(first, chunk)]))
         hidden[i] = value.astype(BF)
-        slope[i] = grad
+        slope[i] = grad.astype(BF)
 
     loop(2 * chunks, hidden_chunk)
 
@@ -339,7 +418,7 @@
     @pl.when(section == 1)
     def _():
         arrived(3, wy)
-        copy(4, wy, wc.at[1], core).start()
+        send(4, wy, wc.at[1], core)
         place(wy, 1, 1 - tensor)
 
     attention(1, lambda r: sent[r].astype(F32), x3)
@@ -358,6 +437,9 @@
         mixing[0, e * SLOTS : (e + 1) * SLOTS] = d_low
         mixing[1, e * SLOTS : (e + 1) * SLOTS] = c_low
         slots[e] = dot(d_low, z3).astype(BF)
+    copy(4, wy, wc.at[1], core).wait_send()
+    sent_off.pop(4)
+
     send(9, slots.at[1 - tensor], slot_in.at[0], beside)
     arrived(7, cw.at[at((1 - tensor) * row_count, extra)])
 
@@ -372,14 +454,14 @@
     send(10, geos.at[1 - tensor], slot_in.at[1], beside)
 
     arrived(9, slot_in.at[0])
-    pack[:SLOTS] = slots[tensor] + slot_in[0]
-    value, grad = gelu_parts(dot(pack[:SLOTS], ei[...]))
+    pack[0] = slots[tensor] + slot_in[0]
+    value, grad = gelu_parts(dot(pack[0], ei[...]))
     eslope[...] = grad
     eout[tensor] = dot(value.astype(BF), eo[...]).astype(BF)
     send(11, eout.at[tensor], eout.at[tensor], beside)
     arrived(10, slot_in.at[1])
-    pack[SLOTS:] = geos[tensor] + slot_in[1]
-    g_hidden = dot_t(pack[SLOTS:], eo[...])
+    pack[1] = geos[tensor] + slot_in[1]
+    g_hidden = dot_t(pack[1], eo[...])
     gslot[tensor] = dot_t((g_hidden * eslope[...]).astype(BF), ei[...]).astype(BF)
     send(12, gslot.at[tensor], gslot.at[tensor], beside)
     arrived(11, eout.at[1 - tensor])
@@ -391,6 +473,28 @@
 
     loop(row_blocks, finish)
     send(13, act.at[at((1 - tensor) * row_count, extra)], edge_in.at[0], beside)
+
+    def nothing():
+        pass
+
+    all_packs, team_like = packs.at[0], packs.at[0, 0]
+
+    def share_slots():
+        halves = [pack[n].astype(F32)[:IMAGES] for n in range(2)]
+        small_pack[...] = jnp.concatenate(halves, axis=0).astype(BF)
+        for k in range(1, team):
+            send(pack_key + k, small_pack, packs.at[0, this_team, spot], mate(k)[0], small_pack)
+
+    def gather_slots():
+        for k in range(1, team):
+            arrived(pack_key + k, packs.at[0, this_team, mate(k)[1]])
+        packs[0, this_team, spot] = small_pack[...]
+        for k in range(1, teams):
+            team_packs = packs.at[0, this_team]
+            send(pack_key + team + k, team_packs, team_packs, partner(k), team_like)
+        for k in range(1, teams):
+            arrived(pack_key + team + k, packs.at[0, lax.rem(this_team + k, teams)])
+        send(pack_key, packs.at[0], packs.at[1], core, all_packs)
 
     per_token = [jnp.sum(dot_t(eout[e], gy) * member, axis=0, keepdims=True) for e in range(2)]
     inner = combine[0] * per_token[0] + combine[1] * per_token[1]
@@ -425,7 +529,14 @@
         return gain_grad + part
 
     small[3:4, :] = lax.fori_loop(0, row_blocks, experts_back, jnp.zeros((1, width), F32))
-    attention_back(1, lambda r: sent[r].astype(F32))
+
+    def share_second():
+        @pl.when(section == 0)
+        def _():
+            attn.to_core(grad_attn.at[1])
+
+    share_pack = [share_slots, gather_slots, nothing]
+    attention_back(1, lambda r: sent[r].astype(F32), share_pack, share_second)
 
     low[...] = gx[...].astype(BF)
     gsent = low[...]
@@ -435,14 +546,24 @@
 
     def hidden_back(i):
         part, first = i // chunks, pl.multiple_of(i % chunks * chunk, chunk)
-        lanes = pl.ds(pl.multiple_of(i * chunk, chunk), chunk)
-        grad_mot[:, lanes] = dot(gsent_t, hidden[i]).astype(BF)
+        lanes = pl.ds(first, chunk)
+        grad_mlp[1, part, :, lanes] = dot(gsent_t, hidden[i]).astype(BF)
         g_hidden = dot_t(gsent, mo[part, pl.ds(first, chunk), :])
-        g_pre = (g_hidden * slope[i]).astype(BF)
+        g_pre = (g_hidden * slope[i].astype(F32)).astype(BF)
         hidden[i] = g_pre
-        grad_mi[:, lanes] = dot(z2_t, g_pre).astype(BF)
+        grad_mlp[0, part, :, lanes] = dot(z2_t, g_pre).astype(BF)
+
+    @pl.when(section == 1)
+    def _():
+        attn.to_beside(grad_attn.at[1, 1 - tensor])
 
     loop(2 * chunks, hidden_back)
+    mlp.to_core(grad_mlp.at[1 - section])
+
+    @pl.when(section == 1)
+    def _():
+        attn.to_team(grad_attn.at[1, tensor])
+
 
     def dense_back(i, gain_grad):
         gz = jnp.zeros((half, width), F32)
@@ -456,9 +577,61 @@
         return gain_grad + part
 
     small[1:2, :] = lax.fori_loop(0, 2, dense_back, jnp.zeros((1, width), F32))
-    attention_back(0, lambda r: xw[r].astype(F32))
+
+    def share_dense():
+        mlp.to_beside(mlp_far)
+
+    def reduce_second():
+        @pl.when(section == 1)
+        def _():
+            attn.add_parts(grad_attn.at[1, tensor])
+
+    def reduce_dense():
+        mlp.to_team(mlp_near)
+
+    def share_first():
+        @pl.when(section == 1)
+        def _():
+            attn.to_core(grad_attn.at[0])
+
+    attention_back(0, lambda r: xw[r].astype(F32), [share_dense, reduce_second, reduce_dense], share_first)
     low[...] = gx[...].astype(BF)
     send(14, low.at[at((1 - tensor) * row_count, extra)], edge_in.at[1], beside)
+    send(small_key, small, small_in.at[0], core)
+
+    @pl.when(section == 0)
+    def _():
+        attn.to_beside(grad_attn.at[0, 1 - tensor])
+
+    arrived(small_key, small_in.at[0])
+    small_in[1] = small[...] + small_in[0]
+    send(small_key + 1, small_in.at[1], small_in.at[2], beside)
+    mlp.add_parts(mlp_near)
+
+    arrived(pack_key, packs.at[1])
+    split_packs = packs[...].astype(F32).reshape(-1, 2, IMAGES, width)
+    every_slot, every_grad = (split_packs[:, n].reshape(-1, width).astype(BF) for n in range(2))
+    every_slot_t = every_slot.T
+
+    few = chunk if teams == 1 else LANES
+
+    def expert_grads(i):
+        lanes = pl.ds(pl.multiple_of(i * few, few), few)
+        value, grad = gelu_parts(dot(every_slot, ei[:, lanes]))
+        g_pre = (dot_t(every_grad, eo[lanes, :]) * grad).astype(BF)
+        expert_in_out[:, lanes] = dot(every_slot_t, g_pre).astype(BF)
+        expert_out_out[lanes, :] = dot(value.astype(BF).T, every_grad).astype(BF)
+
+    loop(2 * chunks * chunk // few, expert_grads)
+
+    arrived(small_key + 1, small_in.at[2])
+    small_parts[0] = small_in[1] + small_in[2]
+    for k in range(1, team):
+        send(small_key + 1 + k, small_parts.at[0], small_parts.at[k], mate(k)[0])
+
+    @pl.when(section == 0)
+    def _():
+        attn.to_team(grad_attn.at[0, tensor])
 
     for n, (source, dest) in enumerate(((act, act_out), (low, pg_out))):
         dest[...] = source[at(tensor * extra, row_count)]
@@ -468,12 +641,33 @@
         merged = jnp.where(wide > 0.0, source[near].astype(F32), edge_in[n].astype(F32)).astype(BF)
         dest[at((1 - tensor) * (row_count - extra), extra)] = merged
 
-    for key, source, dest, device, _ in sending:
-        copy(key, source, dest, device).wait_send()
-    copy(3, w_own, wy, beside).wait_send()
-    copy(4, wy, wc.at[1], core).wait_send()
-    copy(5, mi_own, mi.at[tensor], beside).wait_send()
-    copy(6, mi.at[1 - tensor], mi.at[1 - tensor], core).wait_send()
+    @pl.when(section == 1)
+    def _():
+        attn.finish()
+
+    mlp.finish()
+    send(mlp_key, mlp_sum.at[section], mlp_sum.at[section], core, mlp_sum.at[0])
+
+    for k in range(1, team):
+        arrived(small_key + 1 + k, small_parts.at[k])
+    small_across[0] = sum([small_parts[k] for k in range(1, team)], start=small_parts[0])
+    for k in range(1, teams):
+        send(small_key + 1 + team + k, small_across.at[0], small_across.at[k], partner(k))
+    for k in range(1, teams):
+        arrived(small_key + 1 + team + k, small_across.at[k])
+    small_out[...] = sum([small_across[k] for k in range(1, teams)], start=small_across[0])
+
+    @pl.when(section == 0)
+    def _():
+        attn.add_parts(grad_attn.at[0, tensor])
+        attn.finish()
+
+    arrived(mlp_key, mlp_sum.at[1 - section])
+    attn_out[...] = attn_sum[...]
+    mlp_out[...] = mlp_sum[...]
+
+    for key, like in sent_off.items():
+        copy(key, like, like, core).wait_send()
 
 
 def compute(x_own, c_own, ids, gains, w_own, mi, mo, router, ei, eo):
@@ -485,16 +679,19 @@
     _, kept = bands(window)
     chunk_count = 2 * mi.shape[1] // 256
     vmem = pl.BlockSpec(memory_space=pltpu.VMEM)
-    copies = 15
+    ranks = lax.axis_size("dp")
+    team = min(8, ranks & -ranks)
+    teams = ranks // team
+    copies = 15 + 2 * (3 * team + teams) + 1 + team + teams + 1 + team + teams
     return pl.pallas_call(
-        compute_kernel,
+        functools.partial(compute_kernel, team=team, teams=teams),
         out_shape=(
             jax.ShapeDtypeStruct((row_count, width), BF),
             jax.ShapeDtypeStruct((row_count, width), BF),
-            jax.ShapeDtypeStruct((2, 2, 2 * width, width), BF),
+            jax.ShapeDtypeStruct((2 * width, width), BF),
+            jax.ShapeDtypeStruct((2, width, ff // 2), BF),
             jax.ShapeDtypeStruct((width, ff), BF),
-            jax.ShapeDtypeStruct((width, ff), BF),
-            jax.ShapeDtypeStruct((2 * SLOTS, width), BF),
+            jax.ShapeDtypeStruct((ff, width), BF),
             jax.ShapeDtypeStruct((8, width), F32),
         ),
         in_specs=[vmem] * 10,
@@ -515,20 +712,21 @@
             pltpu.VMEM((2, SLOTS, width), BF),
             pltpu.VMEM((2, SLOTS, width), BF),
             pltpu.VMEM((2, SLOTS, width), BF),
+            pltpu.VMEM((2, SLOTS, width), BF),
             pltpu.VMEM((4, window, width), BF),
             pltpu.VMEM((window, width), F32),
             pltpu.VMEM((window, width), BF),
             pltpu.VMEM((window, width), F32),
             pltpu.VMEM((2, pairs, LANES, window), BF),
             pltpu.VMEM((2, pairs, LANES, window), BF),
-            pltpu.VMEM((2, pairs, LANES, window), BF),
+            pltpu.VMEM((pairs, LANES, window), BF),
             pltpu.VMEM((2, pairs, window, LANES), BF),
             pltpu.VMEM((2, pairs, window, LANES), BF),
             pltpu.VMEM((2, pairs, LANES, window), BF),
             pltpu.VMEM((2, pairs, kept, 2 * LANES), BF),
             pltpu.VMEM((window, width), BF),
             pltpu.VMEM((chunk_count, window, 256), BF),
-            pltpu.VMEM((chunk_count, window, 256), F32),
+            pltpu.VMEM((chunk_count, window, 256), BF),
             pltpu.VMEM((window, width), F32),
             pltpu.VMEM((window, width), BF),
             pltpu.VMEM((pairs, LANES, window), BF),
@@ -542,6 +740,22 @@
             pltpu.VMEM((SLOTS, ff), F32),
             pltpu.VMEM((2, SLOTS, width), BF),
             pltpu.VMEM((2, SLOTS, width), BF),
+            pltpu.VMEM((2, 2, 2 * width, width), BF),
+            pltpu.VMEM((team, 2 * width // team, width), BF),
+            pltpu.VMEM((teams, 2 * width // team, width), BF),
+            pltpu.VMEM((2 * width, width), BF),
+            pltpu.VMEM((2, 2, width, ff // 2), BF),
+            pltpu.VMEM((2, width, ff // 2), BF),
+            pltpu.VMEM((width, ff // 2), BF),
+            pltpu.VMEM((team, width // team, ff // 2), BF),
+            pltpu.VMEM((teams, width // team, ff // 2), BF),
+            pltpu.VMEM((2, width, ff // 2), BF),
+            pltpu.VMEM((8, width), F32),
+            pltpu.VMEM((3, 8, width), F32),
+            pltpu.VMEM((team, 8, width), F32),
+            pltpu.VMEM((teams, 8, width), F32),
+            pltpu.VMEM((2, teams, team, 2 * IMAGES, width), BF),
+            pltpu.VMEM((2 * IMAGES, width), BF),
             pltpu.SemaphoreType.DMA((copies,)),
             pltpu.SemaphoreType.DMA((copies,)),
         ],
@@ -560,36 +774,24 @@
     w_own = jnp.concatenate([jnp.transpose(qkv_weight[0], (1, 2, 0)).reshape(-1, width), out_weight[0]], axis=0)
     gains = jnp.pad(norm_gains[0], ((0, 6), (0, 0)))
     router_own = jnp.pad(router.T, ((0, SLOTS - router.shape[1]), (0, 0)))
-    activations, patch_grad, grad_attn, grad_mi, grad_mot, pack, small = compute(
+    activations, patch_grad, attn, mlp, expert_in_grad, expert_out_grad, small = compute(
         patches[0], cotangent[0], image_ids, gains, w_own, mlp_in, mlp_out, router_own, expert_in[0], expert_out[0]
     )
-    activations, patch_grad = activations[None], patch_grad[None]
-
-    rest = tuple(n for n in ("dp", "section", "tensor"))
-    small = lax.psum(small, rest)
-    gains_grad = lax.dynamic_slice_in_dim(small, 2 * lax.axis_index("section"), 2, 0)[None]
+    rows = 3 * heads * HD
+    qkv_grad = jnp.transpose(attn[:rows].astype(F32).reshape(3, heads * HD, width), (2, 0, 1))
+    gains_grad = lax.dynamic_slice_in_dim(small, 2 * lax.axis_index("section"), 2, 0)
     router_grad = lax.dynamic_slice_in_dim(small, 4 + tensor, 1, 0).T
-    grad_attn = lax.psum(grad_attn.astype(F32), rest)
-    attn = lax.dynamic_index_in_dim(grad_attn, lax.axis_index("section"), 0, keepdims=False)
-    attn = lax.dynamic_index_in_dim(attn, tensor, 0, keepdims=False)
-    rows = 3 * heads * HD
-    qkv_grad = jnp.transpose(attn[:rows].reshape(3, heads * HD, width), (2, 0, 1))[None]
-    out_grad = attn[rows:][None]
-    grad_mi = lax.psum(grad_mi.astype(F32), rest)
-    grad_mot = lax.psum(grad_mot.astype(F32), rest)
-    part = mlp_in.shape[1]
-    mlp_in_grad = lax.dynamic_slice_in_dim(grad_mi, tensor * part, part, 1)
-    mlp_out_grad = lax.dynamic_slice_in_dim(grad_mot, tensor * part, part, 1).T
-    packs = lax.all_gather(pack, ("dp", "section"))
-    slots = packs[:, :SLOTS].reshape(-1, width)
-    geo = packs[:, SLOTS:].reshape(-1, width)
-    value, slope = gelu_parts(dot(slots, expert_in[0]))
-    g_pre = (dot_t(geo, expert_out[0]) * slope).astype(BF)
-    expert_in_grad = t_dot(slots, g_pre)[None]
-    expert_out_grad = t_dot(value.astype(BF), geo)[None]
     return (
-        activations, patch_grad, gains_grad, qkv_grad, out_grad, mlp_in_grad, mlp_out_grad, router_grad,
-        expert_in_grad, expert_out_grad,
+        activations[None],
+        patch_grad[None],
+        gains_grad[None],
+        qkv_grad[None],
+        attn[rows:].astype(F32)[None],
+        mlp[0].astype(F32),
+        mlp[1].astype(F32).T,
+        router_grad,
+        expert_in_grad.astype(F32)[None],
+        expert_out_grad.astype(F32)[None],
     )
 
 

time: 313 us -> 173 us (0.55)
  blocking collectives: 188 us -> 0 us
  Pallas kernels: 103 us -> 155 us
  other arithmetic: 1.97 us -> 9.02 us
  matrix products: 6.42 us -> 0 us
  local copies, waits for them, and re-layouts: 13 us -> 8.51 us
    psum x1 -> x0, blocking collectives: 168 us -> none  [per_device(): small = lax.psum(small, rest)]
    pallas_call x1, Pallas kernels: 103 us -> 155 us  [compute(): pl.pallas_call(functools.partial(compute_kernel, team=team, teams=teams),...]
    all_gather x1 -> x0, blocking collectives: 19.6 us -> none  [per_device(): packs = lax.all_gather(pack, ('dp', 'section'))]
    dot_general x3 -> x0, matrix products: 6.42 us -> none  [the longest x2 5.86 us: t_dot(): lax.dot_general(a, b, (((0,), (0,)), ((), ())), preferred_element_type=F32)]
    broadcast_in_dim x0 -> x4, other arithmetic: none -> 5.87 us  [the longest x1 1.69 us: per_device(): expert_in_grad.astype(F32)[None]]
where the time goes in v3:
time: 173 us
  Pallas kernels  155 us (90%)
  other arithmetic  9.02 us (5%)
  local copies, waits for them, and re-layouts  8.51 us (5%)
    pallas_call x1, Pallas kernels, compute(): pl.pallas_call(functools.partial(compute_kernel, team=team, teams=teams),...  155 us

profile of v3, /device:TPU:0, one launch (start us, length us, event | category | flops | bytes accessed | tf_op | source)
XLA Modules:
  0.0 172.7 jit_solution(17262408645208189092)
XLA Ops:
  0.6 0.0 copy-start.5
  0.7 1.3 pad.8.gains_own
  1.9 2.0 %pad_maximum_fusion.w_own = bf16[768,384]{1,0:T(8,128)(2,1)} fusion(bf16[192,384]{1,0:T(8,128)(2,1)} %bitcast.49, bf16[576,384]{1,0:T(8,128)(2,1)} %bitcast.44), kind=kLoop, calls=%fused_computation.4 | loop fusion | flops 1179648 | bytes 1179648 | tf_op jit(solution)/shard_map/concatenate | solution.py:774
  3.9 0.0 copy-done.5
  3.9 0.6 pad.9.router_own
  4.5 154.5 %shard_map.186 = (bf16[512,384]{1,0:T(8,128)(2,1)}, bf16[512,384]{1,0:T(8,128)(2,1)}, bf16[768,384]{1,0:T(8,128)(2,1)}, bf16[2,384,768]{2,1,0:T(8,128)(2,1)}, bf...) custom-call(bf16[512,384]{1,0:T(8,128)(2,1)} %bitcast.45, bf16[512,384]{1,0:T(8,128)(2,1)} %bitcast.46, ...), custom_call_target="tpu_custom_call" | custom-call | tf_op jit(solution)/shard_map/pallas_call | solution.py:686
  159.1 1.3 dynamic-slice_bitcast_fusion
  160.3 0.0 copy-start.2
  160.3 1.2 slice.12
  161.5 1.0 convert_bitcast_fusion.1
  162.5 1.6 bitcast_convert_fusion.3
  164.1 0.0 copy-done.2
  164.1 1.2 convert_bitcast_fusion
  165.3 0.0 copy-start.1
  165.3 1.4 copy.21
  166.7 1.3 dynamic-slice_bitcast_fusion.1
  168.0 0.0 copy-done.1
  168.0 0.0 copy-start
  168.0 1.7 bitcast_convert_fusion.1
  169.7 0.0 copy-done
  169.7 0.0 copy-start.4
  169.7 0.0 copy-start.3
  169.7 1.6 bitcast_convert_fusion
  171.2 0.0 copy-done.4
  171.2 0.7 copy.24
  172.0 0.0 copy-done.3
  172.0 0.7 copy.25
Async XLA Ops:
  0.6 3.3 %copy-start.5 = (bf16[384,1]{0,1:T(2,128)(2,1)S(1)}, bf16[384,1]{0,1:T(2,128)(2,1)}, u32[]{:S(2)}) copy-start(bf16[384,1]{0,1:T(2,128)(2,1)} %param.19) | copy-start | bytes 2308
  160.3 3.8 %copy-start.2 = (bf16[2,384,768]{2,1,0:T(8,128)(2,1)S(1)}, bf16[2,384,768]{2,1,0:T(8,128)(2,1)}, u32[]{:S(2)}) copy-start(bf16[2,384,768]{2,1,0:T(8,128)(2,1)} %get-tuple-element.21) | copy-start | bytes 3538948
  165.3 2.7 %copy-start.1 = (bf16[384,1536]{1,0:T(8,128)(2,1)S(1)}, bf16[384,1536]{1,0:T(8,128)(2,1)}, u32[]{:S(2)}) copy-start(bf16[384,1536]{1,0:T(8,128)(2,1)} %get-tuple-element.22) | copy-start | bytes 3538948
  168.0 1.7 copy-start
  169.7 1.6 copy-start.4
  169.7 2.3 %copy-start.3 = (bf16[512,384]{1,0:T(8,128)(2,1)S(1)}, bf16[512,384]{1,0:T(8,128)(2,1)}, u32[]{:S(2)}) copy-start(bf16[512,384]{1,0:T(8,128)(2,1)} %get-tuple-element.18) | copy-start | bytes 1179652

commit v4 on v3

--- a/solution.py
+++ b/solution.py
@@ -75,15 +75,13 @@
 
 
 def compute_kernel(
-    x_own, c_own, ids, gains_own, w_own, mi_own, mo_own, router_own, ei, eo,
-    act_out, pg_out, attn_out, mlp_out, expert_in_out, expert_out_out, small_out,
-    xw, cw, gains, wy, wc, wqkv, wo, mi, mo, routert, act, edge_in, slots, geos, slot_in, pack,
+    x_own, c_own, ids, gains_own, qkv_own, out_own, mi_own, mo_own, router_own, ei, eo,
+    act_out, pg_out, qkv_out, attn_out, mi_out, mot_out, expert_in_out, expert_out_out, small_out,
+    xw, cw, gains, wy, wc, w_own, wqkv, wo, mi, mo, routert, act, edge_in, slots, geos, slot_in, pack,
     z, x1, sent, x3, qt, kt, vt, kr, vr, ot, pt, tok, hidden, slope, gx, low, got, gt, gtok, gk_sum, gv_sum,
-    bias, own, mixing, eslope, eout, gslot,
-    grad_attn, attn_parts, attn_across, attn_sum,
-    grad_mlp, mlp_core, mlp_beside, mlp_parts, mlp_across, mlp_sum,
+    bias, own, mixing, eslope, eout, gslot, grad_attn, attn_sum, grad_mlp, mlp_core, mlp_sum,
     small, small_in, small_parts, small_across, packs, small_pack, send_sem, recv_sem,
-    *, team, teams,
+    *boxes, team, teams, mlp_orders, attn_orders,
 ):
     row_count, width = x_own.shape
     window = xw.shape[0]
@@ -146,6 +144,9 @@
     def arrived(key, dest):
         copy(key, dest, dest, core).wait_recv()
 
+    def only(which):
+        return pl.when(section == which)
+
     barrier = pltpu.get_barrier_semaphore()
     neighbours = [core, beside] + [mate(k)[0] for k in range(1, team)] + [partner(k) for k in range(1, teams)]
     for device in neighbours:
@@ -154,10 +155,13 @@
 
     edge = x_own.at[at((1 - tensor) * (row_count - extra), extra)]
     send(0, edge, xw.at[at(tensor * row_count, extra)], beside)
-    send(1, gains_own, gains.at[section], core)
+    gains[section, :2] = gains_own[...]
+    send(1, gains.at[section], gains.at[section], core)
+    w_own[: qkv_own.shape[0]] = qkv_own[...]
+    w_own[qkv_own.shape[0] :] = out_own[...]
     send(2, w_own, wc.at[0], core)
 
-    @pl.when(section == 0)
+    @only(0)
     def _():
         send(3, w_own, wy, beside)
 
@@ -168,7 +172,9 @@
     local(cw.at[at(tensor * extra, row_count)], c_own)
     local(mi.at[tensor], mi_own)
     local(mo.at[tensor], mo_own)
-    local(gains.at[section], gains_own)
+    first_row = lax.broadcasted_iota(jnp.int32, (SLOTS, width), 0) == 0
+    router_rows = jnp.broadcast_to(router_own[...].astype(F32), (SLOTS, width))
+    routert[tensor] = jnp.where(first_row, router_rows, 0.0).astype(BF)
 
     ids_row = ids[pl.ds(section, 1), :].astype(F32)
     image = lax.broadcasted_iota(jnp.int32, (SLOTS, total), 0).astype(F32)
@@ -199,14 +205,14 @@
     place(w_own, section, tensor)
     place(wc.at[0], 1 - section, tensor)
 
-    @pl.when(section == 0)
+    @only(0)
     def _():
         arrived(3, wy)
         send(4, wy, wc.at[1], core)
         send(5, mi_own, mi.at[tensor], beside)
         place(wy, 0, 1 - tensor)
 
-    @pl.when(section == 1)
+    @only(1)
     def _():
         send(5, mo_own, mo.at[tensor], beside)
         send(3, w_own, wy, beside)
@@ -215,66 +221,121 @@
 
     c_edge = c_own.at[at((1 - tensor) * (row_count - extra), extra)]
     send(7, c_edge, cw.at[at(tensor * row_count, extra)], beside)
-    send(8, router_own, routert.at[tensor], beside)
-
-    class Sum:
-        def __init__(self, key, core_in, beside_in, parts, across, total):
-            self.key, self.core_in, self.beside_in = key, core_in, beside_in
-            self.parts, self.across, self.total = parts, across, total
-            self.size = parts.shape[1]
-            self.like = parts.at[0]
-
-        def part(self, place):
-            return at(place * self.size, self.size, 16)
+    send(8, routert.at[tensor], routert.at[tensor], beside)
+
+    class Cube:
+        def __init__(self, key, pick, core_in, total, order, boxes):
+            self.key, self.pick, self.core_in, self.total, self.order = key, pick, core_in, total, order
+            self.boxes, self.across = boxes[:-1], boxes[-1]
+            start, size, self.plan = 0, total.shape[0], []
+            for dim in order:
+                if dim == "tensor":
+                    self.plan.append((dim, start, size, start))
+                else:
+                    size //= 2
+                    bit = lax.rem(spot // dim, 2)
+                    self.plan.append((dim, start + bit * size, size, start + (1 - bit) * size))
+                    start = start + bit * size
+            self.back = [(i, *step) for i, step in enumerate(self.plan) if step[0] != "tensor"][::-1]
+            self.like = {size: total.at[:size] for _, _, _, size, _ in self.back}
+            self.along = order.index("tensor")
 
         def to_core(self, source):
             send(self.key, source, self.core_in, core, self.core_in)
 
-        def to_beside(self, far):
-            arrived(self.key, self.core_in)
-            far[...] = (far[...].astype(F32) + self.core_in[1 - tensor].astype(F32)).astype(BF)
-            send(self.key + 1, far, self.beside_in, beside, self.beside_in)
-
-        def to_team(self, near):
-            arrived(self.key + 1, self.beside_in)
-            both = near[...].astype(F32) + self.core_in[tensor].astype(F32)
-            near[...] = (both + self.beside_in[...].astype(F32)).astype(BF)
-            for k in range(1, team):
-                device, place = mate(k)
-                send(self.key + 1 + k, near.at[self.part(place)], self.parts.at[k], device, self.like)
-
-        def add_parts(self, near):
-            whole = near[self.part(spot)].astype(F32)
-            for k in range(1, team):
-                arrived(self.key + 1 + k, self.parts.at[k])
-                whole = whole + self.parts[k].astype(F32)
-            piece = self.total.at[self.part(spot)]
+        def add(self, parts, start, size, box):
+            for n, part in enumerate(parts):
+                kept = self.pick(part, at(start, size, 16))
+                kept[...] = (kept[...].astype(F32) + box[n].astype(F32)).astype(BF)
+
+        def stage(self, k):
+            steps, rounds = len(self.plan), len(self.back)
+            both = (0, 1)
+            if k == 0:
+                arrived(self.key, self.core_in)
+                self.add(both, 0, self.total.shape[0], self.core_in)
+            elif k <= steps:
+                _, start, size, _ = self.plan[k - 1]
+                arrived(self.key + k, self.boxes[k - 1])
+                self.add((tensor,) if self.along < k else both, start, size, self.boxes[k - 1])
+            else:
+                _, _, _, size, start = self.back[k - steps - 1]
+                arrived(self.key + k, self.total.at[at(start, size, 16)])
+            if k < steps:
+                dim, _, size, start = self.plan[k]
+                if dim == "tensor":
+                    device = beside
+                    source = self.pick(pl.ds(1 - tensor, 1), at(start, size, 16))
+                else:
+                    device = mate(dim)[0]
+                    parts = pl.ds(tensor, 1) if self.along < k else slice(None)
+                    source = self.pick(parts, at(start, size, 16))
+                send(self.key + k + 1, source, self.boxes[k], device, self.boxes[k])
+            elif k == steps:
+                _, start, size, _ = self.plan[-1]
+                piece = self.total.at[at(start, size, 16)]
+                piece[...] = self.pick(tensor, at(start, size, 16))[...]
+                self.exchange_across(piece)
+            if steps <= k < steps + rounds:
+                _, dim, start, size, _ = self.back[k - steps]
+                region = self.total.at[at(start, size, 16)]
+                send(self.key + k + 1, region, region, mate(dim)[0], self.like[size])
+
+        def exchange_across(self, piece):
+            if teams == 1:
+                return
+            first = self.key + Cube.stages
+            for k in range(1, teams):
+                copy(first + k, piece, self.across.at[k], partner(k)).start()
+            whole = piece[...].astype(F32)
+            for k in range(1, teams):
+                arrived(first + k, self.across.at[k])
+                copy(first + k, piece, self.across.at[k], partner(k)).wait_send()
+                whole = whole + self.across[k].astype(F32)
             piece[...] = whole.astype(BF)
-            first = self.key + 2 * team
-            for k in range(1, teams):
-                copy(first + team + k, piece, self.across.at[k], partner(k)).start()
-            for k in range(1, teams):
-                arrived(first + team + k, self.across.at[k])
-                copy(first + team + k, piece, self.across.at[k], partner(k)).wait_send()
-                whole = whole + self.across[k].astype(F32)
-            if teams > 1:
-                piece[...] = whole.astype(BF)
-            for k in range(1, team):
-                send(first + k, piece, piece, mate(k)[0], self.like)
-
-        def finish(self):
-            for k in range(1, team):
-                arrived(self.key + 2 * team + k, self.total.at[self.part(mate(k)[1])])
-
-        keys = 3 * team + teams
-
-    key = 15
-    attn = Sum(key, wc, wy, attn_parts, attn_across, attn_sum)
-    key += Sum.keys
-    mlp = Sum(key, mlp_core, mlp_beside, mlp_parts, mlp_across, mlp_sum.at[section])
-    key += Sum.keys
-    mlp_far, mlp_near = grad_mlp.at[section, 1 - tensor], grad_mlp.at[section, tensor]
+
+        stages = len(attn_orders[0]) * 2
+        keys = stages + teams
+
+    chunks = len(mlp_orders)
+    key, taken = 15, 0
+
+    def boxes_of(order):
+        nonlocal taken
+        found = boxes[taken : taken + len(order) + 1]
+        taken += len(order) + 1
+        return found
+
+    def mlp_pick(q):
+        return lambda parts, where: grad_mlp.at[section, parts, q, where]
+
+    def attn_pick(n):
+        return lambda parts, where: grad_attn.at[section, parts, n, where]
+
+    dense, attn = [], []
+    for q in range(chunks):
+        total_of = mlp_sum.at[section, q]
+        dense.append(Cube(key, mlp_pick(q), mlp_core.at[q], total_of, mlp_orders[q], boxes_of(mlp_orders[q])))
+        key += Cube.keys
+    for n in range(2):
+        heard = wc.at[:, n * width : (n + 1) * width]
+        attn.append(Cube(key, attn_pick(n), heard, attn_sum.at[n], attn_orders[n], boxes_of(attn_orders[n])))
+        key += Cube.keys
     mlp_key, pack_key, small_key = key, key + 1, key + 1 + team + teams
+    mlp_like = mlp_sum.at[0]
+
+    def give_attn(b, n):
+        @only(1 - b)
+        def _():
+            attn[n].to_core(grad_attn.at[b, :, n])
+
+    def attn_stage(b, n, k):
+        @only(b)
+        def _():
+            attn[n].stage(k)
+
+    def give_dense(q):
+        dense[q].to_core(grad_mlp.at[1 - section, :, q])
 
     def attention(b, x_of, out_ref):
         def norm(i):
@@ -311,12 +372,17 @@
 
         loop(2, out)
 
-    def attention_back(b, x_of, beside_pairs, beside_rest):
+    def attention_back(b, x_of, beside_pairs, after_pairs):
         ga = low[...]
         got[...] = dot_t(wo[b], ga).astype(BF).reshape(pairs, LANES, window)
         for j in range(pairs):
             piece = dot(ot[b, j], ga).astype(BF)
-            put_grad(b, 3, j, piece)
+            if j < 2:
+                grad_attn[b, j, 1, 3 * HD : 5 * HD, :] = piece
+            else:
+                for t in range(2):
+                    grad_attn[b, t, 1, 5 * HD : 6 * HD, :] = piece[t * HD : (t + 1) * HD]
+        zz = z[2 * b]
 
         def pair(j):
             for at_pair, body in enumerate(beside_pairs):
@@ -332,27 +398,30 @@
                 inner = jnp.sum(weighted, axis=0, keepdims=True)
                 gs = (weighted - probs * inner).astype(BF)
                 gq = pair_down(dot(kt[b, j, :, k0 : k0 + count], gs)) * HD**-0.5
-                gt[pl.ds(pl.multiple_of(j * LANES, LANES), LANES), q0 : q0 + LANES] = gq.astype(BF)
+                gt[:LANES, q0 : q0 + LANES] = gq.astype(BF)
                 gk_sum[k0 : k0 + count] += dot_t(gs, q_pair)
                 gv_sum[k0 : k0 + count] += dot_t(low_probs, go_pair)
+            gtok[j] = gt[:LANES].T
             for c, total_of in ((1, gk_sum), (2, gv_sum)):
-                gtok[c * pairs + j] = total_of[...].astype(BF)
+                low_sum = total_of[...].astype(BF)
+                gtok[c * pairs + j] = low_sum
+                gt[c * LANES : (c + 1) * LANES] = low_sum.T
+            pieces = [dot(gt[c * LANES : (c + 1) * LANES], zz).astype(BF) for c in range(3)]
+
+            @pl.when(j < 2)
+            def _():
+                for c in range(3):
+                    grad_attn[b, j, 0, c * LANES : (c + 1) * LANES, :] = pieces[c]
+
+            @pl.when(j == 2)
+            def _():
+                for c in range(3):
+                    for t in range(2):
+                        grad_attn[b, t, 1, c * HD : (c + 1) * HD, :] = pieces[c][t * HD : (t + 1) * HD]
 
         loop(pairs, pair)
-        for j in range(pairs):
-            gtok[j] = gt[j * LANES : (j + 1) * LANES].T
-        for c in (1, 2):
-            for j in range(pairs):
-                first = (c * pairs + j) * LANES
-                gt[first : first + LANES] = gtok[c * pairs + j].T
-        zz = z[2 * b]
-        for c in range(3):
-            for j in range(pairs):
-                first = (c * pairs + j) * LANES
-                put_grad(b, c, j, dot(gt[first : first + LANES], zz).astype(BF))
-        beside_rest()
+        after_pairs()
         gain = gains[b, 0:1, :]
-        gain_grad = jnp.zeros((1, width), F32)
 
         def back(i, gain_grad):
             wide = jnp.concatenate([gtok[c, rows(i, half)] for c in range(3 * pairs)], axis=1)
@@ -360,15 +429,7 @@
             gx[rows(i, half)] += step
             return gain_grad + part
 
-        small[2 * b : 2 * b + 1, :] = lax.fori_loop(0, 2, back, gain_grad)
-
-    def put_grad(b, c, j, piece):
-        first = c * 3 * HD
-        if j < 2:
-            grad_attn[b, j, first : first + 2 * HD, :] = piece
-        else:
-            for t in range(2):
-                grad_attn[b, t, first + 2 * HD : first + 3 * HD, :] = piece[t * HD : (t + 1) * HD]
+        small[2 * b : 2 * b + 1, :] = lax.fori_loop(0, 2, back, jnp.zeros((1, width), F32))
 
     attention(0, lambda r: xw[r].astype(F32), x1)
 
@@ -381,20 +442,19 @@
 
     norm_middle(x1, 1)
 
-    @pl.when(section == 0)
+    @only(0)
     def _():
         arrived(5, mi.at[1 - tensor])
         send(6, mi.at[1 - tensor], mi.at[1 - tensor], core, mi_own)
         arrived(6, mo.at[1 - tensor])
 
-    @pl.when(section == 1)
+    @only(1)
     def _():
         arrived(5, mo.at[1 - tensor])
         send(6, mo.at[1 - tensor], mo.at[1 - tensor], core, mo_own)
         arrived(6, mi.at[1 - tensor])
 
     chunk = 256
-    chunks = mi.shape[2] // chunk
 
     def hidden_chunk(i):
         part, first = i // chunks, pl.multiple_of(i % chunks * chunk, chunk)
@@ -410,12 +470,12 @@
 
     loop(2, dense_out)
 
-    @pl.when(section == 0)
+    @only(0)
     def _():
         arrived(4, wc.at[1])
         place(wc.at[1], 1, 1 - tensor)
 
-    @pl.when(section == 1)
+    @only(1)
     def _():
         arrived(3, wy)
         send(4, wy, wc.at[1], core)
@@ -424,7 +484,6 @@
     attention(1, lambda r: sent[r].astype(F32), x3)
     norm_middle(x3, 3)
     z3 = z[3]
-    local(routert.at[tensor], router_own)
     arrived(8, routert.at[1 - tensor])
     powers = [jnp.exp(dot_t(routert[e], z3)[:1]) for e in range(2)]
     dispatch, combine = [], []
@@ -437,9 +496,6 @@
         mixing[0, e * SLOTS : (e + 1) * SLOTS] = d_low
         mixing[1, e * SLOTS : (e + 1) * SLOTS] = c_low
         slots[e] = dot(d_low, z3).astype(BF)
-    copy(4, wy, wc.at[1], core).wait_send()
-    sent_off.pop(4)
-
     send(9, slots.at[1 - tensor], slot_in.at[0], beside)
     arrived(7, cw.at[at((1 - tensor) * row_count, extra)])
 
@@ -530,13 +586,12 @@
 
     small[3:4, :] = lax.fori_loop(0, row_blocks, experts_back, jnp.zeros((1, width), F32))
 
-    def share_second():
-        @pl.when(section == 0)
-        def _():
-            attn.to_core(grad_attn.at[1])
-
-    share_pack = [share_slots, gather_slots, nothing]
-    attention_back(1, lambda r: sent[r].astype(F32), share_pack, share_second)
+    def shares_second():
+        gather_slots()
+        give_attn(1, 0)
+
+    share_slots()
+    attention_back(1, lambda r: sent[r].astype(F32), [nothing, nothing, shares_second], lambda: give_attn(1, 1))
 
     low[...] = gx[...].astype(BF)
     gsent = low[...]
@@ -544,26 +599,29 @@
     z2 = z[1]
     z2_t = z2.T
 
-    def hidden_back(i):
-        part, first = i // chunks, pl.multiple_of(i % chunks * chunk, chunk)
-        lanes = pl.ds(first, chunk)
-        grad_mlp[1, part, :, lanes] = dot(gsent_t, hidden[i]).astype(BF)
+    def hidden_back(n):
+        for ahead, body in ((2, dense_first), (4, dense_second)):
+            pl.when(n == ahead)(body)
+        q, part = n // 2, lax.rem(n, 2)
+        i, first = part * chunks + q, pl.multiple_of(q * chunk, chunk)
+        grad_mlp[1, part, q] = dot(gsent_t, hidden[i]).astype(BF)
         g_hidden = dot_t(gsent, mo[part, pl.ds(first, chunk), :])
         g_pre = (g_hidden * slope[i].astype(F32)).astype(BF)
         hidden[i] = g_pre
-        grad_mlp[0, part, :, lanes] = dot(z2_t, g_pre).astype(BF)
-
-    @pl.when(section == 1)
-    def _():
-        attn.to_beside(grad_attn.at[1, 1 - tensor])
+        grad_mlp[0, part, q] = dot(z2_t, g_pre).astype(BF)
+
+    def dense_first():
+        give_dense(0)
+        attn_stage(1, 0, 0)
+
+    def dense_second():
+        give_dense(1)
+        attn_stage(1, 1, 0)
+        dense[0].stage(0)
 
     loop(2 * chunks, hidden_back)
-    mlp.to_core(grad_mlp.at[1 - section])
-
-    @pl.when(section == 1)
-    def _():
-        attn.to_team(grad_attn.at[1, tensor])
-
+    give_dense(2)
+    dense[1].stage(0)
 
     def dense_back(i, gain_grad):
         gz = jnp.zeros((half, width), F32)
@@ -578,60 +636,85 @@
 
     small[1:2, :] = lax.fori_loop(0, 2, dense_back, jnp.zeros((1, width), F32))
 
-    def share_dense():
-        mlp.to_beside(mlp_far)
-
-    def reduce_second():
-        @pl.when(section == 1)
-        def _():
-            attn.add_parts(grad_attn.at[1, tensor])
-
-    def reduce_dense():
-        mlp.to_team(mlp_near)
-
-    def share_first():
-        @pl.when(section == 1)
-        def _():
-            attn.to_core(grad_attn.at[0])
-
-    attention_back(0, lambda r: xw[r].astype(F32), [share_dense, reduce_second, reduce_dense], share_first)
+    def beside_first():
+        dense[2].stage(0)
+        dense[0].stage(1)
+        attn_stage(1, 0, 1)
+
+    def beside_second():
+        dense[1].stage(1)
+        dense[0].stage(2)
+        attn_stage(1, 1, 1)
+
+    def beside_third():
+        dense[2].stage(1)
+        dense[1].stage(2)
+        attn_stage(1, 0, 2)
+        give_attn(0, 0)
+
+    def beside_rest():
+        dense[0].stage(3)
+        dense[2].stage(2)
+        attn_stage(1, 1, 2)
+        give_attn(0, 1)
+
+    attention_back(0, lambda r: xw[r].astype(F32), [beside_first, beside_second, beside_third], beside_rest)
     low[...] = gx[...].astype(BF)
     send(14, low.at[at((1 - tensor) * row_count, extra)], edge_in.at[1], beside)
     send(small_key, small, small_in.at[0], core)
-
-    @pl.when(section == 0)
-    def _():
-        attn.to_beside(grad_attn.at[0, 1 - tensor])
-
+    attn_stage(0, 0, 0)
+    dense[1].stage(3)
+    attn_stage(1, 0, 3)
+    dense[0].stage(4)
+    attn_stage(0, 1, 0)
     arrived(small_key, small_in.at[0])
     small_in[1] = small[...] + small_in[0]
     send(small_key + 1, small_in.at[1], small_in.at[2], beside)
-    mlp.add_parts(mlp_near)
+    dense[2].stage(3)
+    attn_stage(1, 1, 3)
 
     arrived(pack_key, packs.at[1])
     split_packs = packs[...].astype(F32).reshape(-1, 2, IMAGES, width)
     every_slot, every_grad = (split_packs[:, n].reshape(-1, width).astype(BF) for n in range(2))
     every_slot_t = every_slot.T
-
     few = chunk if teams == 1 else LANES
+    expert_steps = 2 * chunks * chunk // few
 
     def expert_grads(i):
+        for part, body in ((1, beside_experts_first), (2, beside_experts_second)):
+            pl.when(i == part * expert_steps // 3)(body)
         lanes = pl.ds(pl.multiple_of(i * few, few), few)
         value, grad = gelu_parts(dot(every_slot, ei[:, lanes]))
         g_pre = (dot_t(every_grad, eo[lanes, :]) * grad).astype(BF)
         expert_in_out[:, lanes] = dot(every_slot_t, g_pre).astype(BF)
         expert_out_out[lanes, :] = dot(value.astype(BF).T, every_grad).astype(BF)
 
-    loop(2 * chunks * chunk // few, expert_grads)
-
+    def beside_experts_first():
+        attn_stage(0, 0, 1)
+        attn_stage(1, 0, 4)
+        dense[1].stage(4)
+        dense[0].stage(5)
+
+    def beside_experts_second():
+        attn_stage(0, 1, 1)
+        attn_stage(1, 1, 4)
+        dense[2].stage(4)
+
+    loop(expert_steps, expert_grads)
+
+    attn_stage(0, 0, 2)
+    attn_stage(0, 1, 2)
+    attn_stage(1, 0, 5)
+    attn_stage(1, 1, 5)
     arrived(small_key + 1, small_in.at[2])
     small_parts[0] = small_in[1] + small_in[2]
     for k in range(1, team):
         send(small_key + 1 + k, small_parts.at[0], small_parts.at[k], mate(k)[0])
-
-    @pl.when(section == 0)
-    def _():
-        attn.to_team(grad_attn.at[0, tensor])
+    dense[0].stage(6)
+    dense[1].stage(5)
+    dense[2].stage(5)
+    attn_stage(0, 0, 3)
+    attn_stage(0, 1, 3)
 
     for n, (source, dest) in enumerate(((act, act_out), (low, pg_out))):
         dest[...] = source[at(tensor * extra, row_count)]
@@ -641,13 +724,20 @@
         merged = jnp.where(wide > 0.0, source[near].astype(F32), edge_in[n].astype(F32)).astype(BF)
         dest[at((1 - tensor) * (row_count - extra), extra)] = merged
 
-    @pl.when(section == 1)
-    def _():
-        attn.finish()
-
-    mlp.finish()
-    send(mlp_key, mlp_sum.at[section], mlp_sum.at[section], core, mlp_sum.at[0])
-
+    attn_stage(1, 0, 6)
+    attn_stage(1, 1, 6)
+    dense[0].stage(7)
+    dense[1].stage(6)
+    dense[2].stage(6)
+    attn_stage(0, 0, 4)
+    attn_stage(0, 1, 4)
+    attn_stage(1, 0, 7)
+    attn_stage(1, 1, 7)
+    dense[1].stage(7)
+    dense[2].stage(7)
+    send(mlp_key, mlp_sum.at[section], mlp_sum.at[section], core, mlp_like)
+    attn_stage(0, 0, 5)
+    attn_stage(0, 1, 5)
     for k in range(1, team):
         arrived(small_key + 1 + k, small_parts.at[k])
     small_across[0] = sum([small_parts[k] for k in range(1, team)], start=small_parts[0])
@@ -656,52 +746,74 @@
     for k in range(1, teams):
         arrived(small_key + 1 + team + k, small_across.at[k])
     small_out[...] = sum([small_across[k] for k in range(1, teams)], start=small_across[0])
-
-    @pl.when(section == 0)
-    def _():
-        attn.add_parts(grad_attn.at[0, tensor])
-        attn.finish()
-
+    attn_stage(0, 0, 6)
+    attn_stage(0, 1, 6)
     arrived(mlp_key, mlp_sum.at[1 - section])
-    attn_out[...] = attn_sum[...]
-    mlp_out[...] = mlp_sum[...]
+    for q in range(chunks):
+        for n, dest in enumerate((mi_out, mot_out)):
+            dest[:, q * chunk : (q + 1) * chunk] = mlp_sum[n, q]
+    attn_stage(0, 0, 7)
+    attn_stage(0, 1, 7)
+    for c in range(3):
+        first = c * 3 * HD
+        qkv_out[first : first + 2 * HD] = attn_sum[0, c * LANES : (c + 1) * LANES]
+        qkv_out[first + 2 * HD : first + 3 * HD] = attn_sum[1, c * HD : (c + 1) * HD]
+    attn_out[...] = attn_sum[1, 3 * HD :]
 
     for key, like in sent_off.items():
         copy(key, like, like, core).wait_send()
 
 
-def compute(x_own, c_own, ids, gains, w_own, mi, mo, router, ei, eo):
+def compute(x_own, c_own, ids, gains, qkv, out, mi, mo, router, ei, eo):
     row_count, width = x_own.shape
     window = row_count + MOST // 2
     extra = window - row_count
     pairs = width // LANES
     ff = ei.shape[1]
     _, kept = bands(window)
-    chunk_count = 2 * mi.shape[1] // 256
+    chunk_count = ff // 256
+    chunks = chunk_count // 2
     vmem = pl.BlockSpec(memory_space=pltpu.VMEM)
     ranks = lax.axis_size("dp")
     team = min(8, ranks & -ranks)
     teams = ranks // team
-    copies = 15 + 2 * (3 * team + teams) + 1 + team + teams + 1 + team + teams
+    bits = [1 << n for n in range(team.bit_length() - 1)]
+    spread = [bits[:1] + ["tensor"] + bits[1:], ["tensor"] + bits, bits[1::-1] + ["tensor"] + bits[2:]]
+    mlp_orders = [spread[q % 3] for q in range(chunks)]
+    attn_orders = [spread[2], spread[1]]
+    boxes = []
+    for order, lanes in [(order, 256) for order in mlp_orders] + [(order, width) for order in attn_orders]:
+        size = width
+        for n, dim in enumerate(order):
+            size = size if dim == "tensor" else size // 2
+            boxes.append(pltpu.VMEM((2 if "tensor" in order[n + 1 :] else 1, size, lanes), BF))
+        boxes.append(pltpu.VMEM((teams, size, lanes), BF))
+    stages = 2 * len(attn_orders[0])
+    copies = 15 + (chunks + 2) * (stages + teams) + 1 + 2 * (team + teams + 1)
     return pl.pallas_call(
-        functools.partial(compute_kernel, team=team, teams=teams),
+        functools.partial(
+            compute_kernel, team=team, teams=teams, mlp_orders=mlp_orders, attn_orders=attn_orders
+        ),
         out_shape=(
             jax.ShapeDtypeStruct((row_count, width), BF),
             jax.ShapeDtypeStruct((row_count, width), BF),
-            jax.ShapeDtypeStruct((2 * width, width), BF),
-            jax.ShapeDtypeStruct((2, width, ff // 2), BF),
+            jax.ShapeDtypeStruct(qkv.shape, BF),
+            jax.ShapeDtypeStruct(out.shape, BF),
+            jax.ShapeDtypeStruct((width, ff // 2), BF),
+            jax.ShapeDtypeStruct((width, ff // 2), BF),
             jax.ShapeDtypeStruct((width, ff), BF),
             jax.ShapeDtypeStruct((ff, width), BF),
             jax.ShapeDtypeStruct((8, width), F32),
         ),
-        in_specs=[vmem] * 10,
-        out_specs=[vmem] * 7,
+        in_specs=[vmem] * 11,
+        out_specs=[vmem] * 9,
         scratch_shapes=[
             pltpu.VMEM((window, width), BF),
             pltpu.VMEM((window, width), BF),
             pltpu.VMEM((2, 8, width), F32),
             pltpu.VMEM((2 * width, width), BF),
             pltpu.VMEM((2, 2 * width, width), BF),
+            pltpu.VMEM((2 * width, width), BF),
             pltpu.VMEM((2, 3 * width, width), BF),
             pltpu.VMEM((2, width, width), BF),
             pltpu.VMEM((2, *mi.shape), BF),
@@ -730,7 +842,7 @@
             pltpu.VMEM((window, width), F32),
             pltpu.VMEM((window, width), BF),
             pltpu.VMEM((pairs, LANES, window), BF),
-            pltpu.VMEM((3 * width, window), BF),
+            pltpu.VMEM((3 * LANES, window), BF),
             pltpu.VMEM((3 * pairs, window, LANES), BF),
             pltpu.VMEM((window, LANES), F32),
             pltpu.VMEM((window, LANES), F32),
@@ -740,16 +852,11 @@
             pltpu.VMEM((SLOTS, ff), F32),
             pltpu.VMEM((2, SLOTS, width), BF),
             pltpu.VMEM((2, SLOTS, width), BF),
-            pltpu.VMEM((2, 2, 2 * width, width), BF),
-            pltpu.VMEM((team, 2 * width // team, width), BF),
-            pltpu.VMEM((teams, 2 * width // team, width), BF),
-            pltpu.VMEM((2 * width, width), BF),
-            pltpu.VMEM((2, 2, width, ff // 2), BF),
-            pltpu.VMEM((2, width, ff // 2), BF),
-            pltpu.VMEM((width, ff // 2), BF),
-            pltpu.VMEM((team, width // team, ff // 2), BF),
-            pltpu.VMEM((teams, width // team, ff // 2), BF),
-            pltpu.VMEM((2, width, ff // 2), BF),
+            pltpu.VMEM((2, 2, 2, width, width), BF),
+            pltpu.VMEM((2, width, width), BF),
+            pltpu.VMEM((2, 2, chunks, width, 256), BF),
+            pltpu.VMEM((chunks, 2, width, 256), BF),
+            pltpu.VMEM((2, chunks, width, 256), BF),
             pltpu.VMEM((8, width), F32),
             pltpu.VMEM((3, 8, width), F32),
             pltpu.VMEM((team, 8, width), F32),
@@ -758,40 +865,78 @@
             pltpu.VMEM((2 * IMAGES, width), BF),
             pltpu.SemaphoreType.DMA((copies,)),
             pltpu.SemaphoreType.DMA((copies,)),
+            *boxes,
         ],
         compiler_params=pltpu.CompilerParams(
-            vmem_limit_bytes=60 * 1024 * 1024, collective_id=0, has_side_effects=True
+            vmem_limit_bytes=62 * 1024 * 1024, collective_id=0, has_side_effects=True
         ),
-    )(x_own, c_own, ids, gains, w_own, mi, mo, router, ei, eo)
+    )(x_own, c_own, ids, gains, qkv, out, mi, mo, router, ei, eo)
+
+
+def finish_kernel(
+    act, pg, qkv, attn, mi, mot, expert_in, expert_out, small,
+    act_out, pg_out, gains_out, qkv_out, attn_out, mi_out, mo_out, router_out, expert_in_out, expert_out_out,
+):
+    section, tensor = lax.axis_index("section"), lax.axis_index("tensor")
+    act_out[...] = act[...]
+    pg_out[...] = pg[...]
+    gains_out[...] = jnp.where(section == 0, small[0:2], small[2:4])
+    router_out[...] = jnp.where(tensor == 0, small[4:5], small[5:6])
+    pairs = ((qkv, qkv_out), (attn, attn_out), (mi, mi_out), (expert_in, expert_in_out), (expert_out, expert_out_out))
+    for source, dest in pairs:
+        dest[...] = source[...].astype(F32)
+    mo_out[...] = mot[...].astype(F32).T
+
+
+def finish(act, pg, qkv, attn, mi, mot, expert_in, expert_out, small):
+    steps = 3
+
+    def by_rows(a):
+        return pl.BlockSpec((a.shape[0] // steps, a.shape[1]), lambda i: (i, 0))
+
+    def whole(a):
+        return pl.BlockSpec(a.shape, lambda i: (0, 0))
+
+    def like(a):
+        return jax.ShapeDtypeStruct(a.shape, F32)
+
+    gains = jax.ShapeDtypeStruct((2, act.shape[1]), F32)
+    router = jax.ShapeDtypeStruct((1, act.shape[1]), F32)
+    mo = jax.ShapeDtypeStruct(mot.shape[::-1], F32)
+    mot_spec = pl.BlockSpec((mot.shape[0], mot.shape[1] // steps), lambda i: (0, i))
+    return pl.pallas_call(
+        finish_kernel,
+        grid=(steps,),
+        out_shape=(
+            act, pg, gains, like(qkv), like(attn), like(mi), mo, router, like(expert_in), like(expert_out)
+        ),
+        in_specs=[
+            whole(act), whole(pg), by_rows(qkv), by_rows(attn), by_rows(mi), mot_spec, by_rows(expert_in),
+            by_rows(expert_out), whole(small),
+        ],
+        out_specs=[
+            whole(act), whole(pg), whole(gains), by_rows(qkv), by_rows(attn), by_rows(mi), by_rows(mo), whole(router),
+            by_rows(expert_in), by_rows(expert_out),
+        ],
+        compiler_params=pltpu.CompilerParams(vmem_limit_bytes=60 * 1024 * 1024),
+    )(act, pg, qkv, attn, mi, mot, expert_in, expert_out, small)
 
 
 def per_device(
     patches, image_ids, cotangent, norm_gains, qkv_weight, out_weight, mlp_in, mlp_out, router, expert_in, expert_out
 ):
     width = patches.shape[2]
-    tensor = lax.axis_index("tensor")
-    heads = qkv_weight.shape[3] // HD
-    w_own = jnp.concatenate([jnp.transpose(qkv_weight[0], (1, 2, 0)).reshape(-1, width), out_weight[0]], axis=0)
-    gains = jnp.pad(norm_gains[0], ((0, 6), (0, 0)))
-    router_own = jnp.pad(router.T, ((0, SLOTS - router.shape[1]), (0, 0)))
-    activations, patch_grad, attn, mlp, expert_in_grad, expert_out_grad, small = compute(
-        patches[0], cotangent[0], image_ids, gains, w_own, mlp_in, mlp_out, router_own, expert_in[0], expert_out[0]
+    part = qkv_weight.shape[3]
+    qkv = jnp.transpose(qkv_weight[0], (1, 2, 0)).reshape(-1, width)
+    results = compute(
+        patches[0], cotangent[0], image_ids, norm_gains[0], qkv, out_weight[0], mlp_in, mlp_out, router.T,
+        expert_in[0], expert_out[0],
     )
-    rows = 3 * heads * HD
-    qkv_grad = jnp.transpose(attn[:rows].astype(F32).reshape(3, heads * HD, width), (2, 0, 1))
-    gains_grad = lax.dynamic_slice_in_dim(small, 2 * lax.axis_index("section"), 2, 0)
-    router_grad = lax.dynamic_slice_in_dim(small, 4 + tensor, 1, 0).T
+    act, pg, gains, qkv_grad, out_grad, mi_grad, mo_grad, router_grad, ei_grad, eo_grad = finish(*results)
+    qkv_grad = jnp.transpose(qkv_grad.reshape(3, part, width), (2, 0, 1))
     return (
-        activations[None],
-        patch_grad[None],
-        gains_grad[None],
-        qkv_grad[None],
-        attn[rows:].astype(F32)[None],
-        mlp[0].astype(F32),
-        mlp[1].astype(F32).T,
-        router_grad,
-        expert_in_grad.astype(F32)[None],
-        expert_out_grad.astype(F32)[None],
+        act[None], pg[None], gains[None], qkv_grad[None], out_grad[None], mi_grad, mo_grad, router_grad.T,
+        ei_grad[None], eo_grad[None],
     )
 
 

time: 173 us -> 150 us (0.87)
  other arithmetic: 9.02 us -> 0 us
  local copies, waits for them, and re-layouts: 8.51 us -> 0 us
  Pallas kernels: 155 us -> 149 us
    pallas_call x1 -> x2, Pallas kernels: 155 us -> 149 us  [the longest x1 142 us: compute(): pl.pallas_call(functools.partial(compute_kernel, team=team, teams=teams,...]
    broadcast_in_dim x4 -> x0, other arithmetic: 5.87 us -> none  [the longest x1 1.69 us: per_device(): expert_in_grad.astype(F32)[None]]
    unnamed x15 -> x0, local copies, waits for them, and re-layouts: 2.9 us -> none
    concatenate x1 -> x0, other arithmetic: 1.97 us -> none  [per_device(): jnp.concatenate([jnp.transpose(qkv_weight[0], (1, 2, 0)).reshape(-1, widt...]
    pad x2 -> x0, local copies, waits for them, and re-layouts: 1.9 us -> none  [the longest x1 1.29 us: per_device(): gains = jnp.pad(norm_gains[0], ((0, 6), (0, 0)))]
where the time goes in v4:
time: 150 us; the launch traced here: 149 us
  Pallas kernels  149 us (99%)
    pallas_call x1, Pallas kernels, compute(): pl.pallas_call(functools.partial(compute_kernel, team=team, teams=teams,...  142 us
    pallas_call x1, Pallas kernels, finish(): pl.pallas_call(finish_kernel, grid=(steps,), out_shape=(act, pg, gains, l...  6.48 us

profile of v4, /device:TPU:0, one launch (start us, length us, event | category | flops | bytes accessed | tf_op | source)
XLA Modules:
  0.0 149.5 jit_solution(11913040814437861311)
XLA Ops:
  0.6 142.2 %shard_map.186 = (bf16[512,384]{1,0:T(8,128)(2,1)}, bf16[512,384]{1,0:T(8,128)(2,1)}, bf16[576,384]{1,0:T(8,128)(2,1)}, bf16[192,384]{1,0:T(8,128)(2,1)}, bf16[3...) custom-call(bf16[512,384]{1,0:T(8,128)(2,1)} %bitcast.27, ...), custom_call_target="tpu_custom_call" | custom-call | tf_op jit(solution)/shard_map/pallas_call | solution.py:793
  142.8 6.5 %shard_map.187 = (bf16[512,384]{1,0:T(8,128)(2,1)}, bf16[512,384]{1,0:T(8,128)(2,1)}, f32[2,384]{1,0:T(2,128)}, f32[576,384]{1,0:T(8,128)}, f32[192,384]{1,0:T(8...) custom-call(bf16[512,384]{1,0:T(8,128)(2,1)} %get-tuple-element.29.a, ...), custom_call_target="tpu_custom_call" | custom-call | tf_op jit(solution)/shard_map/pallas_call | solution.py:907

commit v5 on v4

--- a/solution.py
+++ b/solution.py
@@ -75,13 +75,13 @@
 
 
 def compute_kernel(
-    x_own, c_own, ids, gains_own, qkv_own, out_own, mi_own, mo_own, router_own, ei, eo,
+    x_own, c_own, ids, gains_own, qkv_own, out_own, mi_own, mo_own, router_own, ei_own, eo_own,
     act_out, pg_out, qkv_out, attn_out, mi_out, mot_out, expert_in_out, expert_out_out, small_out,
-    xw, cw, gains, wy, wc, w_own, wqkv, wo, mi, mo, routert, act, edge_in, slots, geos, slot_in, pack,
+    xw, cw, gains, wy, wc, w_own, wqkv, wo, mi, mo, ei, eo, expert_in_sum, expert_out_sum, routert, act, edge_in, slots, geos, slot_in, pack,
     z, x1, sent, x3, qt, kt, vt, kr, vr, ot, pt, tok, hidden, slope, gx, low, got, gt, gtok, gk_sum, gv_sum,
     bias, own, mixing, eslope, eout, gslot, grad_attn, attn_sum, grad_mlp, mlp_core, mlp_sum,
-    small, small_in, small_parts, small_across, packs, small_pack, send_sem, recv_sem,
-    *boxes, team, teams, mlp_orders, attn_orders,
+    small, small_in, small_parts, small_across, packs, small_pack, send_sem, recv_sem, here_sem,
+    *boxes, team, teams, mlp_orders,
 ):
     row_count, width = x_own.shape
     window = xw.shape[0]
@@ -151,30 +151,46 @@
     neighbours = [core, beside] + [mate(k)[0] for k in range(1, team)] + [partner(k) for k in range(1, teams)]
     for device in neighbours:
         pl.semaphore_signal(barrier, inc=1, device_id=device, device_id_type=MESH)
-    pl.semaphore_wait(barrier, len(neighbours))
-
-    edge = x_own.at[at((1 - tensor) * (row_count - extra), extra)]
-    send(0, edge, xw.at[at(tensor * row_count, extra)], beside)
+
+    def local(key, source, dest):
+        found = pltpu.make_async_copy(source, dest, here_sem.at[key])
+        found.start()
+        return found
+
+    qkv_rows = qkv_own.shape[0]
+    own_rows = at(tensor * extra, row_count)
+    near_copies = [
+        local(0, x_own, xw.at[own_rows]),
+        local(1, qkv_own, w_own.at[:qkv_rows]),
+        local(2, out_own, w_own.at[qkv_rows:]),
+    ]
+    later_copies = [
+        local(3, mi_own, mi.at[tensor]),
+        local(4, mo_own, mo.at[tensor]),
+        local(5, c_own, cw.at[own_rows]),
+        local(6, ei_own, ei),
+        local(7, eo_own, eo),
+    ]
     gains[section, :2] = gains_own[...]
-    send(1, gains.at[section], gains.at[section], core)
-    w_own[: qkv_own.shape[0]] = qkv_own[...]
-    w_own[qkv_own.shape[0] :] = out_own[...]
-    send(2, w_own, wc.at[0], core)
-
-    @only(0)
-    def _():
-        send(3, w_own, wy, beside)
-
-    def local(dest, source):
-        dest[...] = source[...]
-
-    local(xw.at[at(tensor * extra, row_count)], x_own)
-    local(cw.at[at(tensor * extra, row_count)], c_own)
-    local(mi.at[tensor], mi_own)
-    local(mo.at[tensor], mo_own)
     first_row = lax.broadcasted_iota(jnp.int32, (SLOTS, width), 0) == 0
     router_rows = jnp.broadcast_to(router_own[...].astype(F32), (SLOTS, width))
     routert[tensor] = jnp.where(first_row, router_rows, 0.0).astype(BF)
+    pl.semaphore_wait(barrier, len(neighbours))
+
+    qkv_here, out_here = wy.at[:qkv_rows], wy.at[qkv_rows:]
+    qkv_near, out_near = wc.at[0, :qkv_rows], wc.at[0, qkv_rows:]
+    qkv_far, out_far = wc.at[1, :qkv_rows], wc.at[1, qkv_rows:]
+
+    @only(0)
+    def _():
+        send(3, qkv_own, qkv_here, beside)
+        send(15, out_own, out_here, beside)
+
+    edge = x_own.at[at((1 - tensor) * (row_count - extra), extra)]
+    send(0, edge, xw.at[at(tensor * row_count, extra)], beside)
+    send(1, gains.at[section], gains.at[section], core)
+    send(2, qkv_own, qkv_near, core)
+    send(16, out_own, out_near, core)
 
     ids_row = ids[pl.ds(section, 1), :].astype(F32)
     image = lax.broadcasted_iota(jnp.int32, (SLOTS, total), 0).astype(F32)
@@ -192,36 +208,72 @@
         same = ids_col[k0 : k0 + count] == jnp.broadcast_to(window_ids[:, q0 : q0 + LANES], (count, LANES))
         bias[kept : kept + count, :] = jnp.where(same, 0.0, -1e30)
 
-    def place(source, b, t):
-        for c in range(4):
+    def place(source, b, t, kinds=(0, 1, 2, 3)):
+        for c in kinds:
             dest, base = (wqkv, c * width) if c < 3 else (wo, 0)
             first = c * 3 * HD
             dest[b, at(base + t * LANES, 2 * HD)] = source[first : first + 2 * HD]
             dest[b, at(base + 2 * LANES + t * HD, HD, HD)] = source[first + 2 * HD : first + 3 * HD]
 
+    for found in near_copies:
+        found.wait()
+    place(w_own, section, tensor)
+    arrived(1, gains.at[1 - section])
+    arrived(2, qkv_near)
+    arrived(16, out_near)
+    place(wc.at[0], 1 - section, tensor)
     arrived(0, xw.at[at((1 - tensor) * row_count, extra)])
-    arrived(1, gains.at[1 - section])
-    arrived(2, wc.at[0])
-    place(w_own, section, tensor)
-    place(wc.at[0], 1 - section, tensor)
 
     @only(0)
     def _():
-        arrived(3, wy)
-        send(4, wy, wc.at[1], core)
+        arrived(3, qkv_here)
+        send(4, qkv_here, qkv_far, core)
         send(5, mi_own, mi.at[tensor], beside)
-        place(wy, 0, 1 - tensor)
+        place(wy, 0, 1 - tensor, (0, 1, 2))
 
     @only(1)
     def _():
+        arrived(4, qkv_far)
         send(5, mo_own, mo.at[tensor], beside)
-        send(3, w_own, wy, beside)
-        arrived(4, wc.at[1])
-        place(wc.at[1], 0, 1 - tensor)
-
-    c_edge = c_own.at[at((1 - tensor) * (row_count - extra), extra)]
-    send(7, c_edge, cw.at[at(tensor * row_count, extra)], beside)
-    send(8, routert.at[tensor], routert.at[tensor], beside)
+        place(wc.at[1], 0, 1 - tensor, (0, 1, 2))
+
+    def first_out():
+        @only(0)
+        def _():
+            arrived(15, out_here)
+            send(17, out_here, out_far, core)
+            place(wy, 0, 1 - tensor, (3,))
+
+        @only(1)
+        def _():
+            arrived(17, out_far)
+            send(3, qkv_own, qkv_here, beside)
+            send(15, out_own, out_here, beside)
+            place(wc.at[1], 0, 1 - tensor, (3,))
+
+    def second_out():
+        @only(0)
+        def _():
+            arrived(17, out_far)
+            place(wc.at[1], 1, 1 - tensor, (3,))
+
+        @only(1)
+        def _():
+            arrived(15, out_here)
+            send(17, out_here, out_far, core)
+            place(wy, 1, 1 - tensor, (3,))
+
+    def add_across(first, piece, heard):
+        if teams == 1:
+            return
+        for k in range(1, teams):
+            copy(first + k, piece, heard.at[k], partner(k)).start()
+        whole = piece[...].astype(F32)
+        for k in range(1, teams):
+            arrived(first + k, heard.at[k])
+            copy(first + k, piece, heard.at[k], partner(k)).wait_send()
+            whole = whole + heard[k].astype(F32)
+        piece[...] = whole.astype(BF)
 
     class Cube:
         def __init__(self, key, pick, core_in, total, order, boxes):
@@ -275,36 +327,67 @@
                 _, start, size, _ = self.plan[-1]
                 piece = self.total.at[at(start, size, 16)]
                 piece[...] = self.pick(tensor, at(start, size, 16))[...]
-                self.exchange_across(piece)
+                add_across(self.key + Cube.stages, piece, self.across)
             if steps <= k < steps + rounds:
                 _, dim, start, size, _ = self.back[k - steps]
                 region = self.total.at[at(start, size, 16)]
                 send(self.key + k + 1, region, region, mate(dim)[0], self.like[size])
 
-        def exchange_across(self, piece):
-            if teams == 1:
-                return
-            first = self.key + Cube.stages
-            for k in range(1, teams):
-                copy(first + k, piece, self.across.at[k], partner(k)).start()
-            whole = piece[...].astype(F32)
-            for k in range(1, teams):
-                arrived(first + k, self.across.at[k])
-                copy(first + k, piece, self.across.at[k], partner(k)).wait_send()
-                whole = whole + self.across[k].astype(F32)
-            piece[...] = whole.astype(BF)
-
-        stages = len(attn_orders[0]) * 2
+        stages = len(mlp_orders[0]) * 2
         keys = stages + teams
 
+    class Straight:
+        def __init__(self, key, pick, core_in, total, boxes):
+            self.key, self.pick, self.core_in, self.total = key, pick, core_in, total
+            self.beside_in, self.parts, self.across = boxes
+            self.size = total.shape[0] // team
+            self.like = total.at[: self.size]
+
+        def part(self, place):
+            return at(place * self.size, self.size, 16)
+
+        def to_core(self, source):
+            send(self.key, source, self.core_in, core, self.core_in)
+
+        def stage(self, k):
+            every = pl.ds(0, self.total.shape[0])
+            near = self.pick(tensor, every)
+            if k == 0:
+                arrived(self.key, self.core_in)
+                far = self.pick(1 - tensor, every)
+                far[...] = (far[...].astype(F32) + self.core_in[1 - tensor].astype(F32)).astype(BF)
+                send(self.key + 1, far, self.beside_in, beside, self.beside_in)
+            if k == 1:
+                arrived(self.key + 1, self.beside_in)
+                both = near[...].astype(F32) + self.core_in[tensor].astype(F32)
+                near[...] = (both + self.beside_in[...].astype(F32)).astype(BF)
+                for n in range(1, team):
+                    device, place = mate(n)
+                    source = self.pick(tensor, self.part(place))
+                    send(self.key + 1 + n, source, self.parts.at[n], device, self.like)
+            if k == 2:
+                whole = self.pick(tensor, self.part(spot))[...].astype(F32)
+                for n in range(1, team):
+                    arrived(self.key + 1 + n, self.parts.at[n])
+                    whole = whole + self.parts[n].astype(F32)
+                piece = self.total.at[self.part(spot)]
+                piece[...] = whole.astype(BF)
+                add_across(self.key + 1 + 2 * team, piece, self.across)
+                for n in range(1, team):
+                    send(self.key + 1 + team + n, piece, piece, mate(n)[0], self.like)
+            if k == 3:
+                for n in range(1, team):
+                    arrived(self.key + 1 + team + n, self.total.at[self.part(mate(n)[1])])
+
+        keys = 1 + 2 * team + teams
+
     chunks = len(mlp_orders)
-    key, taken = 15, 0
-
-    def boxes_of(order):
+    key, taken = 18, 0
+
+    def boxes_of(count):
         nonlocal taken
-        found = boxes[taken : taken + len(order) + 1]
-        taken += len(order) + 1
-        return found
+        taken += count
+        return boxes[taken - count : taken]
 
     def mlp_pick(q):
         return lambda parts, where: grad_mlp.at[section, parts, q, where]
@@ -315,12 +398,13 @@
     dense, attn = [], []
     for q in range(chunks):
         total_of = mlp_sum.at[section, q]
-        dense.append(Cube(key, mlp_pick(q), mlp_core.at[q], total_of, mlp_orders[q], boxes_of(mlp_orders[q])))
+        found = boxes_of(len(mlp_orders[q]) + 1)
+        dense.append(Cube(key, mlp_pick(q), mlp_core.at[q], total_of, mlp_orders[q], found))
         key += Cube.keys
     for n in range(2):
         heard = wc.at[:, n * width : (n + 1) * width]
-        attn.append(Cube(key, attn_pick(n), heard, attn_sum.at[n], attn_orders[n], boxes_of(attn_orders[n])))
-        key += Cube.keys
+        attn.append(Straight(key, attn_pick(n), heard, attn_sum.at[n], boxes_of(3)))
+        key += Straight.keys
     mlp_key, pack_key, small_key = key, key + 1, key + 1 + team + teams
     mlp_like = mlp_sum.at[0]
 
@@ -337,7 +421,7 @@
     def give_dense(q):
         dense[q].to_core(grad_mlp.at[1 - section, :, q])
 
-    def attention(b, x_of, out_ref):
+    def attention(b, x_of, out_ref, ahead_of_out):
         def norm(i):
             unit, _ = normalise(x_of(rows(i)))
             z[2 * b, rows(i)] = (unit * gains[b, 0:1, :]).astype(BF)
@@ -366,6 +450,8 @@
         loop(pairs, pair)
         for j in range(pairs):
             tok[:, j * LANES : (j + 1) * LANES] = ot[b, j].T
+
+        ahead_of_out()
 
         def out(i):
             out_ref[rows(i, half)] = x_of(rows(i, half)) + dot(tok[rows(i, half)], wo[b])
@@ -431,7 +517,7 @@
 
         small[2 * b : 2 * b + 1, :] = lax.fori_loop(0, 2, back, jnp.zeros((1, width), F32))
 
-    attention(0, lambda r: xw[r].astype(F32), x1)
+    attention(0, lambda r: xw[r].astype(F32), x1, first_out)
 
     def norm_middle(source, which):
         def body(i):
@@ -441,6 +527,9 @@
         loop(row_blocks, body)
 
     norm_middle(x1, 1)
+
+    for found in later_copies:
+        found.wait()
 
     @only(0)
     def _():
@@ -472,16 +561,20 @@
 
     @only(0)
     def _():
-        arrived(4, wc.at[1])
-        place(wc.at[1], 1, 1 - tensor)
+        arrived(4, qkv_far)
+        place(wc.at[1], 1, 1 - tensor, (0, 1, 2))
 
     @only(1)
     def _():
-        arrived(3, wy)
-        send(4, wy, wc.at[1], core)
-        place(wy, 1, 1 - tensor)
-
-    attention(1, lambda r: sent[r].astype(F32), x3)
+        arrived(3, qkv_here)
+        send(4, qkv_here, qkv_far, core)
+        place(wy, 1, 1 - tensor, (0, 1, 2))
+
+    c_edge = c_own.at[at((1 - tensor) * (row_count - extra), extra)]
+    send(7, c_edge, cw.at[at(tensor * row_count, extra)], beside)
+    send(8, routert.at[tensor], routert.at[tensor], beside)
+
+    attention(1, lambda r: sent[r].astype(F32), x3, second_out)
     norm_middle(x3, 3)
     z3 = z[3]
     arrived(8, routert.at[1 - tensor])
@@ -617,11 +710,10 @@
     def dense_second():
         give_dense(1)
         attn_stage(1, 1, 0)
-        dense[0].stage(0)
 
     loop(2 * chunks, hidden_back)
     give_dense(2)
-    dense[1].stage(0)
+    dense[0].stage(0)
 
     def dense_back(i, gain_grad):
         gz = jnp.zeros((half, width), F32)
@@ -637,41 +729,38 @@
     small[1:2, :] = lax.fori_loop(0, 2, dense_back, jnp.zeros((1, width), F32))
 
     def beside_first():
+        dense[1].stage(0)
+        attn_stage(1, 0, 1)
+
+    def beside_second():
         dense[2].stage(0)
         dense[0].stage(1)
-        attn_stage(1, 0, 1)
-
-    def beside_second():
+        attn_stage(1, 1, 1)
+
+    def beside_third():
+        give_attn(0, 0)
         dense[1].stage(1)
+        attn_stage(1, 0, 2)
+
+    def beside_rest():
+        give_attn(0, 1)
+        attn_stage(0, 0, 0)
+        dense[2].stage(1)
         dense[0].stage(2)
-        attn_stage(1, 1, 1)
-
-    def beside_third():
-        dense[2].stage(1)
-        dense[1].stage(2)
-        attn_stage(1, 0, 2)
-        give_attn(0, 0)
-
-    def beside_rest():
-        dense[0].stage(3)
-        dense[2].stage(2)
         attn_stage(1, 1, 2)
-        give_attn(0, 1)
 
     attention_back(0, lambda r: xw[r].astype(F32), [beside_first, beside_second, beside_third], beside_rest)
     low[...] = gx[...].astype(BF)
     send(14, low.at[at((1 - tensor) * row_count, extra)], edge_in.at[1], beside)
     send(small_key, small, small_in.at[0], core)
-    attn_stage(0, 0, 0)
-    dense[1].stage(3)
-    attn_stage(1, 0, 3)
-    dense[0].stage(4)
     attn_stage(0, 1, 0)
+    dense[1].stage(2)
+    dense[2].stage(2)
     arrived(small_key, small_in.at[0])
     small_in[1] = small[...] + small_in[0]
     send(small_key + 1, small_in.at[1], small_in.at[2], beside)
-    dense[2].stage(3)
-    attn_stage(1, 1, 3)
+    attn_stage(0, 0, 1)
+    dense[0].stage(3)
 
     arrived(pack_key, packs.at[1])
     split_packs = packs[...].astype(F32).reshape(-1, 2, IMAGES, width)
@@ -686,58 +775,44 @@
         lanes = pl.ds(pl.multiple_of(i * few, few), few)
         value, grad = gelu_parts(dot(every_slot, ei[:, lanes]))
         g_pre = (dot_t(every_grad, eo[lanes, :]) * grad).astype(BF)
-        expert_in_out[:, lanes] = dot(every_slot_t, g_pre).astype(BF)
-        expert_out_out[lanes, :] = dot(value.astype(BF).T, every_grad).astype(BF)
+        expert_in_sum[:, lanes] = dot(every_slot_t, g_pre).astype(BF)
+        expert_out_sum[lanes, :] = dot(value.astype(BF).T, every_grad).astype(BF)
 
     def beside_experts_first():
-        attn_stage(0, 0, 1)
-        attn_stage(1, 0, 4)
+        attn_stage(0, 1, 1)
+        dense[1].stage(3)
+        dense[2].stage(3)
+
+    def beside_experts_second():
+        dense[0].stage(4)
+        attn_stage(0, 0, 2)
         dense[1].stage(4)
-        dense[0].stage(5)
-
-    def beside_experts_second():
-        attn_stage(0, 1, 1)
-        attn_stage(1, 1, 4)
-        dense[2].stage(4)
 
     loop(expert_steps, expert_grads)
 
-    attn_stage(0, 0, 2)
-    attn_stage(0, 1, 2)
-    attn_stage(1, 0, 5)
-    attn_stage(1, 1, 5)
+    last_copies = [local(0, expert_in_sum, expert_in_out), local(1, expert_out_sum, expert_out_out)]
     arrived(small_key + 1, small_in.at[2])
     small_parts[0] = small_in[1] + small_in[2]
     for k in range(1, team):
         send(small_key + 1 + k, small_parts.at[0], small_parts.at[k], mate(k)[0])
-    dense[0].stage(6)
+    dense[2].stage(4)
+    dense[0].stage(5)
+    attn_stage(0, 1, 2)
     dense[1].stage(5)
     dense[2].stage(5)
-    attn_stage(0, 0, 3)
-    attn_stage(0, 1, 3)
 
     for n, (source, dest) in enumerate(((act, act_out), (low, pg_out))):
-        dest[...] = source[at(tensor * extra, row_count)]
         arrived(13 + n, edge_in.at[n])
         near = at(row_count - extra - tensor * (row_count - 2 * extra), extra)
         wide = jnp.concatenate([own[near]] * pairs, axis=1)
-        merged = jnp.where(wide > 0.0, source[near].astype(F32), edge_in[n].astype(F32)).astype(BF)
-        dest[at((1 - tensor) * (row_count - extra), extra)] = merged
-
-    attn_stage(1, 0, 6)
-    attn_stage(1, 1, 6)
-    dense[0].stage(7)
+        source[near] = jnp.where(wide > 0.0, source[near].astype(F32), edge_in[n].astype(F32)).astype(BF)
+        last_copies.append(local(2 + n, source.at[own_rows], dest))
+
+    attn_stage(1, 0, 3)
+    attn_stage(1, 1, 3)
+    dense[0].stage(6)
     dense[1].stage(6)
     dense[2].stage(6)
-    attn_stage(0, 0, 4)
-    attn_stage(0, 1, 4)
-    attn_stage(1, 0, 7)
-    attn_stage(1, 1, 7)
-    dense[1].stage(7)
-    dense[2].stage(7)
-    send(mlp_key, mlp_sum.at[section], mlp_sum.at[section], core, mlp_like)
-    attn_stage(0, 0, 5)
-    attn_stage(0, 1, 5)
     for k in range(1, team):
         arrived(small_key + 1 + k, small_parts.at[k])
     small_across[0] = sum([small_parts[k] for k in range(1, team)], start=small_parts[0])
@@ -746,19 +821,25 @@
     for k in range(1, teams):
         arrived(small_key + 1 + team + k, small_across.at[k])
     small_out[...] = sum([small_across[k] for k in range(1, teams)], start=small_across[0])
-    attn_stage(0, 0, 6)
-    attn_stage(0, 1, 6)
+    for q in range(chunks):
+        dense[q].stage(7)
+    send(mlp_key, mlp_sum.at[section], mlp_sum.at[section], core, mlp_like)
     arrived(mlp_key, mlp_sum.at[1 - section])
     for q in range(chunks):
         for n, dest in enumerate((mi_out, mot_out)):
-            dest[:, q * chunk : (q + 1) * chunk] = mlp_sum[n, q]
-    attn_stage(0, 0, 7)
-    attn_stage(0, 1, 7)
+            place_out = dest.at[:, q * chunk : (q + 1) * chunk]
+            last_copies.append(local(4 + 2 * q + n, mlp_sum.at[n, q], place_out))
+    attn_stage(0, 0, 3)
+    attn_stage(0, 1, 3)
+    used = 4 + 2 * chunks
     for c in range(3):
         first = c * 3 * HD
-        qkv_out[first : first + 2 * HD] = attn_sum[0, c * LANES : (c + 1) * LANES]
-        qkv_out[first + 2 * HD : first + 3 * HD] = attn_sum[1, c * HD : (c + 1) * HD]
-    attn_out[...] = attn_sum[1, 3 * HD :]
+        main_rows, rest_rows = qkv_out.at[first : first + 2 * HD], qkv_out.at[first + 2 * HD : first + 3 * HD]
+        last_copies.append(local(used + 2 * c, attn_sum.at[0, c * LANES : (c + 1) * LANES], main_rows))
+        last_copies.append(local(used + 2 * c + 1, attn_sum.at[1, c * HD : (c + 1) * HD], rest_rows))
+    last_copies.append(local(used + 6, attn_sum.at[1, 3 * HD :], attn_out))
+    for found in last_copies:
+        found.wait()
 
     for key, like in sent_off.items():
         copy(key, like, like, core).wait_send()
@@ -773,26 +854,27 @@
     _, kept = bands(window)
     chunk_count = ff // 256
     chunks = chunk_count // 2
-    vmem = pl.BlockSpec(memory_space=pltpu.VMEM)
+    vmem, hbm = pl.BlockSpec(memory_space=pltpu.VMEM), pl.BlockSpec(memory_space=pl.ANY)
     ranks = lax.axis_size("dp")
     team = min(8, ranks & -ranks)
     teams = ranks // team
     bits = [1 << n for n in range(team.bit_length() - 1)]
     spread = [bits[:1] + ["tensor"] + bits[1:], ["tensor"] + bits, bits[1::-1] + ["tensor"] + bits[2:]]
     mlp_orders = [spread[q % 3] for q in range(chunks)]
-    attn_orders = [spread[2], spread[1]]
     boxes = []
-    for order, lanes in [(order, 256) for order in mlp_orders] + [(order, width) for order in attn_orders]:
+    for order in mlp_orders:
         size = width
         for n, dim in enumerate(order):
             size = size if dim == "tensor" else size // 2
-            boxes.append(pltpu.VMEM((2 if "tensor" in order[n + 1 :] else 1, size, lanes), BF))
-        boxes.append(pltpu.VMEM((teams, size, lanes), BF))
-    stages = 2 * len(attn_orders[0])
-    copies = 15 + (chunks + 2) * (stages + teams) + 1 + 2 * (team + teams + 1)
+            boxes.append(pltpu.VMEM((2 if "tensor" in order[n + 1 :] else 1, size, 256), BF))
+        boxes.append(pltpu.VMEM((teams, size, 256), BF))
+    for _ in range(2):
+        boxes.append(pltpu.VMEM((width, width), BF))
+        boxes += [pltpu.VMEM((n, width // team, width), BF) for n in (team, teams)]
+    copies = 18 + chunks * (2 * len(mlp_orders[0]) + teams) + 2 * (1 + 2 * team + teams) + 1 + 2 * (team + teams + 1)
     return pl.pallas_call(
         functools.partial(
-            compute_kernel, team=team, teams=teams, mlp_orders=mlp_orders, attn_orders=attn_orders
+            compute_kernel, team=team, teams=teams, mlp_orders=mlp_orders
         ),
         out_shape=(
             jax.ShapeDtypeStruct((row_count, width), BF),
@@ -805,8 +887,8 @@
             jax.ShapeDtypeStruct((ff, width), BF),
             jax.ShapeDtypeStruct((8, width), F32),
         ),
-        in_specs=[vmem] * 11,
-        out_specs=[vmem] * 9,
+        in_specs=[hbm, hbm, vmem, vmem, hbm, hbm, hbm, hbm, vmem, hbm, hbm],
+        out_specs=[hbm] * 8 + [vmem],
         scratch_shapes=[
             pltpu.VMEM((window, width), BF),
             pltpu.VMEM((window, width), BF),
@@ -818,6 +900,10 @@
             pltpu.VMEM((2, width, width), BF),
             pltpu.VMEM((2, *mi.shape), BF),
             pltpu.VMEM((2, *mo.shape), BF),
+            pltpu.VMEM(ei.shape, BF),
+            pltpu.VMEM(eo.shape, BF),
+            pltpu.VMEM(ei.shape, BF),
+            pltpu.VMEM(eo.shape, BF),
             pltpu.VMEM((2, SLOTS, width), BF),
             pltpu.VMEM((window, width), BF),
             pltpu.VMEM((2, extra, width), BF),
@@ -865,6 +951,7 @@
             pltpu.VMEM((2 * IMAGES, width), BF),
             pltpu.SemaphoreType.DMA((copies,)),
             pltpu.SemaphoreType.DMA((copies,)),
+            pltpu.SemaphoreType.DMA((11 + 2 * chunks,)),
             *boxes,
         ],
         compiler_params=pltpu.CompilerParams(

time: 150 us -> 138 us (0.920)
  Pallas kernels: 149 us -> 136 us
    pallas_call x1, Pallas kernels: 142 us -> 129 us  [compute(): pl.pallas_call(functools.partial(compute_kernel, team=team, teams=teams,...]
where the time goes in v5:
time: 138 us; the launch traced here: 137 us
  Pallas kernels  136 us (99%)
    pallas_call x1, Pallas kernels, compute(): pl.pallas_call(functools.partial(compute_kernel, team=team, teams=teams,...  129 us
    pallas_call x1, Pallas kernels, finish(): pl.pallas_call(finish_kernel, grid=(steps,), out_shape=(act, pg, gains, l...  6.48 us

profile of v5, /device:TPU:0, one launch (start us, length us, event | category | flops | bytes accessed | tf_op | source)
XLA Modules:
  0.0 136.8 jit_solution(933397868785168620)
XLA Ops:
  0.6 129.5 %shard_map.186 = (bf16[512,384]{1,0:T(8,128)(2,1)}, bf16[512,384]{1,0:T(8,128)(2,1)}, bf16[576,384]{1,0:T(8,128)(2,1)}, bf16[192,384]{1,0:T(8,128)(2,1)}, bf16[3...) custom-call(bf16[512,384]{1,0:T(8,128)(2,1)} %bitcast.27, ...), custom_call_target="tpu_custom_call" | custom-call | tf_op jit(solution)/shard_map/pallas_call | solution.py:875
  130.1 6.5 %shard_map.187 = (bf16[512,384]{1,0:T(8,128)(2,1)}, bf16[512,384]{1,0:T(8,128)(2,1)}, f32[2,384]{1,0:T(2,128)}, f32[576,384]{1,0:T(8,128)}, f32[192,384]{1,0:T(8...) custom-call(bf16[512,384]{1,0:T(8,128)(2,1)} %get-tuple-element.29.a, ...), custom_call_target="tpu_custom_call" | custom-call | tf_op jit(solution)/shard_map/pallas_call | solution.py:994

commit v6 on v5

--- a/solution.py
+++ b/solution.py
@@ -79,7 +79,7 @@
     act_out, pg_out, qkv_out, attn_out, mi_out, mot_out, expert_in_out, expert_out_out, small_out,
     xw, cw, gains, wy, wc, w_own, wqkv, wo, mi, mo, ei, eo, expert_in_sum, expert_out_sum, routert, act, edge_in, slots, geos, slot_in, pack,
     z, x1, sent, x3, qt, kt, vt, kr, vr, ot, pt, tok, hidden, slope, gx, low, got, gt, gtok, gk_sum, gv_sum,
-    bias, own, mixing, eslope, eout, gslot, grad_attn, attn_sum, grad_mlp, mlp_core, mlp_sum,
+    gz_all, veil, shares, own, mixing, eslope, eout, gslot, grad_attn, attn_sum, grad_mlp, mlp_core, mlp_sum,
     small, small_in, small_parts, small_across, packs, small_pack, send_sem, recv_sem, here_sem,
     *boxes, team, teams, mlp_orders,
 ):
@@ -181,13 +181,15 @@
     qkv_near, out_near = wc.at[0, :qkv_rows], wc.at[0, qkv_rows:]
     qkv_far, out_far = wc.at[1, :qkv_rows], wc.at[1, qkv_rows:]
 
+    edge = x_own.at[at((1 - tensor) * (row_count - extra), extra)]
+    send(0, edge, xw.at[at(tensor * row_count, extra)], beside)
+
     @only(0)
     def _():
         send(3, qkv_own, qkv_here, beside)
         send(15, out_own, out_here, beside)
-
-    edge = x_own.at[at((1 - tensor) * (row_count - extra), extra)]
-    send(0, edge, xw.at[at(tensor * row_count, extra)], beside)
+        send(5, mi_own, mi.at[tensor], beside)
+
     send(1, gains.at[section], gains.at[section], core)
     send(2, qkv_own, qkv_near, core)
     send(16, out_own, out_near, core)
@@ -203,17 +205,22 @@
     member_own = member * mine
     own_row = jnp.sum(member_own, axis=0, keepdims=True)
     own[...] = jnp.broadcast_to(own_row, (LANES, window)).T
-    ids_col = jnp.broadcast_to(window_ids, (LANES, window)).T
-    for q0, k0, count, kept in blocks:
-        same = ids_col[k0 : k0 + count] == jnp.broadcast_to(window_ids[:, q0 : q0 + LANES], (count, LANES))
-        bias[kept : kept + count, :] = jnp.where(same, 0.0, -1e30)
+    blank = jnp.zeros((LANES - SLOTS, window), F32)
+    image_of = jnp.concatenate([member, blank], axis=0).T.astype(BF)
+    for b in range(2):
+        for j in range(pairs):
+            kr[b, j, :, LANES:] = image_of
+    veil[...] = jnp.concatenate([(1.0 - member) * -1e30, blank], axis=0).astype(BF)
 
     def place(source, b, t, kinds=(0, 1, 2, 3)):
         for c in kinds:
-            dest, base = (wqkv, c * width) if c < 3 else (wo, 0)
             first = c * 3 * HD
-            dest[b, at(base + t * LANES, 2 * HD)] = source[first : first + 2 * HD]
-            dest[b, at(base + 2 * LANES + t * HD, HD, HD)] = source[first + 2 * HD : first + 3 * HD]
+            if c < 3:
+                own_pair, mixed_pair, dest = t * width + c * LANES, 2 * width + c * LANES + t * HD, wqkv
+            else:
+                own_pair, mixed_pair, dest = t * LANES, 2 * LANES + t * HD, wo
+            dest[b, at(own_pair, 2 * HD)] = source[first : first + 2 * HD]
+            dest[b, at(mixed_pair, HD, HD)] = source[first + 2 * HD : first + 3 * HD]
 
     for found in near_copies:
         found.wait()
@@ -224,18 +231,31 @@
     place(wc.at[0], 1 - section, tensor)
     arrived(0, xw.at[at((1 - tensor) * row_count, extra)])
 
-    @only(0)
-    def _():
-        arrived(3, qkv_here)
-        send(4, qkv_here, qkv_far, core)
-        send(5, mi_own, mi.at[tensor], beside)
-        place(wy, 0, 1 - tensor, (0, 1, 2))
-
-    @only(1)
-    def _():
-        arrived(4, qkv_far)
-        send(5, mo_own, mo.at[tensor], beside)
-        place(wc.at[1], 0, 1 - tensor, (0, 1, 2))
+
+    def first_far():
+        @only(0)
+        def _():
+            arrived(3, qkv_here)
+            send(4, qkv_here, qkv_far, core)
+            place(wy, 0, 1 - tensor, (0, 1, 2))
+
+        @only(1)
+        def _():
+            arrived(4, qkv_far)
+            send(5, mo_own, mo.at[tensor], beside)
+            place(wc.at[1], 0, 1 - tensor, (0, 1, 2))
+
+    def second_far():
+        @only(0)
+        def _():
+            arrived(4, qkv_far)
+            place(wc.at[1], 1, 1 - tensor, (0, 1, 2))
+
+        @only(1)
+        def _():
+            arrived(3, qkv_here)
+            send(4, qkv_here, qkv_far, core)
+            place(wy, 1, 1 - tensor, (0, 1, 2))
 
     def first_out():
         @only(0)
@@ -405,8 +425,8 @@
         heard = wc.at[:, n * width : (n + 1) * width]
         attn.append(Straight(key, attn_pick(n), heard, attn_sum.at[n], boxes_of(3)))
         key += Straight.keys
-    mlp_key, pack_key, small_key = key, key + 1, key + 1 + team + teams
-    mlp_like = mlp_sum.at[0]
+    mlp_key, pack_key, small_key = key, key + chunks, key + chunks + team + teams
+    mlp_like = mlp_sum.at[0, 0]
 
     def give_attn(b, n):
         @only(1 - b)
@@ -421,31 +441,36 @@
     def give_dense(q):
         dense[q].to_core(grad_mlp.at[1 - section, :, q])
 
-    def attention(b, x_of, out_ref, ahead_of_out):
+    def attention(b, x_of, out_ref, ahead_of_far, ahead_of_out):
         def norm(i):
             unit, _ = normalise(x_of(rows(i)))
             z[2 * b, rows(i)] = (unit * gains[b, 0:1, :]).astype(BF)
 
         loop(row_blocks, norm)
-        zz = z[2 * b]
-        for c, dest in enumerate((qt.at[b], kt.at[b], vt)):
-            tall = dot_t(wqkv[b, c * width : (c + 1) * width], zz)
-            tall = (tall.astype(BF) * jnp.asarray(HD**-0.5 if c == 0 else 1.0, BF)).reshape(pairs, LANES, window)
-            dest[...] = tall
-        for c, dest in ((1, kr), (2, vr)):
-            flat = dot_t(zz, wqkv[b, c * width : (c + 1) * width]).astype(BF)
-            for j in range(pairs):
-                dest[b, j] = flat[:, j * LANES : (j + 1) * LANES]
-
-        def pair(j):
+
+        def pair(n):
+            pl.when(n == 1)(ahead_of_far)
+            j = jnp.where(n == 0, tensor, jnp.where(n == 1, 1 - tensor, n))
+            zz, weights = z[2 * b], wqkv.at[b, at(j * width, width)]
+            flat = dot_t(zz, weights[...])
+            qt[b, j] = (flat[:, :LANES] * HD**-0.5).astype(BF).T
+            keys, values = flat[:, LANES : 2 * LANES].astype(BF), flat[:, 2 * LANES :].astype(BF)
+            kr[b, j, :, :LANES] = keys
+            vr[b, j] = values
+            kt[b, j] = keys.T
+            vt[...] = values.T
             for q0, k0, count, kept in blocks:
-                scores = dot(kr[b, j, k0 : k0 + count, :], pair_up(qt[b, j, :, q0 : q0 + LANES]))
-                veil = bias[kept : kept + count, :]
-                scores = scores + jnp.concatenate([veil, veil], axis=1)
+                queries = pair_up(qt[b, j, :, q0 : q0 + LANES])
+                hidden_part = veil[:, q0 : q0 + LANES]
+                queries = jnp.concatenate([queries, jnp.concatenate([hidden_part, hidden_part], axis=1)], axis=0)
+                scores = dot(kr[b, j, k0 : k0 + count, :], queries)
                 powers = jnp.exp(scores - jnp.max(scores, axis=0, keepdims=True))
-                probs = (powers * (1.0 / jnp.sum(powers, axis=0, keepdims=True))).astype(BF)
-                pt[b, j, kept : kept + count, :] = probs
-                ot[b, j, :, q0 : q0 + LANES] = pair_down(dot(vt[j, :, k0 : k0 + count], probs)).astype(BF)
+                inverse = 1.0 / jnp.sum(powers, axis=0, keepdims=True)
+                low_powers = powers.astype(BF)
+                pt[b, j, kept : kept + count, :] = low_powers
+                shares[b, j, q0 // LANES : q0 // LANES + 1, :] = inverse
+                mixed = dot(vt[:, k0 : k0 + count], low_powers) * inverse
+                ot[b, j, :, q0 : q0 + LANES] = pair_down(mixed).astype(BF)
 
         loop(pairs, pair)
         for j in range(pairs):
@@ -453,57 +478,51 @@
 
         ahead_of_out()
 
-        def out(i):
-            out_ref[rows(i, half)] = x_of(rows(i, half)) + dot(tok[rows(i, half)], wo[b])
-
-        loop(2, out)
+        out_ref[...] = x_of(slice(None)) + dot(tok[...], wo[b])
 
     def attention_back(b, x_of, beside_pairs, after_pairs):
         ga = low[...]
         got[...] = dot_t(wo[b], ga).astype(BF).reshape(pairs, LANES, window)
-        for j in range(pairs):
-            piece = dot(ot[b, j], ga).astype(BF)
-            if j < 2:
-                grad_attn[b, j, 1, 3 * HD : 5 * HD, :] = piece
-            else:
-                for t in range(2):
-                    grad_attn[b, t, 1, 5 * HD : 6 * HD, :] = piece[t * HD : (t + 1) * HD]
-        zz = z[2 * b]
-
+        pieces = dot(ot[b].reshape(width, window), ga).astype(BF)
+        for t in range(2):
+            grad_attn[b, t, 1, 3 * HD : 5 * HD, :] = pieces[t * LANES : (t + 1) * LANES]
+            grad_attn[b, t, 1, 5 * HD : 6 * HD, :] = pieces[2 * LANES + t * HD : 2 * LANES + (t + 1) * HD]
         def pair(j):
-            for at_pair, body in enumerate(beside_pairs):
-                pl.when(j == at_pair)(body)
             gk_sum[...] = jnp.zeros_like(gk_sum)
             gv_sum[...] = jnp.zeros_like(gv_sum)
             for q0, k0, count, kept in blocks:
-                go_pair = pair_up(got[j, :, q0 : q0 + LANES])
+                for (at_pair, at_query), body in beside_pairs.items():
+                    if at_query == q0 // LANES:
+                        pl.when(j == at_pair)(body)
+                inverse = shares[b, j, q0 // LANES : q0 // LANES + 1, :]
+                go_pair = (pair_up(got[j, :, q0 : q0 + LANES]).astype(F32) * inverse).astype(BF)
                 q_pair = pair_up(qt[b, j, :, q0 : q0 + LANES])
-                low_probs = pt[b, j, kept : kept + count, :]
-                probs = low_probs.astype(F32)
-                weighted = dot(vr[b, j, k0 : k0 + count, :], go_pair) * probs
-                inner = jnp.sum(weighted, axis=0, keepdims=True)
-                gs = (weighted - probs * inner).astype(BF)
+                low_powers = pt[b, j, kept : kept + count, :]
+                powers = low_powers.astype(F32)
+                weighted = dot(vr[b, j, k0 : k0 + count, :], go_pair) * powers
+                inner = jnp.sum(weighted, axis=0, keepdims=True) * inverse
+                gs = (weighted - powers * inner).astype(BF)
                 gq = pair_down(dot(kt[b, j, :, k0 : k0 + count], gs)) * HD**-0.5
                 gt[:LANES, q0 : q0 + LANES] = gq.astype(BF)
                 gk_sum[k0 : k0 + count] += dot_t(gs, q_pair)
-                gv_sum[k0 : k0 + count] += dot_t(low_probs, go_pair)
-            gtok[j] = gt[:LANES].T
+                gv_sum[k0 : k0 + count] += dot_t(low_powers, go_pair)
+            gtok[3 * j] = gt[:LANES].T
             for c, total_of in ((1, gk_sum), (2, gv_sum)):
                 low_sum = total_of[...].astype(BF)
-                gtok[c * pairs + j] = low_sum
+                gtok[3 * j + c] = low_sum
                 gt[c * LANES : (c + 1) * LANES] = low_sum.T
-            pieces = [dot(gt[c * LANES : (c + 1) * LANES], zz).astype(BF) for c in range(3)]
+            pieces = dot(gt[...], z[2 * b]).astype(BF)
 
             @pl.when(j < 2)
             def _():
-                for c in range(3):
-                    grad_attn[b, j, 0, c * LANES : (c + 1) * LANES, :] = pieces[c]
+                grad_attn[b, j, 0] = pieces
 
             @pl.when(j == 2)
             def _():
                 for c in range(3):
                     for t in range(2):
-                        grad_attn[b, t, 1, c * HD : (c + 1) * HD, :] = pieces[c][t * HD : (t + 1) * HD]
+                        first = c * LANES + t * HD
+                        grad_attn[b, t, 1, c * HD : (c + 1) * HD, :] = pieces[first : first + HD]
 
         loop(pairs, pair)
         after_pairs()
@@ -517,7 +536,7 @@
 
         small[2 * b : 2 * b + 1, :] = lax.fori_loop(0, 2, back, jnp.zeros((1, width), F32))
 
-    attention(0, lambda r: xw[r].astype(F32), x1, first_out)
+    attention(0, lambda r: xw[r].astype(F32), x1, first_far, first_out)
 
     def norm_middle(source, which):
         def body(i):
@@ -531,50 +550,42 @@
     for found in later_copies:
         found.wait()
 
+    def far_hidden():
+        @only(0)
+        def _():
+            arrived(5, mi.at[1 - tensor])
+            send(6, mi.at[1 - tensor], mi.at[1 - tensor], core, mi_own)
+
+        @only(1)
+        def _():
+            arrived(5, mo.at[1 - tensor])
+            send(6, mo.at[1 - tensor], mo.at[1 - tensor], core, mo_own)
+            arrived(6, mi.at[1 - tensor])
+
+    chunk = 256
+
+    def hidden_chunk(n):
+        pl.when(n == chunks)(far_hidden)
+        q = lax.rem(n, chunks)
+        part, first = jnp.where(n < chunks, tensor, 1 - tensor), pl.multiple_of(q * chunk, chunk)
+        value, grad = gelu_parts(dot(z[1], mi[part, :, pl.ds(first, chunk)]))
+        hidden[part * chunks + q] = value.astype(BF)
+        slope[part * chunks + q] = grad.astype(BF)
+
+    loop(2 * chunks, hidden_chunk)
+
     @only(0)
     def _():
-        arrived(5, mi.at[1 - tensor])
-        send(6, mi.at[1 - tensor], mi.at[1 - tensor], core, mi_own)
         arrived(6, mo.at[1 - tensor])
 
-    @only(1)
-    def _():
-        arrived(5, mo.at[1 - tensor])
-        send(6, mo.at[1 - tensor], mo.at[1 - tensor], core, mo_own)
-        arrived(6, mi.at[1 - tensor])
-
-    chunk = 256
-
-    def hidden_chunk(i):
-        part, first = i // chunks, pl.multiple_of(i % chunks * chunk, chunk)
-        value, grad = gelu_parts(dot(z[1], mi[part, :, pl.ds(first, chunk)]))
-        hidden[i] = value.astype(BF)
-        slope[i] = grad.astype(BF)
-
-    loop(2 * chunks, hidden_chunk)
-
-    def dense_out(i):
-        h = jnp.concatenate([hidden[c, rows(i, half)] for c in range(2 * chunks)], axis=1)
-        sent[rows(i, half)] = (x1[rows(i, half)] + dot(h, mo[...].reshape(-1, width))).astype(BF)
-
-    loop(2, dense_out)
-
-    @only(0)
-    def _():
-        arrived(4, qkv_far)
-        place(wc.at[1], 1, 1 - tensor, (0, 1, 2))
-
-    @only(1)
-    def _():
-        arrived(3, qkv_here)
-        send(4, qkv_here, qkv_far, core)
-        place(wy, 1, 1 - tensor, (0, 1, 2))
+    h = jnp.concatenate([hidden[c] for c in range(2 * chunks)], axis=1)
+    sent[...] = (x1[...] + dot(h, mo[...].reshape(-1, width))).astype(BF)
 
     c_edge = c_own.at[at((1 - tensor) * (row_count - extra), extra)]
     send(7, c_edge, cw.at[at(tensor * row_count, extra)], beside)
     send(8, routert.at[tensor], routert.at[tensor], beside)
 
-    attention(1, lambda r: sent[r].astype(F32), x3, second_out)
+    attention(1, lambda r: sent[r].astype(F32), x3, second_far, second_out)
     norm_middle(x3, 3)
     z3 = z[3]
     arrived(8, routert.at[1 - tensor])
@@ -622,9 +633,6 @@
 
     loop(row_blocks, finish)
     send(13, act.at[at((1 - tensor) * row_count, extra)], edge_in.at[0], beside)
-
-    def nothing():
-        pass
 
     all_packs, team_like = packs.at[0], packs.at[0, 0]
 
@@ -684,7 +692,7 @@
         give_attn(1, 0)
 
     share_slots()
-    attention_back(1, lambda r: sent[r].astype(F32), [nothing, nothing, shares_second], lambda: give_attn(1, 1))
+    attention_back(1, lambda r: sent[r].astype(F32), {(2, 0): shares_second}, lambda: give_attn(1, 1))
 
     low[...] = gx[...].astype(BF)
     gsent = low[...]
@@ -710,10 +718,11 @@
     def dense_second():
         give_dense(1)
         attn_stage(1, 1, 0)
+        dense[0].stage(0)
 
     loop(2 * chunks, hidden_back)
     give_dense(2)
-    dense[0].stage(0)
+    dense[1].stage(0)
 
     def dense_back(i, gain_grad):
         gz = jnp.zeros((half, width), F32)
@@ -728,39 +737,41 @@
 
     small[1:2, :] = lax.fori_loop(0, 2, dense_back, jnp.zeros((1, width), F32))
 
+    dense[2].stage(0)
+    attn_stage(1, 0, 1)
+
     def beside_first():
-        dense[1].stage(0)
-        attn_stage(1, 0, 1)
-
-    def beside_second():
-        dense[2].stage(0)
         dense[0].stage(1)
         attn_stage(1, 1, 1)
 
     def beside_third():
         give_attn(0, 0)
-        dense[1].stage(1)
         attn_stage(1, 0, 2)
+        dense[0].stage(2)
+
+    def beside_last():
+        dense[1].stage(2)
+        attn_stage(0, 0, 0)
 
     def beside_rest():
         give_attn(0, 1)
-        attn_stage(0, 0, 0)
-        dense[2].stage(1)
-        dense[0].stage(2)
         attn_stage(1, 1, 2)
-
-    attention_back(0, lambda r: xw[r].astype(F32), [beside_first, beside_second, beside_third], beside_rest)
+        dense[2].stage(2)
+        dense[0].stage(3)
+
+    beside_pairs = {
+        (0, 3): beside_first,
+        (1, 0): lambda: dense[1].stage(1),
+        (1, 3): lambda: dense[2].stage(1),
+        (2, 0): beside_third,
+        (2, 3): beside_last,
+    }
+    attention_back(0, lambda r: xw[r].astype(F32), beside_pairs, beside_rest)
     low[...] = gx[...].astype(BF)
     send(14, low.at[at((1 - tensor) * row_count, extra)], edge_in.at[1], beside)
     send(small_key, small, small_in.at[0], core)
     attn_stage(0, 1, 0)
-    dense[1].stage(2)
-    dense[2].stage(2)
-    arrived(small_key, small_in.at[0])
-    small_in[1] = small[...] + small_in[0]
-    send(small_key + 1, small_in.at[1], small_in.at[2], beside)
-    attn_stage(0, 0, 1)
-    dense[0].stage(3)
+    dense[1].stage(3)
 
     arrived(pack_key, packs.at[1])
     split_packs = packs[...].astype(F32).reshape(-1, 2, IMAGES, width)
@@ -779,27 +790,26 @@
         expert_out_sum[lanes, :] = dot(value.astype(BF).T, every_grad).astype(BF)
 
     def beside_experts_first():
-        attn_stage(0, 1, 1)
-        dense[1].stage(3)
+        attn_stage(0, 0, 1)
+        dense[0].stage(4)
         dense[2].stage(3)
+        arrived(small_key, small_in.at[0])
+        small_in[1] = small[...] + small_in[0]
+        send(small_key + 1, small_in.at[1], small_in.at[2], beside, small)
 
     def beside_experts_second():
-        dense[0].stage(4)
-        attn_stage(0, 0, 2)
         dense[1].stage(4)
 
     loop(expert_steps, expert_grads)
 
     last_copies = [local(0, expert_in_sum, expert_in_out), local(1, expert_out_sum, expert_out_out)]
+    attn_stage(0, 1, 1)
     arrived(small_key + 1, small_in.at[2])
     small_parts[0] = small_in[1] + small_in[2]
     for k in range(1, team):
         send(small_key + 1 + k, small_parts.at[0], small_parts.at[k], mate(k)[0])
+    dense[0].stage(5)
     dense[2].stage(4)
-    dense[0].stage(5)
-    attn_stage(0, 1, 2)
-    dense[1].stage(5)
-    dense[2].stage(5)
 
     for n, (source, dest) in enumerate(((act, act_out), (low, pg_out))):
         arrived(13 + n, edge_in.at[n])
@@ -810,9 +820,10 @@
 
     attn_stage(1, 0, 3)
     attn_stage(1, 1, 3)
+    dense[1].stage(5)
     dense[0].stage(6)
-    dense[1].stage(6)
-    dense[2].stage(6)
+    attn_stage(0, 0, 2)
+    dense[2].stage(5)
     for k in range(1, team):
         arrived(small_key + 1 + k, small_parts.at[k])
     small_across[0] = sum([small_parts[k] for k in range(1, team)], start=small_parts[0])
@@ -821,22 +832,32 @@
     for k in range(1, teams):
         arrived(small_key + 1 + team + k, small_across.at[k])
     small_out[...] = sum([small_across[k] for k in range(1, teams)], start=small_across[0])
+    dense[1].stage(6)
+
+    def pass_dense(q):
+        dense[q].stage(7)
+        done = mlp_sum.at[section, q]
+        send(mlp_key + q, done, done, core, mlp_like)
+
+    dense[2].stage(6)
+    attn_stage(0, 1, 2)
+    pass_dense(0)
+    pass_dense(1)
+    pass_dense(2)
     for q in range(chunks):
-        dense[q].stage(7)
-    send(mlp_key, mlp_sum.at[section], mlp_sum.at[section], core, mlp_like)
-    arrived(mlp_key, mlp_sum.at[1 - section])
-    for q in range(chunks):
+        arrived(mlp_key + q, mlp_sum.at[1 - section, q])
         for n, dest in enumerate((mi_out, mot_out)):
             place_out = dest.at[:, q * chunk : (q + 1) * chunk]
             last_copies.append(local(4 + 2 * q + n, mlp_sum.at[n, q], place_out))
     attn_stage(0, 0, 3)
-    attn_stage(0, 1, 3)
     used = 4 + 2 * chunks
     for c in range(3):
-        first = c * 3 * HD
-        main_rows, rest_rows = qkv_out.at[first : first + 2 * HD], qkv_out.at[first + 2 * HD : first + 3 * HD]
-        last_copies.append(local(used + 2 * c, attn_sum.at[0, c * LANES : (c + 1) * LANES], main_rows))
-        last_copies.append(local(used + 2 * c + 1, attn_sum.at[1, c * HD : (c + 1) * HD], rest_rows))
+        place_out = qkv_out.at[c * 3 * HD : c * 3 * HD + 2 * HD]
+        last_copies.append(local(used + c, attn_sum.at[0, c * LANES : (c + 1) * LANES], place_out))
+    attn_stage(0, 1, 3)
+    for c in range(3):
+        place_out = qkv_out.at[c * 3 * HD + 2 * HD : (c + 1) * 3 * HD]
+        last_copies.append(local(used + 3 + c, attn_sum.at[1, c * HD : (c + 1) * HD], place_out))
     last_copies.append(local(used + 6, attn_sum.at[1, 3 * HD :], attn_out))
     for found in last_copies:
         found.wait()
@@ -871,7 +892,7 @@
     for _ in range(2):
         boxes.append(pltpu.VMEM((width, width), BF))
         boxes += [pltpu.VMEM((n, width // team, width), BF) for n in (team, teams)]
-    copies = 18 + chunks * (2 * len(mlp_orders[0]) + teams) + 2 * (1 + 2 * team + teams) + 1 + 2 * (team + teams + 1)
+    copies = 18 + chunks * (2 * len(mlp_orders[0]) + teams) + 2 * (1 + 2 * team + teams) + chunks + 2 * (team + teams + 1)
     return pl.pallas_call(
         functools.partial(
             compute_kernel, team=team, teams=teams, mlp_orders=mlp_orders
@@ -917,8 +938,8 @@
             pltpu.VMEM((window, width), F32),
             pltpu.VMEM((2, pairs, LANES, window), BF),
             pltpu.VMEM((2, pairs, LANES, window), BF),
-            pltpu.VMEM((pairs, LANES, window), BF),
-            pltpu.VMEM((2, pairs, window, LANES), BF),
+            pltpu.VMEM((LANES, window), BF),
+            pltpu.VMEM((2, pairs, window, 2 * LANES), BF),
             pltpu.VMEM((2, pairs, window, LANES), BF),
             pltpu.VMEM((2, pairs, LANES, window), BF),
             pltpu.VMEM((2, pairs, kept, 2 * LANES), BF),
@@ -932,7 +953,9 @@
             pltpu.VMEM((3 * pairs, window, LANES), BF),
             pltpu.VMEM((window, LANES), F32),
             pltpu.VMEM((window, LANES), F32),
-            pltpu.VMEM((kept, LANES), F32),
+            pltpu.VMEM((window, width), F32),
+            pltpu.VMEM((LANES, window), BF),
+            pltpu.VMEM((2, pairs, 8, 2 * LANES), F32),
             pltpu.VMEM((window, LANES), F32),
             pltpu.VMEM((2, 2 * SLOTS, window), BF),
             pltpu.VMEM((SLOTS, ff), F32),

time: 138 us -> 129 us (0.935)
  Pallas kernels: 136 us -> 128 us
    pallas_call x1, Pallas kernels: 129 us -> 122 us  [compute(): pl.pallas_call(functools.partial(compute_kernel, team=team, teams=teams,...]
where the time goes in v6:
time: 129 us
  Pallas kernels  128 us (99%)
    pallas_call x1, Pallas kernels, compute(): pl.pallas_call(functools.partial(compute_kernel, team=team, teams=teams,...  122 us
    pallas_call x1, Pallas kernels, finish(): pl.pallas_call(finish_kernel, grid=(steps,), out_shape=(act, pg, gains, l...  6.48 us

profile of v6, /device:TPU:0, one launch (start us, length us, event | category | flops | bytes accessed | tf_op | source)
XLA Modules:
  0.0 129.0 jit_solution(14917300291418134657)
XLA Ops:
  0.6 121.7 %shard_map.186 = (bf16[512,384]{1,0:T(8,128)(2,1)}, bf16[512,384]{1,0:T(8,128)(2,1)}, bf16[576,384]{1,0:T(8,128)(2,1)}, bf16[192,384]{1,0:T(8,128)(2,1)}, bf16[3...) custom-call(bf16[512,384]{1,0:T(8,128)(2,1)} %bitcast.27, ...), custom_call_target="tpu_custom_call" | custom-call | tf_op jit(solution)/shard_map/pallas_call | solution.py:896
  122.3 6.5 %shard_map.187 = (bf16[512,384]{1,0:T(8,128)(2,1)}, bf16[512,384]{1,0:T(8,128)(2,1)}, f32[2,384]{1,0:T(2,128)}, f32[576,384]{1,0:T(8,128)}, f32[192,384]{1,0:T(8...) custom-call(bf16[512,384]{1,0:T(8,128)(2,1)} %get-tuple-element.29.a, ...), custom_call_target="tpu_custom_call" | custom-call | tf_op jit(solution)/shard_map/pallas_call | solution.py:1017

commit v7 on v6

--- a/solution.py
+++ b/solution.py
@@ -81,7 +81,7 @@
     z, x1, sent, x3, qt, kt, vt, kr, vr, ot, pt, tok, hidden, slope, gx, low, got, gt, gtok, gk_sum, gv_sum,
     gz_all, veil, shares, own, mixing, eslope, eout, gslot, grad_attn, attn_sum, grad_mlp, mlp_core, mlp_sum,
     small, small_in, small_parts, small_across, packs, small_pack, send_sem, recv_sem, here_sem,
-    *boxes, team, teams, mlp_orders,
+    *boxes, team, teams, mlp_orders, attn_orders,
 ):
     row_count, width = x_own.shape
     window = xw.shape[0]
@@ -125,7 +125,7 @@
 
         lax.fori_loop(0, n, step, 0)
 
-    sent_off = {}
+    sent_off, sent_by, within = {}, {}, (0, 1)
 
     def copy(key, source, dest, device):
         return pltpu.make_async_remote_copy(
@@ -140,12 +140,33 @@
     def send(key, source, dest, device, like=None):
         copy(key, source, dest, device).start()
         sent_off[key] = source if like is None else like
+        sent_by.setdefault(key, set()).update(within)
+
+    def settle(last=False):
+        for key in list(sent_off):
+            like = sent_off[key]
+            if len(sent_by[key]) == 2:
+                copy(key, like, like, core).wait_send()
+            elif last:
+                only(*sent_by[key])(lambda key=key, like=like: copy(key, like, like, core).wait_send())
+            else:
+                continue
+            sent_off.pop(key)
 
     def arrived(key, dest):
         copy(key, dest, dest, core).wait_recv()
 
     def only(which):
-        return pl.when(section == which)
+        def run(body):
+            def marked():
+                nonlocal within
+                within = (which,)
+                body()
+                within = (0, 1)
+
+            pl.when(section == which)(marked)
+
+        return run
 
     barrier = pltpu.get_barrier_semaphore()
     neighbours = [core, beside] + [mate(k)[0] for k in range(1, team)] + [partner(k) for k in range(1, teams)]
@@ -242,8 +263,12 @@
         @only(1)
         def _():
             arrived(4, qkv_far)
+            place(wc.at[1], 0, 1 - tensor, (0, 1, 2))
+
+    def send_dense():
+        @only(1)
+        def _():
             send(5, mo_own, mo.at[tensor], beside)
-            place(wc.at[1], 0, 1 - tensor, (0, 1, 2))
 
     def second_far():
         @only(0)
@@ -267,8 +292,6 @@
         @only(1)
         def _():
             arrived(17, out_far)
-            send(3, qkv_own, qkv_here, beside)
-            send(15, out_own, out_here, beside)
             place(wc.at[1], 0, 1 - tensor, (3,))
 
     def second_out():
@@ -421,9 +444,14 @@
         found = boxes_of(len(mlp_orders[q]) + 1)
         dense.append(Cube(key, mlp_pick(q), mlp_core.at[q], total_of, mlp_orders[q], found))
         key += Cube.keys
+    attn = {}
+    for n in range(2):
+        heard, found = wc.at[:, n * width : (n + 1) * width], boxes_of(len(attn_orders[n]) + 1)
+        attn[1, n] = Cube(key, attn_pick(n), heard, attn_sum.at[n], attn_orders[n], found)
+        key += Cube.keys
     for n in range(2):
         heard = wc.at[:, n * width : (n + 1) * width]
-        attn.append(Straight(key, attn_pick(n), heard, attn_sum.at[n], boxes_of(3)))
+        attn[0, n] = Straight(key, attn_pick(n), heard, attn_sum.at[n], boxes_of(3))
         key += Straight.keys
     mlp_key, pack_key, small_key = key, key + chunks, key + chunks + team + teams
     mlp_like = mlp_sum.at[0, 0]
@@ -431,12 +459,12 @@
     def give_attn(b, n):
         @only(1 - b)
         def _():
-            attn[n].to_core(grad_attn.at[b, :, n])
+            attn[b, n].to_core(grad_attn.at[b, :, n])
 
     def attn_stage(b, n, k):
         @only(b)
         def _():
-            attn[n].stage(k)
+            attn[b, n].stage(k)
 
     def give_dense(q):
         dense[q].to_core(grad_mlp.at[1 - section, :, q])
@@ -450,6 +478,8 @@
 
         def pair(n):
             pl.when(n == 1)(ahead_of_far)
+            if b == 0:
+                pl.when(n == 2)(send_dense)
             j = jnp.where(n == 0, tensor, jnp.where(n == 1, 1 - tensor, n))
             zz, weights = z[2 * b], wqkv.at[b, at(j * width, width)]
             flat = dot_t(zz, weights[...])
@@ -558,6 +588,8 @@
 
         @only(1)
         def _():
+            send(3, qkv_own, qkv_here, beside)
+            send(15, out_own, out_here, beside)
             arrived(5, mo.at[1 - tensor])
             send(6, mo.at[1 - tensor], mo.at[1 - tensor], core, mo_own)
             arrived(6, mi.at[1 - tensor])
@@ -744,25 +776,34 @@
         dense[0].stage(1)
         attn_stage(1, 1, 1)
 
+    def beside_second():
+        dense[1].stage(1)
+        attn_stage(1, 0, 2)
+
+    def beside_middle():
+        dense[2].stage(1)
+        attn_stage(1, 1, 2)
+
     def beside_third():
         give_attn(0, 0)
-        attn_stage(1, 0, 2)
+        attn_stage(1, 0, 3)
         dense[0].stage(2)
 
     def beside_last():
         dense[1].stage(2)
+        attn_stage(1, 1, 3)
         attn_stage(0, 0, 0)
 
     def beside_rest():
         give_attn(0, 1)
-        attn_stage(1, 1, 2)
+        attn_stage(1, 0, 4)
         dense[2].stage(2)
         dense[0].stage(3)
 
     beside_pairs = {
         (0, 3): beside_first,
-        (1, 0): lambda: dense[1].stage(1),
-        (1, 3): lambda: dense[2].stage(1),
+        (1, 0): beside_second,
+        (1, 3): beside_middle,
         (2, 0): beside_third,
         (2, 3): beside_last,
     }
@@ -771,6 +812,7 @@
     send(14, low.at[at((1 - tensor) * row_count, extra)], edge_in.at[1], beside)
     send(small_key, small, small_in.at[0], core)
     attn_stage(0, 1, 0)
+    attn_stage(1, 1, 4)
     dense[1].stage(3)
 
     arrived(pack_key, packs.at[1])
@@ -791,6 +833,7 @@
 
     def beside_experts_first():
         attn_stage(0, 0, 1)
+        attn_stage(1, 0, 5)
         dense[0].stage(4)
         dense[2].stage(3)
         arrived(small_key, small_in.at[0])
@@ -798,12 +841,14 @@
         send(small_key + 1, small_in.at[1], small_in.at[2], beside, small)
 
     def beside_experts_second():
+        attn_stage(1, 1, 5)
         dense[1].stage(4)
 
     loop(expert_steps, expert_grads)
 
     last_copies = [local(0, expert_in_sum, expert_in_out), local(1, expert_out_sum, expert_out_out)]
     attn_stage(0, 1, 1)
+    attn_stage(1, 0, 6)
     arrived(small_key + 1, small_in.at[2])
     small_parts[0] = small_in[1] + small_in[2]
     for k in range(1, team):
@@ -818,10 +863,10 @@
         source[near] = jnp.where(wide > 0.0, source[near].astype(F32), edge_in[n].astype(F32)).astype(BF)
         last_copies.append(local(2 + n, source.at[own_rows], dest))
 
-    attn_stage(1, 0, 3)
-    attn_stage(1, 1, 3)
+    attn_stage(1, 1, 6)
     dense[1].stage(5)
     dense[0].stage(6)
+    attn_stage(1, 0, 7)
     attn_stage(0, 0, 2)
     dense[2].stage(5)
     for k in range(1, team):
@@ -841,6 +886,7 @@
 
     dense[2].stage(6)
     attn_stage(0, 1, 2)
+    attn_stage(1, 1, 7)
     pass_dense(0)
     pass_dense(1)
     pass_dense(2)
@@ -854,6 +900,7 @@
     for c in range(3):
         place_out = qkv_out.at[c * 3 * HD : c * 3 * HD + 2 * HD]
         last_copies.append(local(used + c, attn_sum.at[0, c * LANES : (c + 1) * LANES], place_out))
+    settle()
     attn_stage(0, 1, 3)
     for c in range(3):
         place_out = qkv_out.at[c * 3 * HD + 2 * HD : (c + 1) * 3 * HD]
@@ -862,8 +909,7 @@
     for found in last_copies:
         found.wait()
 
-    for key, like in sent_off.items():
-        copy(key, like, like, core).wait_send()
+    settle(True)
 
 
 def compute(x_own, c_own, ids, gains, qkv, out, mi, mo, router, ei, eo):
@@ -882,20 +928,21 @@
     bits = [1 << n for n in range(team.bit_length() - 1)]
     spread = [bits[:1] + ["tensor"] + bits[1:], ["tensor"] + bits, bits[1::-1] + ["tensor"] + bits[2:]]
     mlp_orders = [spread[q % 3] for q in range(chunks)]
+    attn_orders = [spread[2], spread[1]]
     boxes = []
-    for order in mlp_orders:
+    for order, lanes in [(order, 256) for order in mlp_orders] + [(order, width) for order in attn_orders]:
         size = width
         for n, dim in enumerate(order):
             size = size if dim == "tensor" else size // 2
-            boxes.append(pltpu.VMEM((2 if "tensor" in order[n + 1 :] else 1, size, 256), BF))
-        boxes.append(pltpu.VMEM((teams, size, 256), BF))
+            boxes.append(pltpu.VMEM((2 if "tensor" in order[n + 1 :] else 1, size, lanes), BF))
+        boxes.append(pltpu.VMEM((teams, size, lanes), BF))
     for _ in range(2):
         boxes.append(pltpu.VMEM((width, width), BF))
         boxes += [pltpu.VMEM((n, width // team, width), BF) for n in (team, teams)]
-    copies = 18 + chunks * (2 * len(mlp_orders[0]) + teams) + 2 * (1 + 2 * team + teams) + chunks + 2 * (team + teams + 1)
+    copies = 18 + (chunks + 2) * (2 * len(mlp_orders[0]) + teams) + 2 * (1 + 2 * team + teams) + chunks + 2 * (team + teams + 1)
     return pl.pallas_call(
         functools.partial(
-            compute_kernel, team=team, teams=teams, mlp_orders=mlp_orders
+            compute_kernel, team=team, teams=teams, mlp_orders=mlp_orders, attn_orders=attn_orders
         ),
         out_shape=(
             jax.ShapeDtypeStruct((row_count, width), BF),
@@ -999,7 +1046,7 @@
 
 
 def finish(act, pg, qkv, attn, mi, mot, expert_in, expert_out, small):
-    steps = 3
+    steps = 2
 
     def by_rows(a):
         return pl.BlockSpec((a.shape[0] // steps, a.shape[1]), lambda i: (i, 0))

time: 129 us -> 125 us (0.969)
  Pallas kernels: 128 us -> 124 us
    pallas_call x1, Pallas kernels: 122 us -> 118 us  [compute(): pl.pallas_call(functools.partial(compute_kernel, team=team, teams=teams,...]
where the time goes in v7:
time: 125 us
  Pallas kernels  124 us (99%)
    pallas_call x1, Pallas kernels, compute(): pl.pallas_call(functools.partial(compute_kernel, team=team, teams=teams,...  118 us
    pallas_call x1, Pallas kernels, finish(): pl.pallas_call(finish_kernel, grid=(steps,), out_shape=(act, pg, gains, l...  5.65 us

profile of v7, /device:TPU:0, one launch (start us, length us, event | category | flops | bytes accessed | tf_op | source)
XLA Modules:
  0.0 125.0 jit_solution(15969361332687103168)
XLA Ops:
  0.6 118.5 %shard_map.186 = (bf16[512,384]{1,0:T(8,128)(2,1)}, bf16[512,384]{1,0:T(8,128)(2,1)}, bf16[576,384]{1,0:T(8,128)(2,1)}, bf16[192,384]{1,0:T(8,128)(2,1)}, bf16[3...) custom-call(bf16[512,384]{1,0:T(8,128)(2,1)} %bitcast.27, ...), custom_call_target="tpu_custom_call" | custom-call | tf_op jit(solution)/shard_map/pallas_call | solution.py:943
  119.2 5.7 %shard_map.187 = (bf16[512,384]{1,0:T(8,128)(2,1)}, bf16[512,384]{1,0:T(8,128)(2,1)}, f32[2,384]{1,0:T(2,128)}, f32[576,384]{1,0:T(8,128)}, f32[192,384]{1,0:T(8...) custom-call(bf16[512,384]{1,0:T(8,128)(2,1)} %get-tuple-element.29.a, ...), custom_call_target="tpu_custom_call" | custom-call | tf_op jit(solution)/shard_map/pallas_call | solution.py:1064

commit v8 on v7

--- a/solution.py
+++ b/solution.py
@@ -656,6 +656,8 @@
     g_hidden = dot_t(pack[1], eo[...])
     gslot[tensor] = dot_t((g_hidden * eslope[...]).astype(BF), ei[...]).astype(BF)
     send(12, gslot.at[tensor], gslot.at[tensor], beside)
+    per_own = jnp.sum(dot_t(eout[tensor], gy) * member, axis=0, keepdims=True)
+    to_own = jnp.sum(dot_t(gslot[tensor], z3) * member_own, axis=0, keepdims=True)
     arrived(11, eout.at[1 - tensor])
     outputs = eout[...].reshape(2 * SLOTS, width)
 
@@ -682,16 +684,19 @@
             team_packs = packs.at[0, this_team]
             send(pack_key + team + k, team_packs, team_packs, partner(k), team_like)
         for k in range(1, teams):
-            arrived(pack_key + team + k, packs.at[0, lax.rem(this_team + k, teams)])
+            arrived(pack_key + team + k, packs.at[0, lax.rem(this_team + teams - k, teams)])
         send(pack_key, packs.at[0], packs.at[1], core, all_packs)
 
-    per_token = [jnp.sum(dot_t(eout[e], gy) * member, axis=0, keepdims=True) for e in range(2)]
+    per_other = jnp.sum(dot_t(eout[1 - tensor], gy) * member, axis=0, keepdims=True)
+    first = tensor == 0
+    per_token = [jnp.where(first, per_own, per_other), jnp.where(first, per_other, per_own)]
     inner = combine[0] * per_token[0] + combine[1] * per_token[1]
     arrived(12, gslot.at[1 - tensor])
+    to_other = jnp.sum(dot_t(gslot[1 - tensor], z3) * member_own, axis=0, keepdims=True)
+    to_dispatch = [jnp.where(first, to_own, to_other), jnp.where(first, to_other, to_own)]
     logit_grads = []
     for e in range(2):
-        g_dispatch = jnp.sum(dot_t(gslot[e], z3) * member_own, axis=0, keepdims=True)
-        weighted = dispatch[e] * g_dispatch
+        weighted = dispatch[e] * to_dispatch[e]
         sums = jnp.sum(member * weighted, axis=1, keepdims=True)
         from_dispatch = weighted - dispatch[e] * jnp.sum(member * sums, axis=0, keepdims=True)
         logit_grads.append(combine[e] * (per_token[e] - inner) + from_dispatch)
@@ -864,11 +869,12 @@
         last_copies.append(local(2 + n, source.at[own_rows], dest))
 
     attn_stage(1, 1, 6)
+    attn_stage(0, 0, 2)
     dense[1].stage(5)
     dense[0].stage(6)
     attn_stage(1, 0, 7)
-    attn_stage(0, 0, 2)
     dense[2].stage(5)
+    attn_stage(0, 1, 2)
     for k in range(1, team):
         arrived(small_key + 1 + k, small_parts.at[k])
     small_across[0] = sum([small_parts[k] for k in range(1, team)], start=small_parts[0])
@@ -877,15 +883,13 @@
     for k in range(1, teams):
         arrived(small_key + 1 + team + k, small_across.at[k])
     small_out[...] = sum([small_across[k] for k in range(1, teams)], start=small_across[0])
-    dense[1].stage(6)
-
     def pass_dense(q):
         dense[q].stage(7)
         done = mlp_sum.at[section, q]
         send(mlp_key + q, done, done, core, mlp_like)
 
+    dense[1].stage(6)
     dense[2].stage(6)
-    attn_stage(0, 1, 2)
     attn_stage(1, 1, 7)
     pass_dense(0)
     pass_dense(1)
@@ -1068,11 +1072,11 @@
             act, pg, gains, like(qkv), like(attn), like(mi), mo, router, like(expert_in), like(expert_out)
         ),
         in_specs=[
-            whole(act), whole(pg), by_rows(qkv), by_rows(attn), by_rows(mi), mot_spec, by_rows(expert_in),
+            by_rows(act), by_rows(pg), by_rows(qkv), by_rows(attn), by_rows(mi), mot_spec, by_rows(expert_in),
             by_rows(expert_out), whole(small),
         ],
         out_specs=[
-            whole(act), whole(pg), whole(gains), by_rows(qkv), by_rows(attn), by_rows(mi), by_rows(mo), whole(router),
+            by_rows(act), by_rows(pg), whole(gains), by_rows(qkv), by_rows(attn), by_rows(mi), by_rows(mo), whole(router),
             by_rows(expert_in), by_rows(expert_out),
         ],
         compiler_params=pltpu.CompilerParams(vmem_limit_bytes=60 * 1024 * 1024),

time: 125 us -> 123 us (0.984)
  Pallas kernels: 124 us -> 122 us
    pallas_call x1, Pallas kernels: 118 us -> 116 us  [compute(): pl.pallas_call(functools.partial(compute_kernel, team=team, teams=teams,...]
where the time goes in v8:
time: 123 us
  Pallas kernels  122 us (99%)
    pallas_call x1, Pallas kernels, compute(): pl.pallas_call(functools.partial(compute_kernel, team=team, teams=teams,...  116 us
    pallas_call x1, Pallas kernels, finish(): pl.pallas_call(finish_kernel, grid=(steps,), out_shape=(act, pg, gains, l...  5.4 us

profile of v8, /device:TPU:0, one launch (start us, length us, event | category | flops | bytes accessed | tf_op | source)
XLA Modules:
  0.0 122.6 jit_solution(8631590714204678923)
XLA Ops:
  0.6 116.4 %shard_map.186 = (bf16[512,384]{1,0:T(8,128)(2,1)}, bf16[512,384]{1,0:T(8,128)(2,1)}, bf16[576,384]{1,0:T(8,128)(2,1)}, bf16[192,384]{1,0:T(8,128)(2,1)}, bf16[3...) custom-call(bf16[512,384]{1,0:T(8,128)(2,1)} %bitcast.27, ...), custom_call_target="tpu_custom_call" | custom-call | tf_op jit(solution)/shard_map/pallas_call | solution.py:947
  117.1 5.4 %shard_map.187 = (bf16[512,384]{1,0:T(8,128)(2,1)}, bf16[512,384]{1,0:T(8,128)(2,1)}, f32[2,384]{1,0:T(2,128)}, f32[576,384]{1,0:T(8,128)}, f32[192,384]{1,0:T(8...) custom-call(bf16[512,384]{1,0:T(8,128)(2,1)} %get-tuple-element.29.a, ...), custom_call_target="tpu_custom_call" | custom-call | tf_op jit(solution)/shard_map/pallas_call | solution.py:1068
